TPU v7x, 128 devices: a whole 4x4x4 slice. The times are simulated.
128 devices in a mesh: gx: 32 (over z, y_lo, x), gy: 4 (over y_hi, core).
Axes of the slice: x: 4, y: 4 (y_hi: 2, y_lo: 2; y = y_hi * 2 + y_lo), z: 4, core: 2. Of those that a mesh axis runs over, the one named last changes fastest.
Arguments:
- fluid_source: float32 [256, 128, 512], P('gx', 'gy'), may hold values from -6 to 6
- fluid_diag: float32 [256, 128, 512], P('gx', 'gy'), may hold values from 0.05 to 2
- stiff_ref: float32 [81, 81], replicated
- elem_coef: float32 [49152], P(('gx', 'gy')), may hold values from 0.3 to 3
- connect: int32 [27, 49152], P(None, ('gx', 'gy')), may hold values from 0 to 12543
- live_count: int32 [128], P(('gx', 'gy')), may hold values from 48 to 384, as said below
- node_mass: float32 [393216], P(('gx', 'gy')), may hold values from 0.5 to 2
- solid_load: float32 [3, 393216], P(None, ('gx', 'gy')), may hold values from -24 to 24
- wet_normal: float32 [3, 32768], P(None, ('gx', 'gy')), may hold values from -6 to 6
- trac_face: int32 [4, 32768], P(None, ('gx', 'gy')), may hold values from 0 to 1023
- trac_weight: float32 [4, 32768], P(None, ('gx', 'gy')), may hold values from 0 to 0.5
- wall_node: int32 [4, 256, 128], P(None, 'gx', 'gy'), may hold values from 0 to 1023
- wall_weight: float32 [4, 256, 128], P(None, 'gx', 'gy'), may hold values from 0 to 0.5
Outputs:
- pressure: float32 [256, 128, 512], P('gx', 'gy')
- displacement: float32 [3, 393216], P(None, ('gx', 'gy'))
Inputs may be any that keep to these rules, and one draw needn't show every extreme that they name: `connect`: entries number columns of the extended node list of the element's segment: its 12288 own nodes, then the first 256 nodes of the next segment. `live_count`: live slots of each device come first in its 384 slots; some device is full. `trac_face`: indices into the wall faces of the node's span slab, in the order of wall_seg. `wall_node`: indices into the face's segment's list of 1024 wetted nodes.
All inputs are finite; a program needn't handle non-finite values.
Results may differ from a plain program's by a relative error of at most 0.00014.
Values sent between devices are 32-bit elements; how exact they have to be, the bound alone decides.
No kernel may reach another device: no remote copies, remote signals or barrier semaphores. Data moves between devices by JAX's collectives and lax.ppermute only.
A program may use at most 64 MiB of HBM per device.

v0:
```python
import jax
import jax.numpy as jnp
from jax import lax
from jax.sharding import PartitionSpec as P

PLANE = 256
BLK = 384
ITERS = 2
PSEUDO = 2
COUPLE = 2


pseudo_weight = 0.8
traction_scale = 30.0
motion_scale = 2.0
relax_weight = 0.5


def padded_2(block, sides, width):
    for axis, dim in sides:
        count = lax.axis_size(axis)
        forward = [(i, i + 1) for i in range(count - 1)]
        backward = [(target, source) for source, target in forward]
        low = lax.ppermute(
            lax.slice_in_dim(block, block.shape[dim] - width, None, axis=dim), axis, forward
        )
        high = lax.ppermute(lax.slice_in_dim(block, 0, width, axis=dim), axis, backward)
        block = jnp.concatenate([low, block, high], axis=dim)
    return block


def from_behind(value, axis, by):
    length = lax.axis_size(axis)
    pairs = [(i, i + by) for i in range(length) if 0 <= i + by < length]
    return lax.ppermute(value, axis, pairs)


def fluid_step(pressure, fluid_diag, forcing):
    framed = padded_2(pressure, (("gx", 0), ("gy", 1)), 1)
    padded = jnp.pad(framed, ((0, 0), (0, 0), (1, 1)))
    beside = padded[2:, 1:-1, 1:-1] + padded[:-2, 1:-1, 1:-1]
    beside = beside + padded[1:-1, 2:, 1:-1] + padded[1:-1, :-2, 1:-1]
    beside = beside + padded[1:-1, 1:-1, 2:] + padded[1:-1, 1:-1, :-2]
    center = 6.0 + fluid_diag
    applied = center * pressure - beside
    return pressure + pseudo_weight * (forcing - applied) / center


def global_sums(values):
    totals = lax.psum((values[0],), ("gx", "gy"))
    return totals


def conjugate(apply_fn, solid_force):
    solution = jnp.zeros_like(solid_force)
    residual = solid_force
    direction = residual
    norm_now = global_sums((jnp.sum(residual * residual),))[0]
    for iteration in range(ITERS):
        applied = apply_fn(direction)
        curvature = global_sums((jnp.sum(direction * applied),))[0]
        step_size = norm_now / curvature
        solution = solution + step_size * direction
        residual = residual - step_size * applied
        norm_next = global_sums((jnp.sum(residual * residual),))[0]
        direction = residual + norm_next / norm_now * direction
        norm_now = norm_next
    return solution


def local(
    fluid_source,
    fluid_diag,
    stiff_ref,
    elem_coef,
    connect,
    live_count,
    node_mass,
    solid_load,
    wet_normal,
    trac_face,
    trac_weight,
    wall_node,
    wall_weight,
):
    owned_nodes = node_mass.shape[0]
    wet_count = wet_normal.shape[1]
    elem_count = connect.shape[1]
    node_order = connect.shape[0]
    chord_parts = lax.axis_size("gy")
    seg_nodes = owned_nodes * chord_parts
    turn_width = BLK
    live_here = live_count[0]
    position = jnp.arange(elem_count, dtype=jnp.int32)
    elem_weight = elem_coef * (position < live_here).astype(jnp.float32)
    turn_count = elem_count // turn_width

    def element_terms(extended):

        def one_turn(turn_index, summed):
            gathered = extended[:, connect].reshape(3 * node_order, turn_width)
            product = jnp.dot(
                stiff_ref,
                gathered,
                precision=lax.Precision.HIGHEST,
                preferred_element_type=jnp.float32,
            )
            product = product * elem_weight[None, :]
            return summed.at[:, connect].add(product.reshape(3, node_order, turn_width))

        return lax.fori_loop(0, turn_count, one_turn, jnp.zeros(extended.shape, jnp.float32))

    def plane_terms(segment_vec):
        following = from_behind(segment_vec[:, :PLANE], "gx", -1)
        summed = element_terms(jnp.concatenate([segment_vec, following], axis=1))
        tail_part = from_behind(summed[:, seg_nodes:], "gx", 1)
        return summed[:, :seg_nodes].at[:, :PLANE].add(tail_part)

    def apply_fn(vector_in):
        segment_vec = lax.all_gather(vector_in, "gy", axis=1, tiled=True)
        return (
            lax.psum_scatter(plane_terms(segment_vec), "gy", scatter_dimension=1, tiled=True)
            + node_mass[None, :] * vector_in
        )

    displacement = jnp.zeros(solid_load.shape, jnp.float32)
    pressure = jnp.zeros(fluid_source.shape, jnp.float32)
    for coupling in range(COUPLE):
        motion = jnp.sum(wet_normal * displacement[:, :wet_count], axis=0)
        motion_all = lax.all_gather(motion, "gy", axis=0, tiled=True)
        wall_source = motion_scale * jnp.sum(wall_weight * motion_all[wall_node], axis=0)
        forcing = fluid_source.at[:, :, 0].add(wall_source)
        for pseudo_step in range(PSEUDO):
            pressure = fluid_step(pressure, fluid_diag, forcing)
        wall_all = lax.all_gather(pressure[:, :, 0].reshape(-1), "gy", axis=0, tiled=True)
        traction = jnp.sum(trac_weight * wall_all[trac_face], axis=0)
        solid_force = solid_load.at[:, :wet_count].add(
            traction_scale * traction[None, :] * wet_normal
        )
        solution = conjugate(apply_fn, solid_force)
        displacement = displacement + relax_weight * (solution - displacement)
    return (pressure, displacement)


def solution(mesh):
    in_specs = (
        P("gx", "gy", None),
        P("gx", "gy", None),
        P(),
        P(("gx", "gy")),
        P(None, ("gx", "gy")),
        P(("gx", "gy")),
        P(("gx", "gy")),
        P(None, ("gx", "gy")),
        P(None, ("gx", "gy")),
        P(None, ("gx", "gy")),
        P(None, ("gx", "gy")),
        P(None, "gx", "gy"),
        P(None, "gx", "gy"),
    )
    out_specs = (P("gx", "gy", None), P(None, ("gx", "gy")))
    return jax.shard_map(local, mesh=mesh, in_specs=in_specs, out_specs=out_specs, check_vma=False)
```

profile of v0, /device:TPU:1, one launch (start us, length us, event | category | flops | bytes accessed | tf_op | source)
XLA Modules:
  0.0 1283.9 jit_solution(11407972666191639603)
XLA Ops:
  10.4 4.6 collective-permute-start.1
  16.6 7.8 all-gather
  24.4 4.5 gather_fusion
  31.3 5.0 collective-permute-start.3
  39.4 4.0 collective-permute-start.5
  46.7 6.8 collective-permute-start.7
  56.0 6.6 all-gather.1
  62.6 4.5 gather_fusion.1
  67.9 7.5 all_gather.26
  80.3 4.3 copy.164
  84.6 22.8 %gather_fusion.2 = f32[10368,3]{1,0:T(8,128)} fusion(f32[3,12544]{0,1:T(8,128)} %copy.164, s32[11264]{0:T(1024)S(1)} %pad_clamp_fusion), kind=kCustom, calls=%fused_computation.2 | custom fusion | bytes 290304 | tf_op jit(solution)/shard_map/while/body/eval_jaxpr/gather | solution.py:101
  107.3 4.2 copy.165
  115.6 61.1 %scatter_custom_fusion = f32[3,12544]{0,1:T(8,128)} fusion(s32[10368]{0:T(1024)S(1)} %reshape.330, f32[10368,3]{1,0:T(8,128)} %bitcast.64, f32[]{:T(128)} %constant.216.clone.1), kind=kCustom, calls=%fused_computation.18 | custom fusion | flops 31104 | bytes 151040 | tf_op jit(solution)/shard_map/while/body/eval_jaxpr/scatter-add | solution.py:109
  181.9 4.7 slice.442
  188.9 77.8 %reduce-scatter.13.cloned.1.call-done = f32[3072,3]{1,0:T(8,128)} async-done(((f32[12288,3]{1,0:T(8,128)}), f32[3072,3]{1,0:T(8,128)}) %reduce-scatter.13.cloned.1.call-update) | async-done | bytes 36880
  269.4 65.1 %all-reduce.7 = (f32[]{:T(128)}, f32[]{:T(128)}) all-reduce(f32[]{:T(128)} %get-tuple-element.181, f32[]{:T(128)} %get-tuple-element.180), channel_id=1, replica_groups=mesh['gx'=32,'gy'=4] {'gx','gy'}, use_global_device_ids=true, to_apply=%region_5.6 | all-reduce | flops 2 | bytes 16 | tf_op jit(solution)/shard_map/psum | solution.py:50
  336.3 64.0 %psum.58 = f32[]{:T(128)} all-reduce(f32[]{:T(128)} %multiply_reduce_fusion.5), channel_id=1, replica_groups=mesh['gx'=32,'gy'=4] {'gx','gy'}, use_global_device_ids=true, to_apply=%region_12.13 | all-reduce | flops 1 | bytes 8 | tf_op jit(solution)/shard_map/psum | solution.py:50
  401.6 7.9 all_gather.27
  413.8 4.3 copy.168
  418.1 22.8 %gather_fusion.3 = f32[10368,3]{1,0:T(8,128)} fusion(f32[3,12544]{0,1:T(8,128)} %copy.168, s32[11264]{0:T(1024)S(1)} %pad_clamp_fusion), kind=kCustom, calls=%fused_computation.3 | custom fusion | bytes 290304 | tf_op jit(solution)/shard_map/while/body/eval_jaxpr/gather | solution.py:101
  440.9 4.2 copy.169
  449.1 61.1 %scatter_custom_fusion.1 = f32[3,12544]{0,1:T(8,128)} fusion(s32[10368]{0:T(1024)S(1)} %reshape.330, f32[10368,3]{1,0:T(8,128)} %bitcast.65, f32[]{:T(128)} %constant.216.clone.1), kind=kCustom, calls=%fused_computation.16 | custom fusion | flops 31104 | bytes 151040 | tf_op jit(solution)/shard_map/while/body/eval_jaxpr/scatter-add | solution.py:109
  512.8 4.7 slice.446
  521.1 4.0 collective-permute-start.13
  526.5 4.5 collective-permute-start.14
  534.0 52.5 %reduce-scatter.15.cloned.1.call-done = f32[3072,3]{1,0:T(8,128)} async-done(((f32[12288,3]{1,0:T(8,128)}), f32[3072,3]{1,0:T(8,128)}) %reduce-scatter.15.cloned.1.call-update) | async-done | bytes 36880
  589.6 65.1 %psum.59 = f32[]{:T(128)} all-reduce(f32[]{:T(128)} %multiply_reduce_fusion.4), channel_id=1, replica_groups=mesh['gx'=32,'gy'=4] {'gx','gy'}, use_global_device_ids=true, to_apply=%region_16.17 | all-reduce | flops 1 | bytes 8 | tf_op jit(solution)/shard_map/psum | solution.py:50
  656.1 7.0 all-gather.2
  663.1 4.5 gather_fusion.4
  684.2 7.0 all-gather.3
  691.3 4.5 gather_fusion.5
  696.5 7.7 all_gather.30
  708.9 4.3 copy.173
  713.1 22.8 %gather_fusion.6 = f32[10368,3]{1,0:T(8,128)} fusion(f32[3,12544]{0,1:T(8,128)} %copy.173, s32[11264]{0:T(1024)S(1)} %pad_clamp_fusion), kind=kCustom, calls=%fused_computation.6 | custom fusion | bytes 290304 | tf_op jit(solution)/shard_map/while/body/eval_jaxpr/gather | solution.py:101
  735.9 4.2 copy.174
  744.1 61.1 %scatter_custom_fusion.2 = f32[3,12544]{0,1:T(8,128)} fusion(s32[10368]{0:T(1024)S(1)} %reshape.330, f32[10368,3]{1,0:T(8,128)} %bitcast.66, f32[]{:T(128)} %constant.216.clone.1), kind=kCustom, calls=%fused_computation.14 | custom fusion | flops 31104 | bytes 151040 | tf_op jit(solution)/shard_map/while/body/eval_jaxpr/scatter-add | solution.py:109
  809.5 4.7 slice.460
  816.6 71.1 %reduce-scatter.17.cloned.1.call-done = f32[3072,3]{1,0:T(8,128)} async-done(((f32[12288,3]{1,0:T(8,128)}), f32[3072,3]{1,0:T(8,128)}) %reduce-scatter.17.cloned.1.call-update) | async-done | bytes 36880
  890.3 65.1 %all-reduce.6 = (f32[]{:T(128)}, f32[]{:T(128)}) all-reduce(f32[]{:T(128)} %get-tuple-element.179, f32[]{:T(128)} %get-tuple-element.178), channel_id=1, replica_groups=mesh['gx'=32,'gy'=4] {'gx','gy'}, use_global_device_ids=true, to_apply=%region_21.22 | all-reduce | flops 2 | bytes 16 | tf_op jit(solution)/shard_map/psum | solution.py:50
  957.3 63.8 %psum.62 = f32[]{:T(128)} all-reduce(f32[]{:T(128)} %multiply_reduce_fusion.1), channel_id=1, replica_groups=mesh['gx'=32,'gy'=4] {'gx','gy'}, use_global_device_ids=true, to_apply=%region_27.28 | all-reduce | flops 1 | bytes 8 | tf_op jit(solution)/shard_map/psum | solution.py:50
  1022.4 7.8 all_gather.31
  1034.6 4.3 copy.177
  1038.9 22.8 %gather_fusion.7 = f32[10368,3]{1,0:T(8,128)} fusion(f32[3,12544]{0,1:T(8,128)} %copy.177, s32[11264]{0:T(1024)S(1)} %pad_clamp_fusion), kind=kCustom, calls=%fused_computation.7 | custom fusion | bytes 290304 | tf_op jit(solution)/shard_map/while/body/eval_jaxpr/gather | solution.py:101
  1061.6 4.2 copy.178
  1069.8 61.1 %scatter_custom_fusion.3 = f32[3,12544]{0,1:T(8,128)} fusion(s32[10368]{0:T(1024)S(1)} %reshape.330, f32[10368,3]{1,0:T(8,128)} %bitcast.63, f32[]{:T(128)} %constant.216.clone.1), kind=kCustom, calls=%fused_computation.12 | custom fusion | flops 31104 | bytes 151040 | tf_op jit(solution)/shard_map/while/body/eval_jaxpr/scatter-add | solution.py:109
  1133.6 4.7 slice.464
  1140.5 66.8 %reduce-scatter.19.cloned.1.call-done = f32[3072,3]{1,0:T(8,128)} async-done(((f32[12288,3]{1,0:T(8,128)}), f32[3072,3]{1,0:T(8,128)}) %reduce-scatter.19.cloned.1.call-update) | async-done | bytes 36880
  1209.9 65.0 %psum.63 = f32[]{:T(128)} all-reduce(f32[]{:T(128)} %multiply_reduce_fusion), channel_id=1, replica_groups=mesh['gx'=32,'gy'=4] {'gx','gy'}, use_global_device_ids=true, to_apply=%region_31.0 | all-reduce | flops 1 | bytes 8 | tf_op jit(solution)/shard_map/psum | solution.py:50
  (175 shorter events, 109.7 us)
Async XLA Ops:
  7.2 104.4 %copy-start = (f32[81,81]{1,0:T(8,128)S(1)}, f32[81,81]{1,0:T(8,128)}, u32[]{:S(2)}) copy-start(f32[81,81]{1,0:T(8,128)} %param.31) | copy-start | bytes 78736
  7.2 259.6 %reduce-scatter.13.cloned.1.call-start = ((), (), s32[]{:S(2)}) async-start(), calls=%async_computation.4 | async-start | bytes 7864320
  9.1 20.0 %collective-permute-start = (f32[1,32,512]{2,1,0:T(8,128)S(1)}, f32[1,32,512]{2,1,0:T(8,128)S(1)}, u32[]{:S(2)}, u32[]{:S(2)}) collective-permute-start(f32[1,32,512]{2,1,0:T(8,128)S(1)} %broadcast.217), channel_id=1, source_target_pairs={{4,0},{8,4},{12,8},{16,12},{20,16},{24,20},{28,24},{32,28},{36,32}... | collective-permute-start | bytes 196616 | tf_op jit(solution)/shard_map/ppermute | solution.py:27
  10.4 18.7 %collective-permute-start.1 = (f32[1,32,512]{2,1,0:T(8,128)S(1)}, f32[1,32,512]{2,1,0:T(8,128)S(1)}, u32[]{:S(2)}, u32[]{:S(2)}) collective-permute-start(f32[1,32,512]{2,1,0:T(8,128)S(1)} %broadcast.217), channel_id=1, source_target_pairs={{0,4},{4,8},{8,12},{12,16},{16,20},{20,24},{24,28},{28,32},{32,36}... | collective-permute-start | bytes 196616 | tf_op jit(solution)/shard_map/ppermute | solution.py:24
  24.4 4.6 copy-start.6
  24.4 4.7 copy-start.5
  24.4 13.2 %copy-start.1 = (f32[8,32,512]{2,1,0:T(8,128)S(1)}, f32[8,32,512]{2,1,0:T(8,128)}, u32[]{:S(2)}) copy-start(f32[8,32,512]{2,1,0:T(8,128)} %param.30) | copy-start | bytes 1572868
  28.9 14.5 %copy-start.8 = (s32[4,256]{1,0:T(4,128)S(1)}, s32[4,256]{1,0:T(4,128)}, u32[]{:S(2)}) copy-start(s32[4,256]{1,0:T(4,128)} %param.38) | copy-start | bytes 12292
  29.2 7.4 collective-permute-start.2
  31.3 5.9 collective-permute-start.3
  37.6 29.5 %copy-start.7 = (f32[4,256]{1,0:T(4,128)S(1)}, f32[4,256]{1,0:T(4,128)}, u32[]{:S(2)}) copy-start(f32[4,256]{1,0:T(4,128)} %param.39) | copy-start | bytes 12292
  37.6 29.6 %copy-start.4 = (f32[3,256]{1,0:T(4,128)S(1)}, f32[3,256]{1,0:T(4,128)}, u32[]{:S(2)}) copy-start(f32[3,256]{1,0:T(4,128)} %param.37) | copy-start | bytes 9220
  37.6 39.0 %copy-start.9 = (f32[384]{0:T(512)S(1)}, f32[384]{0:T(512)}, u32[]{:S(2)}) copy-start(f32[384]{0:T(512)} %param.32) | copy-start | bytes 4612
  38.1 5.3 collective-permute-start.4
  39.4 5.3 collective-permute-start.5
  44.8 10.1 collective-permute-start.6
  46.7 8.2 collective-permute-start.7
  75.3 5.0 collective-permute-start.8
  177.6 9.0 collective-permute-start.9
  186.7 82.0 %copy-start.3 = (f32[3072]{0:T(1024)S(1)}, f32[3072]{0:T(1024)}, u32[]{:S(2)}) copy-start(f32[3072]{0:T(1024)} %param.35) | copy-start | bytes 36868
  188.9 397.6 %reduce-scatter.15.cloned.1.call-start = ((), (), s32[]{:S(2)}) async-start(), calls=%async_computation.5 | async-start | bytes 7864320
  409.5 4.3 collective-permute-start.10
  511.1 6.4 collective-permute-start.11
  519.8 367.9 %reduce-scatter.17.cloned.1.call-start = ((), (), s32[]{:S(2)}) async-start(), calls=%async_computation.6 | async-start | bytes 7864320
  519.8 5.3 collective-permute-start.12
  521.1 5.3 collective-permute-start.13
  526.5 62.7 %collective-permute-start.14 = (f32[10,1,512]{2,1,0:T(1,128)S(1)}, f32[10,1,512]{2,1,0:T(1,128)S(1)}, u32[]{:S(2)}, u32[]{:S(2)}) collective-permute-start(f32[10,1,512]{2,1,0:T(1,128)S(1)} %get-tuple-element.189), channel_id=1, source_target_pairs={{1,0},{2,1},{3,2},{5,4},{6,5},{7,6},{9,8},{10,9},{11,10},{13,12},{... | collective-permute-start | bytes 61448 | tf_op jit(solution)/shard_map/ppermute | solution.py:27
  531.0 58.1 %collective-permute-start.15 = (f32[10,1,512]{2,1,0:T(1,128)S(1)}, f32[10,1,512]{2,1,0:T(1,128)S(1)}, u32[]{:S(2)}, u32[]{:S(2)}) collective-permute-start(f32[10,1,512]{2,1,0:T(1,128)S(1)} %get-tuple-element.188), channel_id=1, source_target_pairs={{0,1},{1,2},{2,3},{4,5},{5,6},{6,7},{8,9},{9,10},{10,11},{12,13},{... | collective-permute-start | bytes 61448 | tf_op jit(solution)/shard_map/ppermute | solution.py:24
  668.5 5.4 collective-permute-start.16
  669.8 5.3 collective-permute-start.17
  675.1 7.1 collective-permute-start.18
  678.4 4.7 collective-permute-start.19
  684.0 51.9 %copy-start.2 = (f32[8,32,512]{2,1,0:T(8,128)}, f32[8,32,512]{2,1,0:T(8,128)S(1)}, u32[]{:S(2)}) copy-start(f32[8,32,512]{2,1,0:T(8,128)S(1)} %fusion.26) | copy-start | bytes 1572868
  704.2 4.7 collective-permute-start.20
  806.2 8.1 collective-permute-start.21
  816.5 390.8 %reduce-scatter.19.cloned.1.call-start = ((), (), s32[]{:S(2)}) async-start(), calls=%async_computation.7 | async-start | bytes 7864320
  1030.2 4.3 collective-permute-start.22
  1131.9 6.4 collective-permute-start.23
Sparse Core Ops, SparseCore 0:
  189.0 77.7 reduce-scatter.12
  519.9 66.5 reduce-scatter.14
  816.6 71.0 reduce-scatter.16
  1140.6 66.6 reduce-scatter.18
where the time goes:
time: 1290 us; the launch traced here: 1280 us
  blocking collectives  447 us (35%)
  waiting for transfers between devices  287 us (22%)
  other arithmetic  266 us (21%)
  local copies, waits for them, and re-layouts  191 us (15%)
  starting transfers between devices  68 us (5%)
  between operations  23.4 us (2%)
    psum x6, blocking collectives, global_sums(): totals = lax.psum((values[0],), ('gx', 'gy'))  388 us
    unnamed x8, waiting for transfers between devices  268 us
    scatter-add x4, other arithmetic, one_turn(): return summed.at[:, connect].add(product.reshape(3, node_order, turn_width))  245 us
    gather x8, local copies, waits for them, and re-layouts, one_turn(): gathered = extended[:, connect].reshape(3 * node_order, turn_width)  108 us
    ppermute x8, starting transfers between devices, padded_2(): lax.ppermute(lax.slice_in_dim(block, block.shape[dim] - width, None, axis...  35.2 us
    all_gather x4, blocking collectives, apply_fn(): segment_vec = lax.all_gather(vector_in, 'gy', axis=1, tiled=True)  30.8 us
  transfers between devices with their start and end apart: 28, of which 14 were waited for; matrix products, arithmetic and copies ran while one was open for 2% of the time, Pallas kernels for 0%

commit v1 on v0

v1 whole, which is shorter than its diff:
```python
import functools

import jax
import jax.numpy as jnp
from jax import lax
from jax.experimental import pallas as pl
from jax.experimental.pallas import tpu as pltpu
from jax.sharding import PartitionSpec as P

F32 = jnp.float32
BF = jnp.bfloat16
AXES = ("gx", "gy")
N_GX = 32
N_DEV = 128
LR = 64
VR = 56
OWN = 48
CORE = 1
YHI = 2

pseudo_weight = 0.8
traction_scale = 30.0
motion_scale = 2.0
relax_weight = 0.5

VM = pl.BlockSpec(memory_space=pltpu.VMEM)
SM = pl.BlockSpec(memory_space=pltpu.SMEM)


def params(mib=40):
    return pltpu.CompilerParams(vmem_limit_bytes=mib << 20)


def swap(x, mask):
    return lax.ppermute(x, AXES, [(i, i ^ mask) for i in range(N_DEV)])


def from_gx(x, by):
    return lax.ppermute(x, "gx", [(i, i + by) for i in range(N_GX) if 0 <= i + by < N_GX])


def from_gy(x, by):
    return lax.ppermute(x, "gy", [(i, i + by) for i in range(4) if 0 <= i + by < 4])


def split(v):
    hi = v.astype(BF)
    return hi, (v - hi.astype(F32)).astype(BF)


def apply_body(nblk_ref, v_ref, conn_ref, ew_ref, s_ref, out_ref, t_scr, oh_scr, ml_scr, x_scr, a_scr, acc):
    for c in range(3):
        v = jnp.concatenate([v_ref[c], jnp.zeros((LR - VR, 256), F32)], axis=0)
        hi, lo = split(v)
        t_scr[c * LR : (c + 1) * LR, 0:256] = hi
        t_scr[c * LR : (c + 1) * LR, 256:512] = lo
    acc[...] = jnp.zeros_like(acc)
    i256 = lax.broadcasted_iota(jnp.int32, (256, 128), 0)
    i64 = lax.broadcasted_iota(jnp.int32, (LR, 128), 0)

    def block(b, carry):
        for p in range(14):
            for h in range(2):
                k = 2 * p + h
                sl = slice(p * 256 + h * 128, p * 256 + h * 128 + 128)
                if k == 27:
                    oh_scr[:, sl] = jnp.zeros((256, 128), BF)
                    ml_scr[:, sl] = jnp.zeros((LR, 128), BF)
                    a_scr[:, sl] = jnp.zeros((384, 128), BF)
                    continue
                idx = conn_ref[b, k : k + 1, :]
                oh_scr[:, sl] = (i256 == (idx & 255)).astype(F32).astype(BF)
                ml_scr[:, sl] = (i64 == (idx >> 8)).astype(F32).astype(BF)
            sp = slice(p * 256, p * 256 + 256)
            oh = oh_scr[:, sp]
            g = jnp.dot(t_scr[...], jnp.concatenate([oh, oh], axis=0), preferred_element_type=F32)
            m = ml_scr[:, sp].astype(F32)
            for c in range(3):
                s = (g[c * LR : (c + 1) * LR] * m).reshape(8, 8, 256).sum(axis=0)
                for h in range(2):
                    k = 2 * p + h
                    if k < 27:
                        x_scr[k * 24 + c * 8 : k * 24 + c * 8 + 8, :] = s[:, h * 128 : h * 128 + 128]
        xh, xl = split(x_scr[...])
        r = jnp.dot(s_ref[...], xh, preferred_element_type=F32)
        prod = r[:88] + r[88:] + jnp.dot(s_ref[0:88, :], xl, preferred_element_type=F32)
        prod = prod * ew_ref[b]
        ph = prod.astype(BF).astype(F32)
        parts = (ph, prod - ph)
        for k in range(27):
            sl = slice(k * 128, k * 128 + 128)
            m = ml_scr[:, sl].reshape(4, 16, 128)
            for c in range(3):
                row = c * 27 + k
                for j, src in enumerate(parts):
                    r16 = jnp.broadcast_to(src[row : row + 1, :], (16, 128)).astype(BF)
                    at = j * 192 + c * LR
                    a_scr[at : at + LR, sl] = (m * r16[None]).reshape(LR, 128)
        acc[...] += lax.dot_general(
            a_scr[...], oh_scr[...], (((1,), (1,)), ((), ())), preferred_element_type=F32
        )
        return carry

    lax.fori_loop(0, nblk_ref[0], block, 0)
    for c in range(3):
        s = acc[c * LR : (c + 1) * LR, :] + acc[192 + c * LR : 192 + (c + 1) * LR, :]
        out_ref[c] = s[:VR]


def stiff_apply(nblk, v, conn, ew, s):
    return pl.pallas_call(
        apply_body,
        out_shape=jax.ShapeDtypeStruct((3, VR, 256), F32),
        in_specs=[SM] + [VM] * 4,
        out_specs=VM,
        scratch_shapes=[
            pltpu.VMEM((192, 512), BF),
            pltpu.VMEM((256, 3584), BF),
            pltpu.VMEM((LR, 3584), BF),
            pltpu.VMEM((648, 128), F32),
            pltpu.VMEM((384, 3584), BF),
            pltpu.VMEM((384, 256), F32),
        ],
        compiler_params=params(),
    )(nblk, v, conn, ew, s)


def prep_stiff(stiff):
    e = jnp.repeat(stiff.reshape(81, 3, 27).transpose(0, 2, 1).reshape(81, 81), 8, axis=1)
    e = jnp.concatenate([e, jnp.zeros((7, 648), F32)], axis=0)
    h = lax.reduce_precision(e, 8, 7)
    return jnp.concatenate([h.astype(BF), (e - h).astype(BF)], axis=0)


def finish_body(at_ref, p_ref, q_ref, mass_ref, v_ref, w_ref, dots_ref, *, second):
    keep = lax.broadcasted_iota(jnp.int32, (VR, 256), 0)
    live = jnp.where(at_ref[0] == N_GX - 1, OWN, OWN + 1)
    mask = (keep < live).astype(F32)
    dots = [jnp.zeros((8, 256), F32) for _ in range(3)]
    for c in range(3):
        v = v_ref[c]
        w = (p_ref[c] + q_ref[c] + mass_ref[...] * v) * mask
        w_ref[c] = w
        pairs = ((v, w),) if second else ((v, v), (v, w), (w, w))
        for i, (x, y) in enumerate(pairs):
            dots[i] = dots[i] + (x[:OWN] * y[:OWN]).reshape(6, 8, 256).sum(axis=0)
    rows = [d.sum(axis=0, keepdims=True) for d in dots]
    rows = [d[:, :128] + d[:, 128:] for d in rows]
    dots_ref[...] = jnp.concatenate(rows + [jnp.zeros((5, 128), F32)], axis=0)


def finish(at, p, q, mass, v, second):
    return pl.pallas_call(
        functools.partial(finish_body, second=second),
        out_shape=(jax.ShapeDtypeStruct((3, VR, 256), F32), jax.ShapeDtypeStruct((8, 128), F32)),
        in_specs=[SM] + [VM] * 4,
        out_specs=(VM, VM),
        compiler_params=params(),
    )(at, p, q, mass, v)


def rows_in(at_ref):
    x = lax.broadcasted_iota(jnp.int32, (16, 128), 0) + at_ref[0] * 8 - 3
    return ((x >= 0) & (x < N_GX * 8)).astype(F32)


def wall_step(p, gain, force, inside, depth):
    lane = lax.broadcasted_iota(jnp.int32, (16, 128), 1)
    out = []
    for z in range(depth):
        c = p[z]
        n = pltpu.roll(c, 1, 0) + pltpu.roll(c, 15, 0)
        n = n + jnp.where(lane == 0, 0.0, pltpu.roll(c, 1, 1))
        n = n + jnp.where(lane == 127, 0.0, pltpu.roll(c, 127, 1))
        n = n + p[z + 1]
        if z > 0:
            n = n + p[z - 1]
        out.append(((1.0 - pseudo_weight) * c + gain[z] * (force[z] + n)) * inside)
    return out


def wall_front(at_ref, slab_ref):
    inside = rows_in(at_ref)
    fs = [slab_ref[z * 16 : z * 16 + 16, :] for z in range(4)]
    gain = [pseudo_weight / (6.0 + slab_ref[64 + z * 16 : 64 + z * 16 + 16, :]) for z in range(4)]
    p1 = [gain[z] * fs[z] * inside for z in range(4)]
    p2 = wall_step(p1, gain, fs, inside, 3)
    return inside, fs, gain, p2


def push(wall16, load_ref, seg_ref, f_ref):
    wall = pltpu.roll(wall16, 13, 0)[0:8]
    hi, lo = split(wall)
    table = jnp.concatenate([hi, lo], axis=0)
    i128 = lax.broadcasted_iota(jnp.int32, (128, 256), 0)
    i8 = lax.broadcasted_iota(jnp.int32, (8, 256), 0)
    f_ref[...] = load_ref[...]
    for g in range(4):
        total = jnp.zeros((8, 256), F32)
        for k in range(4):
            face = seg_ref[g, k : k + 1, :].astype(jnp.int32)
            oh = (i128 == ((face >> 8) * 32 + (face & 31))).astype(F32).astype(BF)
            r = jnp.dot(table, oh, preferred_element_type=F32)
            w = jnp.where(i8 == ((face >> 5) & 7), seg_ref[g, 4 + k : 5 + k, :], 0.0)
            total = total + (r[:8] + r[8:]) * w
        traction = total.sum(axis=0, keepdims=True)
        for c in range(3):
            f_ref[c, 12 * g : 12 * g + 1, :] = (
                f_ref[c, 12 * g : 12 * g + 1, :]
                + traction_scale * traction * seg_ref[g, 8 + c : 9 + c, :]
            )


def first_body(at_ref, slab_ref, load_ref, seg_ref, f_ref):
    inside, fs, gain, p2 = wall_front(at_ref, slab_ref)
    push(p2[0], load_ref, seg_ref, f_ref)


def first_force(at, slab, load, seg):
    return pl.pallas_call(
        first_body,
        out_shape=jax.ShapeDtypeStruct((3, VR, 256), F32),
        in_specs=[SM, VM, VM, VM],
        out_specs=VM,
        compiler_params=params(),
    )(at, slab, load, seg)


def second_body(at_ref, slab_ref, load_ref, seg_ref, ws_ref, f_ref):
    inside, fs, gain, p2 = wall_front(at_ref, slab_ref)
    force = [fs[0] + ws_ref[...], fs[1]]
    p3 = wall_step(p2, gain, force, inside, 2)
    p4 = wall_step(p3, gain, force, inside, 1)
    push(p4[0], load_ref, seg_ref, f_ref)


def second_force(at, slab, load, seg, ws):
    return pl.pallas_call(
        second_body,
        out_shape=jax.ShapeDtypeStruct((3, VR, 256), F32),
        in_specs=[SM] + [VM] * 4,
        out_specs=VM,
        compiler_params=params(),
    )(at, slab, load, seg, ws)


def weights_of(sums):
    a, b, c, d = [sums[i : i + 1, :].sum(axis=1, keepdims=True) for i in range(4)]
    alpha = a / b
    beta = (c - b * (b / a)) / (d - c * (c / b))
    return alpha + beta * (alpha * (c / b)), -alpha * beta


def source_body(sums_ref, inv_ref, f_ref, w_ref, seg_ref, pick_ref, ws_ref):
    c0, c1 = weights_of(sums_ref[...])
    c0, c1 = c0 * inv_ref[0], c1 * inv_ref[0]
    rows = []
    for g in range(4):
        total = jnp.zeros((1, 256), F32)
        for c in range(3):
            sl = slice(12 * g, 12 * g + 1)
            disp = relax_weight * (c0 * f_ref[c, sl, :] + c1 * w_ref[c, sl, :])
            total = total + seg_ref[g, 8 + c : 9 + c, :] * disp
        rows.append(total)
    hi, lo = split(jnp.concatenate(rows + [jnp.zeros((4, 256), F32)], axis=0))
    table = jnp.concatenate([hi, lo], axis=0)
    i256 = lax.broadcasted_iota(jnp.int32, (256, 128), 0)
    i8 = lax.broadcasted_iota(jnp.int32, (8, 128), 0)
    for x in range(8):
        total = jnp.zeros((8, 128), F32)
        for k in range(4):
            at = k * 8 + x
            node = pick_ref[at : at + 1, :].astype(jnp.int32)
            oh = (i256 == (node & 255)).astype(F32).astype(BF)
            r = jnp.dot(table, oh, preferred_element_type=F32)
            w = jnp.where(i8 == (node >> 8), pick_ref[32 + at : 33 + at, :], 0.0)
            total = total + (r[:8] + r[8:]) * w
        ws_ref[x : x + 1, :] = motion_scale * total.sum(axis=0, keepdims=True)


def wall_source(sums, inv, f, w, seg, pick):
    return pl.pallas_call(
        source_body,
        out_shape=jax.ShapeDtypeStruct((8, 128), F32),
        in_specs=[VM, SM] + [VM] * 4,
        out_specs=VM,
        compiler_params=params(),
    )(sums, inv, f, w, seg, pick)


def fluid_body(at_ref, fs_ref, fd_ref, xlo_ref, xhi_ref, ylo_ref, yhi_ref, ws_ref, out_ref, src, gain, pa, pb):
    for j, (ref, dst) in enumerate(((fs_ref, src), (fd_ref, gain))):
        for x in range(14):
            if x < 3:
                own = xlo_ref[j, x]
            elif x < 11:
                own = ref[x - 3]
            else:
                own = xhi_ref[j, x - 11]
            dst[x, 8:40, :] = own
            dst[x, 0:8, :] = ylo_ref[j, x]
            dst[x, 40:48, :] = yhi_ref[j, x]
    lane = lax.broadcasted_iota(jnp.int32, (48, 512), 1)
    y = lax.broadcasted_iota(jnp.int32, (48, 512), 0) + at_ref[1] * 32 - 8
    y_in = ((y >= 0) & (y < 128)).astype(F32)

    def x_in(x):
        gx = at_ref[0] * 8 + x - 3
        return jnp.where((gx >= 0) & (gx < N_GX * 8), 1.0, 0.0).astype(F32)

    def start(x, carry):
        g = pseudo_weight / (6.0 + gain[x]) * (y_in * x_in(x))
        gain[x] = g
        pa[x] = g * src[x]
        return carry

    lax.fori_loop(0, 14, start, 0)

    def new_row(p, x):
        c = p[x]
        n = p[x - 1] + p[x + 1] + pltpu.roll(c, 1, 0) + pltpu.roll(c, 47, 0)
        n = n + jnp.where(lane == 0, 0.0, pltpu.roll(c, 1, 1))
        n = n + jnp.where(lane == 511, 0.0, pltpu.roll(c, 511, 1))
        return (1.0 - pseudo_weight) * c + gain[x] * (src[x] + n)

    def second(x, carry):
        pb[x] = new_row(pa, x)
        return carry

    lax.fori_loop(1, 13, second, 0)

    def add_source(x, carry):
        src[x, :, 0:128] = src[x, :, 0:128] + ws_ref[x]
        return carry

    lax.fori_loop(2, 12, add_source, 0)

    def third(x, carry):
        pa[x] = new_row(pb, x)
        return carry

    lax.fori_loop(2, 12, third, 0)

    def fourth(x, carry):
        out_ref[x - 3] = new_row(pa, x)[8:40]
        return carry

    lax.fori_loop(3, 11, fourth, 0)


def fluid(at, fs, fd, xlo, xhi, ylo, yhi, ws):
    return pl.pallas_call(
        fluid_body,
        out_shape=jax.ShapeDtypeStruct((8, 32, 512), F32),
        in_specs=[SM] + [VM] * 7,
        out_specs=VM,
        scratch_shapes=[pltpu.VMEM((14, 48, 512), F32)] * 4,
        compiler_params=params(),
    )(at, fs, fd, xlo, xhi, ylo, yhi, ws)


def last_body(s1_ref, s2_ref, inv_ref, f1_ref, w1_ref, f2_ref, w2_ref, out_ref):
    c0, c1 = weights_of(s1_ref[...])
    d0, d1 = weights_of(s2_ref[...])
    inv = inv_ref[0]
    c0, c1, d0, d1 = c0 * inv, c1 * inv, d0 * inv, d1 * inv
    for c in range(3):
        before = relax_weight * (c0 * f1_ref[c] + c1 * w1_ref[c])
        solved = d0 * f2_ref[c] + d1 * w2_ref[c]
        out_ref[c] = before + relax_weight * (solved - before)


def last(s1, s2, inv, f1, w1, f2, w2):
    return pl.pallas_call(
        last_body,
        out_shape=jax.ShapeDtypeStruct((3, 12, 256), F32),
        in_specs=[VM, VM, SM] + [VM] * 4,
        out_specs=VM,
        compiler_params=params(),
    )(s1, s2, inv, f1, w1, f2, w2)


def local(
    fluid_source,
    fluid_diag,
    stiff_ref,
    elem_coef,
    connect,
    live_count,
    node_mass,
    solid_load,
    wet_normal,
    trac_face,
    trac_weight,
    wall_node,
    wall_weight,
):
    gx = lax.axis_index("gx")
    gy = lax.axis_index("gy")
    core = gy & 1
    yhi = gy >> 1
    at = jnp.stack([gx, gy]).astype(jnp.int32)

    def by_core(own, other, axis):
        lo = jnp.where(core == 0, own, other)
        hi = jnp.where(core == 0, other, own)
        return jnp.concatenate([lo, hi], axis=axis)

    def by_yhi(own, other, axis):
        lo = jnp.where(yhi == 0, own, other)
        hi = jnp.where(yhi == 0, other, own)
        return jnp.concatenate([lo, hi], axis=axis)

    def gather(x, axis):
        pair = by_core(x, swap(x, CORE), axis)
        return by_yhi(pair, swap(pair, YHI), axis)

    layers = jnp.stack([fluid_source[:, :, :4], fluid_diag[:, :, :4]]).transpose(0, 3, 1, 2)
    below = from_gx(layers[:, :, 5:8], 1)
    above = from_gx(layers[:, :, 0:3], -1)
    layers = jnp.concatenate([below, layers, above, jnp.zeros((2, 4, 2, 32), F32)], axis=2)
    picks = jnp.concatenate([wall_node.astype(F32).reshape(32, 32), wall_weight.reshape(32, 32)], axis=0)
    wide = gather(jnp.concatenate([layers.reshape(128, 32), picks], axis=0), 1)
    slab, pick = wide[:128], wide[128:]

    scale = 1.0 / jnp.maximum(1.0, jnp.trace(stiff_ref))
    inv = scale.reshape(1)
    parts = jnp.concatenate(
        [
            solid_load.reshape(36, 256),
            node_mass.reshape(12, 256) * scale,
            trac_face.astype(F32),
            trac_weight,
            wet_normal,
        ],
        axis=0,
    )
    parts = gather(parts[None], 0)
    load = jnp.concatenate(
        [parts[:, :36].reshape(4, 3, 12, 256).transpose(1, 0, 2, 3).reshape(3, OWN, 256), jnp.zeros((3, VR - OWN, 256), F32)],
        axis=1,
    )
    mass = parts[:, 36:48].reshape(OWN, 256)
    mass_next = from_gx(mass[0:1], -1)
    mass = jnp.concatenate([mass, mass_next, jnp.zeros((VR - OWN - 1, 256), F32)], axis=0)
    seg = jnp.concatenate([parts[:, 48:59], jnp.zeros((4, 5, 256), F32)], axis=1)

    stiff = prep_stiff(stiff_ref * scale)
    conn = connect.reshape(27, 3, 128).transpose(1, 0, 2)
    live = live_count[0]
    nblk = ((live + 127) // 128).reshape(1)
    position = jnp.arange(384, dtype=jnp.int32)
    ew = (elem_coef * (position < live).astype(F32)).reshape(3, 1, 128)

    row = lax.broadcasted_iota(jnp.int32, (3, VR, 256), 1)

    def with_plane(f):
        following = from_gx(f[:, 0, :], -1)
        return jnp.where(row == OWN, following[:, None, :], f)

    def apply_fn(v, second):
        s = stiff_apply(nblk, v, conn, ew, stiff)
        tail = from_gx(s[:, OWN, :], 1)
        head = from_gx(s[:, 0, :], -1)
        s = s + jnp.where(row == 0, tail[:, None, :], 0.0) + jnp.where(row == OWN, head[:, None, :], 0.0)
        pair = s + swap(s, CORE)
        return finish(at, pair, swap(pair, YHI), mass, v, second)

    def total(x):
        for mask in (1, 3, 4, 8, 24):
            x = x + swap(x, mask * 4)
        return x

    def solve(f):
        w, dots = apply_fn(f, False)
        _, more = apply_fn(w, True)
        return w, total(jnp.concatenate([dots[0:3], more[0:1], jnp.zeros((4, 128), F32)], axis=0))

    f1 = with_plane(first_force(at, slab, load, seg))
    w1, s1 = solve(f1)
    ws = wall_source(s1, inv, f1, w1, seg, pick)
    ws_lo = from_gx(ws[7:8], 1)
    ws_hi = from_gx(ws[0:1], -1)
    ws = jnp.concatenate([jnp.zeros((2, 128), F32), ws_lo, ws, ws_hi, jnp.zeros((4, 128), F32)], axis=0)
    f2 = with_plane(second_force(at, slab, load, seg, ws))
    w2, s2 = solve(f2)

    def mine(x):
        return lax.dynamic_slice_in_dim(x, gy * 12, 12, axis=1)

    displacement = last(s1, s2, inv, mine(f1), mine(w1), mine(f2), mine(w2)).reshape(3, 3072)

    both = jnp.stack([fluid_source, fluid_diag])
    xlo = from_gx(both[:, 5:8], 1)
    xhi = from_gx(both[:, 0:3], -1)
    tall = jnp.concatenate([xlo, both, xhi], axis=1)
    ylo = from_gy(tall[:, :, 24:32], 1)
    yhi_block = from_gy(tall[:, :, 0:8], -1)
    padded = jnp.pad(ws, ((0, 0), (8, 8)))
    wall = lax.dynamic_slice_in_dim(padded, gy * 32, 48, axis=1)
    lane = lax.broadcasted_iota(jnp.int32, (16, 48, 128), 2)
    wall = jnp.where(lane == 0, wall[:, :, None], 0.0)
    pressure = fluid(at, fluid_source, fluid_diag, xlo, xhi, ylo, yhi_block, wall)
    return pressure, displacement


def solution(mesh):
    in_specs = (
        P("gx", "gy", None),
        P("gx", "gy", None),
        P(),
        P(("gx", "gy")),
        P(None, ("gx", "gy")),
        P(("gx", "gy")),
        P(("gx", "gy")),
        P(None, ("gx", "gy")),
        P(None, ("gx", "gy")),
        P(None, ("gx", "gy")),
        P(None, ("gx", "gy")),
        P(None, "gx", "gy"),
        P(None, "gx", "gy"),
    )
    out_specs = (P("gx", "gy", None), P(None, ("gx", "gy")))
    return jax.shard_map(local, mesh=mesh, in_specs=in_specs, out_specs=out_specs, check_vma=False)
```

time: 1290 us -> 239 us (0.19)
  blocking collectives: 447 us -> 0 us
  other arithmetic: 266 us -> 6.3 us
  waiting for transfers between devices: 287 us -> 46.3 us
  local copies, waits for them, and re-layouts: 191 us -> 4.29 us
  starting transfers between devices: 68 us -> 155 us
  Pallas kernels: 0 us -> 21.8 us
  between operations: 23.4 us -> 2.93 us
    psum x6 -> x0, blocking collectives: 388 us -> none  [global_sums(): totals = lax.psum((values[0],), ('gx', 'gy'))]
    unnamed x8 -> x0, waiting for transfers between devices: 268 us -> none
    scatter-add x10 -> x0, other arithmetic: 255 us -> none  [the longest x4 245 us: one_turn(): return summed.at[:, connect].add(product.reshape(3, node_order, turn_width))]
    gather x16 -> x0, local copies, waits for them, and re-layouts: 126 us -> none  [the longest x8 108 us: one_turn(): gathered = extended[:, connect].reshape(3 * node_order, turn_width)]
    ppermute x24 -> x41, starting transfers between devices: 67.8 us -> 155 us  [the longest x22 92.3 us: swap(): return lax.ppermute(x, AXES, [(i, i ^ mask) for i in range(N_DEV)])]
    all_gather x8 -> x0, blocking collectives: 59.2 us -> none  [the longest x4 30.8 us: apply_fn(): segment_vec = lax.all_gather(vector_in, 'gy', axis=1, tiled=True)]
    ppermute x24 -> x41, waiting for transfers between devices: 18.2 us -> 46.3 us  [the longest x22 32.9 us: swap(): return lax.ppermute(x, AXES, [(i, i ^ mask) for i in range(N_DEV)])]
    pallas_call x0 -> x13, Pallas kernels: none -> 21.8 us  [the longest x4 9.66 us: stiff_apply(): pl.pallas_call(apply_body, out_shape=jax.ShapeDtypeStruct((3, VR, 256), F...]
  transfers between devices with their start and end apart: 28 -> 41, of which waited for: 14 -> 27; matrix products, arithmetic and copies ran while one was open for 2% -> 1% of each run, Pallas kernels for 0% -> 3%
where the time goes in v1:
time: 239 us; the launch traced here: 237 us
  starting transfers between devices  155 us (65%)
  waiting for transfers between devices  46.3 us (19%)
  Pallas kernels  21.8 us (9%)
  other arithmetic  6.3 us (3%)
  local copies, waits for them, and re-layouts  4.29 us (2%)
  between operations  2.93 us (1%)
    ppermute x22, starting transfers between devices, swap(): return lax.ppermute(x, AXES, [(i, i ^ mask) for i in range(N_DEV)])  92.3 us
    ppermute x17, starting transfers between devices, from_gx(): lax.ppermute(x, 'gx', [(i, i + by) for i in range(N_GX) if 0 <= i + by <...  52.3 us
    ppermute x22, waiting for transfers between devices, swap(): return lax.ppermute(x, AXES, [(i, i ^ mask) for i in range(N_DEV)])  32.9 us
    ppermute x17, waiting for transfers between devices, from_gx(): lax.ppermute(x, 'gx', [(i, i + by) for i in range(N_GX) if 0 <= i + by <...  13.4 us
    ppermute x2, starting transfers between devices, from_gy(): lax.ppermute(x, 'gy', [(i, i + by) for i in range(4) if 0 <= i + by < 4])  10.5 us
    pallas_call x4, Pallas kernels, stiff_apply(): pl.pallas_call(apply_body, out_shape=jax.ShapeDtypeStruct((3, VR, 256), F...  9.66 us
    pallas_call x1, Pallas kernels, fluid(): pl.pallas_call(fluid_body, out_shape=jax.ShapeDtypeStruct((8, 32, 512), F...  5.58 us
  transfers between devices with their start and end apart: 41, of which 27 were waited for; matrix products, arithmetic and copies ran while one was open for 1% of the time, Pallas kernels for 3%

profile of v1, /device:TPU:1, one launch (start us, length us, event | category | flops | bytes accessed | tf_op | source)
XLA Modules:
  0.0 236.7 jit_solution(3265696359519578645)
XLA Ops:
  0.6 1.4 select_reduce_fusion
  5.0 1.5 collective-permute-start.8
  7.7 3.3 %collective-permute-start.4 = (f32[2,4,3,32]{3,2,1,0:T(4,128)S(1)}, f32[2,4,3,32]{3,2,1,0:T(4,128)S(1)}, u32[]{:S(2)}, u32[]{:S(2)}) collective-permute-start(f32[2,4,3,32]{3,2,1,0:T(4,128)S(1)} %get-tuple-element.36), channel_id=1, source_target_pairs={{0,4},{4,8},{8,12},{12,16},{16,20},{20,24},{24,28},{28,32},{32,36}... | collective-permute-start | bytes 9224 | tf_op jit(solution)/shard_map/ppermute | solution.py:39
  11.0 1.3 collective-permute-start.5
  15.6 2.2 collective-permute-start.6
  18.9 3.0 %collective-permute-start.7 = (f32[192,64]{1,0:T(8,128)S(1)}, f32[192,64]{1,0:T(8,128)S(1)}, u32[]{:S(2)}, u32[]{:S(2)}) collective-permute-start(f32[192,64]{1,0:T(8,128)S(1)} %pad_maximum_fusion.9), channel_id=1, source_target_pairs={{0,2},{1,3},{2,0},{3,1},{4,6},{5,7},{6,4},{7,5},{8,10},{9,11},{10,... | collective-permute-start | bytes 147464 | tf_op jit(solution)/shard_map/ppermute | solution.py:35
  22.0 2.4 %collective-permute-done.7 = f32[192,64]{1,0:T(8,128)S(1)} collective-permute-done((f32[192,64]{1,0:T(8,128)S(1)}, f32[192,64]{1,0:T(8,128)S(1)}, u32[]{:S(2)}, u32[]{:S(2)}) %collective-permute-start.7) | collective-permute-done | bytes 49184 | tf_op jit(solution)/shard_map/ppermute | solution.py:35
  24.7 3.2 %collective-permute-done.9 = f32[2,59,256]{2,1,0:T(8,128)S(1)} collective-permute-done((f32[2,59,256]{2,1,0:T(8,128)S(1)}, f32[2,59,256]{2,1,0:T(8,128)S(1)}, u32[]{:S(2)}, u32[]{:S(2)}) %collective-permute-start.9) | collective-permute-done | bytes 120864 | tf_op jit(solution)/shard_map/ppermute | solution.py:35
  29.1 1.3 collective-permute-start.10
  30.5 2.9 %collective-permute-done.10 = f32[3,256]{1,0:T(4,128)S(1)} collective-permute-done((f32[3,256]{1,0:T(4,128)S(1)}, f32[3,256]{1,0:T(4,128)S(1)}, u32[]{:S(2)}, u32[]{:S(2)}) %collective-permute-start.10) | collective-permute-done | bytes 3104 | tf_op jit(solution)/shard_map/ppermute | solution.py:39
  33.6 2.4 %shard_map.141 = f32[3,56,256]{2,1,0:T(8,128)S(1)} custom-call(s32[1]{0:T(128)} %bitcast.5.nblk_ref, f32[3,56,256]{2,1,0:T(8,128)S(1)} %broadcast_select_fusion.2.v_ref.f_ref, s32[3,27,128]{2,1,0:T(8,128)S(1)} %bitcast.69, f32[3,1,128]{2,1,0:T(1,128)S(1)} %reshape.71.ew_ref, bf16[176,648]{1,0:T(8,128)(2,1)S(1)} %pad_maximum_fusion.6.s_ref), custom_call_target="tpu_custom_call" | custom-call | tf_op jit(solution)/shard_map/pallas_call | solution.py:111
  36.0 1.3 collective-permute-start.12
  37.3 6.1 %collective-permute-start.11 = (f32[3,256]{1,0:T(4,128)S(1)}, f32[3,256]{1,0:T(4,128)S(1)}, u32[]{:S(2)}, u32[]{:S(2)}) collective-permute-start(f32[3,256]{1,0:T(4,128)S(1)} %bitcast.85), channel_id=1, source_target_pairs={{0,4},{4,8},{8,12},{12,16},{16,20},{20,24},{24,28},{28,32},{32,36}... | collective-permute-start | bytes 9224 | tf_op jit(solution)/shard_map/ppermute | solution.py:39
  44.2 1.8 collective-permute-start.13
  46.1 1.3 collective-permute-start.15
  47.5 6.7 %collective-permute-start.14 = (f32[3,56,256]{2,1,0:T(8,128)S(1)}, f32[3,56,256]{2,1,0:T(8,128)S(1)}, u32[]{:S(2)}, u32[]{:S(2)}) collective-permute-start(f32[3,56,256]{2,1,0:T(8,128)S(1)} %fusion.16.p_ref), channel_id=1, source_target_pairs={{0,2},{1,3},{2,0},{3,1},{4,6},{5,7},{6,4},{7,5},{8,10},{9,11},{10,... | collective-permute-start | bytes 516104 | tf_op jit(solution)/shard_map/ppermute | solution.py:35
  54.3 4.7 %collective-permute-done.14.q_ref = f32[3,56,256]{2,1,0:T(8,128)S(1)} collective-permute-done((f32[3,56,256]{2,1,0:T(8,128)S(1)}, f32[3,56,256]{2,1,0:T(8,128)S(1)}, u32[]{:S(2)}, u32[]{:S(2)}) %collective-permute-start.14) | collective-permute-done | bytes 172064 | tf_op jit(solution)/shard_map/ppermute | solution.py:35
  59.5 2.4 %shard_map.143 = f32[3,56,256]{2,1,0:T(8,128)S(1)} custom-call(s32[1]{0:T(128)} %bitcast.5.nblk_ref, f32[3,56,256]{2,1,0:T(8,128)S(1)} %get-tuple-element.9.v_ref.w_ref, s32[3,27,128]{2,1,0:T(8,128)S(1)} %bitcast.70, f32[3,1,128]{2,1,0:T(1,128)S(1)} %reshape.71.ew_ref, bf16[176,648]{1,0:T(8,128)(2,1)S(1)} %pad_maximum_fusion.6.s_ref), custom_call_target="tpu_custom_call" | custom-call | tf_op jit(solution)/shard_map/pallas_call | solution.py:111
  63.3 7.5 %collective-permute-start.16 = (f32[3,256]{1,0:T(4,128)S(1)}, f32[3,256]{1,0:T(4,128)S(1)}, u32[]{:S(2)}, u32[]{:S(2)}) collective-permute-start(f32[3,256]{1,0:T(4,128)S(1)} %bitcast.86), channel_id=1, source_target_pairs={{0,4},{4,8},{8,12},{12,16},{16,20},{20,24},{24,28},{28,32},{32,36}... | collective-permute-start | bytes 9224 | tf_op jit(solution)/shard_map/ppermute | solution.py:39
  71.7 1.4 collective-permute-done.18
  73.2 5.6 %collective-permute-start.19 = (f32[3,56,256]{2,1,0:T(8,128)S(1)}, f32[3,56,256]{2,1,0:T(8,128)S(1)}, u32[]{:S(2)}, u32[]{:S(2)}) collective-permute-start(f32[3,56,256]{2,1,0:T(8,128)S(1)} %fusion.15.p_ref), channel_id=1, source_target_pairs={{0,2},{1,3},{2,0},{3,1},{4,6},{5,7},{6,4},{7,5},{8,10},{9,11},{10,... | collective-permute-start | bytes 516104 | tf_op jit(solution)/shard_map/ppermute | solution.py:35
  78.7 4.5 %collective-permute-done.19.q_ref = f32[3,56,256]{2,1,0:T(8,128)S(1)} collective-permute-done((f32[3,56,256]{2,1,0:T(8,128)S(1)}, f32[3,56,256]{2,1,0:T(8,128)S(1)}, u32[]{:S(2)}, u32[]{:S(2)}) %collective-permute-start.19) | collective-permute-done | bytes 172064 | tf_op jit(solution)/shard_map/ppermute | solution.py:35
  84.5 2.8 %collective-permute-start.20 = (f32[8,128]{1,0:T(8,128)S(1)}, f32[8,128]{1,0:T(8,128)S(1)}, u32[]{:S(2)}, u32[]{:S(2)}) collective-permute-start(f32[8,128]{1,0:T(8,128)S(1)} %pad_maximum_fusion.13), channel_id=1, source_target_pairs={{0,4},{1,5},{2,6},{3,7},{4,0},{5,1},{6,2},{7,3},{8,12},{9,13},{10,... | collective-permute-start | bytes 12296 | tf_op jit(solution)/shard_map/ppermute | solution.py:35
  88.3 11.0 %collective-permute-start.21 = (f32[8,128]{1,0:T(8,128)S(1)}, f32[8,128]{1,0:T(8,128)S(1)}, u32[]{:S(2)}, u32[]{:S(2)}) collective-permute-start(f32[8,128]{1,0:T(8,128)S(1)} %fusion.5), channel_id=1, source_target_pairs={{0,12},{1,13},{2,14},{3,15},{4,8},{5,9},{6,10},{7,11},{8,4},{9,5},... | collective-permute-start | bytes 12296 | tf_op jit(solution)/shard_map/ppermute | solution.py:35
  100.3 4.4 %collective-permute-start.22 = (f32[8,128]{1,0:T(8,128)S(1)}, f32[8,128]{1,0:T(8,128)S(1)}, u32[]{:S(2)}, u32[]{:S(2)}) collective-permute-start(f32[8,128]{1,0:T(8,128)S(1)} %add.95), channel_id=1, source_target_pairs={{0,16},{1,17},{2,18},{3,19},{4,20},{5,21},{6,22},{7,23},{8,24},{9,... | collective-permute-start | bytes 12296 | tf_op jit(solution)/shard_map/ppermute | solution.py:35
  108.2 8.0 %collective-permute-start.24 = (f32[8,128]{1,0:T(8,128)S(1)}, f32[8,128]{1,0:T(8,128)S(1)}, u32[]{:S(2)}, u32[]{:S(2)}) collective-permute-start(f32[8,128]{1,0:T(8,128)S(1)} %add.97), channel_id=1, source_target_pairs={{0,96},{1,97},{2,98},{3,99},{4,100},{5,101},{6,102},{7,103},{8,104... | collective-permute-start | bytes 12296 | tf_op jit(solution)/shard_map/ppermute | solution.py:35
  117.8 1.3 collective-permute-start.26
  119.1 4.0 %collective-permute-start.25 = (f32[1,128]{1,0:T(1,128)S(1)}, f32[1,128]{1,0:T(1,128)S(1)}, u32[]{:S(2)}, u32[]{:S(2)}) collective-permute-start(f32[1,128]{1,0:T(1,128)S(1)} %get-tuple-element.39), channel_id=1, source_target_pairs={{0,4},{4,8},{8,12},{12,16},{16,20},{20,24},{24,28},{28,32},{32,36}... | collective-permute-start | bytes 1544 | tf_op jit(solution)/shard_map/ppermute | solution.py:39
  125.1 1.3 collective-permute-start.27
  126.4 3.3 %collective-permute-done.27 = f32[3,256]{1,0:T(4,128)S(1)} collective-permute-done((f32[3,256]{1,0:T(4,128)S(1)}, f32[3,256]{1,0:T(4,128)S(1)}, u32[]{:S(2)}, u32[]{:S(2)}) %collective-permute-start.27) | collective-permute-done | bytes 3104 | tf_op jit(solution)/shard_map/ppermute | solution.py:39
  129.7 2.5 %shard_map.148 = f32[3,56,256]{2,1,0:T(8,128)S(1)} custom-call(s32[1]{0:T(128)} %bitcast.5.nblk_ref, f32[3,56,256]{2,1,0:T(8,128)S(1)} %broadcast_select_fusion.1.v_ref, s32[3,27,128]{2,1,0:T(8,128)S(1)} %bitcast.71, f32[3,1,128]{2,1,0:T(1,128)S(1)} %reshape.71.ew_ref, bf16[176,648]{1,0:T(8,128)(2,1)S(1)} %pad_maximum_fusion.6.s_ref), custom_call_target="tpu_custom_call" | custom-call | tf_op jit(solution)/shard_map/pallas_call | solution.py:111
  133.6 6.3 %collective-permute-start.28 = (f32[3,256]{1,0:T(4,128)S(1)}, f32[3,256]{1,0:T(4,128)S(1)}, u32[]{:S(2)}, u32[]{:S(2)}) collective-permute-start(f32[3,256]{1,0:T(4,128)S(1)} %bitcast.87), channel_id=1, source_target_pairs={{0,4},{4,8},{8,12},{12,16},{16,20},{20,24},{24,28},{28,32},{32,36}... | collective-permute-start | bytes 9224 | tf_op jit(solution)/shard_map/ppermute | solution.py:39
  140.8 7.3 %collective-permute-start.30 = (f32[3,56,256]{2,1,0:T(8,128)S(1)}, f32[3,56,256]{2,1,0:T(8,128)S(1)}, u32[]{:S(2)}, u32[]{:S(2)}) collective-permute-start(f32[3,56,256]{2,1,0:T(8,128)S(1)} %select_add_fusion.1), channel_id=1, source_target_pairs={{0,1},{1,0},{2,3},{3,2},{4,5},{5,4},{6,7},{7,6},{8,9},{9,8},{10,11... | collective-permute-start | bytes 516104 | tf_op jit(solution)/shard_map/ppermute | solution.py:35
  149.2 7.7 %collective-permute-start.31 = (f32[3,56,256]{2,1,0:T(8,128)S(1)}, f32[3,56,256]{2,1,0:T(8,128)S(1)}, u32[]{:S(2)}, u32[]{:S(2)}) collective-permute-start(f32[3,56,256]{2,1,0:T(8,128)S(1)} %fusion.14.p_ref), channel_id=1, source_target_pairs={{0,2},{1,3},{2,0},{3,1},{4,6},{5,7},{6,4},{7,5},{8,10},{9,11},{10,... | collective-permute-start | bytes 516104 | tf_op jit(solution)/shard_map/ppermute | solution.py:35
  156.8 4.5 %collective-permute-done.31.q_ref = f32[3,56,256]{2,1,0:T(8,128)S(1)} collective-permute-done((f32[3,56,256]{2,1,0:T(8,128)S(1)}, f32[3,56,256]{2,1,0:T(8,128)S(1)}, u32[]{:S(2)}, u32[]{:S(2)}) %collective-permute-start.31) | collective-permute-done | bytes 172064 | tf_op jit(solution)/shard_map/ppermute | solution.py:35
  161.9 2.4 %shard_map.150 = f32[3,56,256]{2,1,0:T(8,128)S(1)} custom-call(s32[1]{0:T(128)} %bitcast.5.nblk_ref, f32[3,56,256]{2,1,0:T(8,128)S(1)} %get-tuple-element.12.v_ref, s32[3,27,128]{2,1,0:T(8,128)S(1)} %bitcast.72, f32[3,1,128]{2,1,0:T(1,128)S(1)} %reshape.71.ew_ref, bf16[176,648]{1,0:T(8,128)(2,1)S(1)} %pad_maximum_fusion.6.s_ref), custom_call_target="tpu_custom_call" | custom-call | tf_op jit(solution)/shard_map/pallas_call | solution.py:111
  165.6 6.8 %collective-permute-start.32 = (f32[3,256]{1,0:T(4,128)S(1)}, f32[3,256]{1,0:T(4,128)S(1)}, u32[]{:S(2)}, u32[]{:S(2)}) collective-permute-start(f32[3,256]{1,0:T(4,128)S(1)} %bitcast.88), channel_id=1, source_target_pairs={{0,4},{4,8},{8,12},{12,16},{16,20},{20,24},{24,28},{28,32},{32,36}... | collective-permute-start | bytes 9224 | tf_op jit(solution)/shard_map/ppermute | solution.py:39
  176.1 5.4 %collective-permute-start = (f32[2,3,32,512]{3,2,1,0:T(8,128)S(1)}, f32[2,3,32,512]{3,2,1,0:T(8,128)S(1)}, u32[]{:S(2)}, u32[]{:S(2)}) collective-permute-start(f32[2,3,32,512]{3,2,1,0:T(8,128)S(1)} %get-tuple-element.17), channel_id=1, source_target_pairs={{0,4},{4,8},{8,12},{12,16},{16,20},{20,24},{24,28},{28,32},{32,36}... | collective-permute-start | bytes 1179656 | tf_op jit(solution)/shard_map/ppermute | solution.py:39
  181.6 6.1 %collective-permute-start.35 = (f32[3,56,256]{2,1,0:T(8,128)S(1)}, f32[3,56,256]{2,1,0:T(8,128)S(1)}, u32[]{:S(2)}, u32[]{:S(2)}) collective-permute-start(f32[3,56,256]{2,1,0:T(8,128)S(1)} %fusion.13.p_ref), channel_id=1, source_target_pairs={{0,2},{1,3},{2,0},{3,1},{4,6},{5,7},{6,4},{7,5},{8,10},{9,11},{10,... | collective-permute-start | bytes 516104 | tf_op jit(solution)/shard_map/ppermute | solution.py:35
  187.6 1.5 collective-permute-done.1.xhi_ref
  190.0 2.7 %collective-permute-start.3 = (f32[2,14,8,512]{3,2,1,0:T(8,128)S(1)}, f32[2,14,8,512]{3,2,1,0:T(8,128)S(1)}, u32[]{:S(2)}, u32[]{:S(2)}) collective-permute-start(f32[2,14,8,512]{3,2,1,0:T(8,128)S(1)} %get-tuple-element.14), channel_id=1, source_target_pairs={{1,0},{2,1},{3,2},{5,4},{6,5},{7,6},{9,8},{10,9},{11,10},{13,12},{... | collective-permute-start | bytes 1376264 | tf_op jit(solution)/shard_map/ppermute | solution.py:43
  192.7 7.8 %collective-permute-start.2 = (f32[2,14,8,512]{3,2,1,0:T(8,128)S(1)}, f32[2,14,8,512]{3,2,1,0:T(8,128)S(1)}, u32[]{:S(2)}, u32[]{:S(2)}) collective-permute-start(f32[2,14,8,512]{3,2,1,0:T(8,128)S(1)} %get-tuple-element.15), channel_id=1, source_target_pairs={{0,1},{1,2},{2,3},{4,5},{5,6},{6,7},{8,9},{9,10},{10,11},{12,13},{... | collective-permute-start | bytes 1376264 | tf_op jit(solution)/shard_map/ppermute | solution.py:43
  201.8 3.2 %collective-permute-start.36 = (f32[8,128]{1,0:T(8,128)S(1)}, f32[8,128]{1,0:T(8,128)S(1)}, u32[]{:S(2)}, u32[]{:S(2)}) collective-permute-start(f32[8,128]{1,0:T(8,128)S(1)} %pad_maximum_fusion.12), channel_id=1, source_target_pairs={{0,4},{1,5},{2,6},{3,7},{4,0},{5,1},{6,2},{7,3},{8,12},{9,13},{10,... | collective-permute-start | bytes 12296 | tf_op jit(solution)/shard_map/ppermute | solution.py:35
  206.0 8.7 %collective-permute-start.37 = (f32[8,128]{1,0:T(8,128)S(1)}, f32[8,128]{1,0:T(8,128)S(1)}, u32[]{:S(2)}, u32[]{:S(2)}) collective-permute-start(f32[8,128]{1,0:T(8,128)S(1)} %fusion.6), channel_id=1, source_target_pairs={{0,12},{1,13},{2,14},{3,15},{4,8},{5,9},{6,10},{7,11},{8,4},{9,5},... | collective-permute-start | bytes 12296 | tf_op jit(solution)/shard_map/ppermute | solution.py:35
  215.7 4.6 %collective-permute-start.38 = (f32[8,128]{1,0:T(8,128)S(1)}, f32[8,128]{1,0:T(8,128)S(1)}, u32[]{:S(2)}, u32[]{:S(2)}) collective-permute-start(f32[8,128]{1,0:T(8,128)S(1)} %add.107), channel_id=1, source_target_pairs={{0,16},{1,17},{2,18},{3,19},{4,20},{5,21},{6,22},{7,23},{8,24},{9,... | collective-permute-start | bytes 12296 | tf_op jit(solution)/shard_map/ppermute | solution.py:35
  220.5 5.6 %shard_map.146 = f32[8,32,512]{2,1,0:T(8,128)} custom-call(s32[2]{0:T(128)S(1)} %pad_add_fusion.at_ref, f32[8,32,512]{2,1,0:T(8,128)S(1)} %copy-done, f32[8,32,512]{2,1,0:T(8,128)S(1)} %copy-done.1, f32[2,3,32,512]{3,2,1,0:T(8,128)S(1)} %collective-permute-done.xlo_ref, f32[2,3,32,512]{3,2,1,0:T(8,128)S(1)} %collective-permute-done.1.xhi_ref, ...), custom_call_target="tpu_custom_call" | custom-call | tf_op jit(solution)/shard_map/pallas_call | solution.py:352
  226.1 2.4 %collective-permute-done.39 = f32[8,128]{1,0:T(8,128)S(1)} collective-permute-done((f32[8,128]{1,0:T(8,128)S(1)}, f32[8,128]{1,0:T(8,128)S(1)}, u32[]{:S(2)}, u32[]{:S(2)}) %collective-permute-start.39) | collective-permute-done | bytes 4128 | tf_op jit(solution)/shard_map/ppermute | solution.py:35
  228.5 6.3 %collective-permute-start.40 = (f32[8,128]{1,0:T(8,128)S(1)}, f32[8,128]{1,0:T(8,128)S(1)}, u32[]{:S(2)}, u32[]{:S(2)}) collective-permute-start(f32[8,128]{1,0:T(8,128)S(1)} %add.109), channel_id=1, source_target_pairs={{0,96},{1,97},{2,98},{3,99},{4,100},{5,101},{6,102},{7,103},{8,104... | collective-permute-start | bytes 12296 | tf_op jit(solution)/shard_map/ppermute | solution.py:35
  (179 shorter events, 38.0 us)
Async XLA Ops:
  0.6 3.5 %copy-start.5 = (f32[3,3072]{1,0:T(4,128)S(1)}, f32[3,3072]{1,0:T(4,128)}, u32[]{:S(2)}) copy-start(f32[3,3072]{1,0:T(4,128)} %param.20) | copy-start | bytes 110596
  5.0 1.5 slice-start
  5.0 16.9 %collective-permute-start.8 = (f32[1,59,256]{2,1,0:T(8,128)S(1)}, f32[1,59,256]{2,1,0:T(8,128)S(1)}, u32[]{:S(2)}, u32[]{:S(2)}) collective-permute-start(f32[1,59,256]{2,1,0:T(8,128)S(1)} %bitcast.77), channel_id=1, source_target_pairs={{0,1},{1,0},{2,3},{3,2},{4,5},{5,4},{6,7},{7,6},{8,9},{9,8},{10,11... | collective-permute-start | bytes 181256 | tf_op jit(solution)/shard_map/ppermute | solution.py:35
  7.6 4.7 %copy-start.2 = (f32[81,81]{1,0:T(8,128)S(1)}, f32[81,81]{1,0:T(8,128)}, u32[]{:S(2)}) copy-start(f32[81,81]{1,0:T(8,128)} %param.15) | copy-start | bytes 78736
  7.7 6.6 %collective-permute-start.4 = (f32[2,4,3,32]{3,2,1,0:T(4,128)S(1)}, f32[2,4,3,32]{3,2,1,0:T(4,128)S(1)}, u32[]{:S(2)}, u32[]{:S(2)}) collective-permute-start(f32[2,4,3,32]{3,2,1,0:T(4,128)S(1)} %get-tuple-element.36), channel_id=1, source_target_pairs={{0,4},{4,8},{8,12},{12,16},{16,20},{20,24},{24,28},{28,32},{32,36}... | collective-permute-start | bytes 9224 | tf_op jit(solution)/shard_map/ppermute | solution.py:39
  11.0 2.0 copy-start.6
  11.0 4.5 %collective-permute-start.5 = (f32[2,4,3,32]{3,2,1,0:T(4,128)S(1)}, f32[2,4,3,32]{3,2,1,0:T(4,128)S(1)}, u32[]{:S(2)}, u32[]{:S(2)}) collective-permute-start(f32[2,4,3,32]{3,2,1,0:T(4,128)S(1)} %get-tuple-element.37), channel_id=1, source_target_pairs={{4,0},{8,4},{12,8},{16,12},{20,16},{24,20},{28,24},{32,28},{36,32}... | collective-permute-start | bytes 9224 | tf_op jit(solution)/shard_map/ppermute | solution.py:39
  15.6 3.1 %collective-permute-start.6 = (f32[192,32]{1,0:T(8,128)S(1)}, f32[192,32]{1,0:T(8,128)S(1)}, u32[]{:S(2)}, u32[]{:S(2)}) collective-permute-start(f32[192,32]{1,0:T(8,128)S(1)} %pad_maximum_fusion.8), channel_id=1, source_target_pairs={{0,1},{1,0},{2,3},{3,2},{4,5},{5,4},{6,7},{7,6},{8,9},{9,8},{10,11... | collective-permute-start | bytes 73736 | tf_op jit(solution)/shard_map/ppermute | solution.py:35
  18.9 5.6 %collective-permute-start.7 = (f32[192,64]{1,0:T(8,128)S(1)}, f32[192,64]{1,0:T(8,128)S(1)}, u32[]{:S(2)}, u32[]{:S(2)}) collective-permute-start(f32[192,64]{1,0:T(8,128)S(1)} %pad_maximum_fusion.9), channel_id=1, source_target_pairs={{0,2},{1,3},{2,0},{3,1},{4,6},{5,7},{6,4},{7,5},{8,10},{9,11},{10,... | collective-permute-start | bytes 147464 | tf_op jit(solution)/shard_map/ppermute | solution.py:35
  21.9 6.0 %collective-permute-start.9 = (f32[2,59,256]{2,1,0:T(8,128)S(1)}, f32[2,59,256]{2,1,0:T(8,128)S(1)}, u32[]{:S(2)}, u32[]{:S(2)}) collective-permute-start(f32[2,59,256]{2,1,0:T(8,128)S(1)} %pad_maximum_fusion.7), channel_id=1, source_target_pairs={{0,2},{1,3},{2,0},{3,1},{4,6},{5,7},{6,4},{7,5},{8,10},{9,11},{10,... | collective-permute-start | bytes 362504 | tf_op jit(solution)/shard_map/ppermute | solution.py:35
  28.1 2.3 copy-start.4
  29.1 4.4 %collective-permute-start.10 = (f32[3,256]{1,0:T(4,128)S(1)}, f32[3,256]{1,0:T(4,128)S(1)}, u32[]{:S(2)}, u32[]{:S(2)}) collective-permute-start(f32[3,256]{1,0:T(4,128)S(1)} %bitcast.84), channel_id=1, source_target_pairs={{4,0},{8,4},{12,8},{16,12},{20,16},{24,20},{28,24},{32,28},{36,32}... | collective-permute-start | bytes 9224 | tf_op jit(solution)/shard_map/ppermute | solution.py:39
  36.0 7.4 %collective-permute-start.12 = (f32[3,256]{1,0:T(4,128)S(1)}, f32[3,256]{1,0:T(4,128)S(1)}, u32[]{:S(2)}, u32[]{:S(2)}) collective-permute-start(f32[3,256]{1,0:T(4,128)S(1)} %bitcast.89), channel_id=1, source_target_pairs={{4,0},{8,4},{12,8},{16,12},{20,16},{24,20},{28,24},{32,28},{36,32}... | collective-permute-start | bytes 9224 | tf_op jit(solution)/shard_map/ppermute | solution.py:39
  37.3 6.8 %collective-permute-start.11 = (f32[3,256]{1,0:T(4,128)S(1)}, f32[3,256]{1,0:T(4,128)S(1)}, u32[]{:S(2)}, u32[]{:S(2)}) collective-permute-start(f32[3,256]{1,0:T(4,128)S(1)} %bitcast.85), channel_id=1, source_target_pairs={{0,4},{4,8},{8,12},{12,16},{16,20},{20,24},{24,28},{28,32},{32,36}... | collective-permute-start | bytes 9224 | tf_op jit(solution)/shard_map/ppermute | solution.py:39
  44.2 3.2 %collective-permute-start.13 = (f32[3,56,256]{2,1,0:T(8,128)S(1)}, f32[3,56,256]{2,1,0:T(8,128)S(1)}, u32[]{:S(2)}, u32[]{:S(2)}) collective-permute-start(f32[3,56,256]{2,1,0:T(8,128)S(1)} %select_add_fusion.3), channel_id=1, source_target_pairs={{0,1},{1,0},{2,3},{3,2},{4,5},{5,4},{6,7},{7,6},{8,9},{9,8},{10,11... | collective-permute-start | bytes 516104 | tf_op jit(solution)/shard_map/ppermute | solution.py:35
  46.1 8.1 %collective-permute-start.15 = (f32[1,256]{1,0:T(1,128)S(1)}, f32[1,256]{1,0:T(1,128)S(1)}, u32[]{:S(2)}, u32[]{:S(2)}) collective-permute-start(f32[1,256]{1,0:T(1,128)S(1)} %slice.131), channel_id=1, source_target_pairs={{4,0},{8,4},{12,8},{16,12},{20,16},{24,20},{28,24},{32,28},{36,32}... | collective-permute-start | bytes 3080 | tf_op jit(solution)/shard_map/ppermute | solution.py:39
  47.5 11.4 %collective-permute-start.14 = (f32[3,56,256]{2,1,0:T(8,128)S(1)}, f32[3,56,256]{2,1,0:T(8,128)S(1)}, u32[]{:S(2)}, u32[]{:S(2)}) collective-permute-start(f32[3,56,256]{2,1,0:T(8,128)S(1)} %fusion.16.p_ref), channel_id=1, source_target_pairs={{0,2},{1,3},{2,0},{3,1},{4,6},{5,7},{6,4},{7,5},{8,10},{9,11},{10,... | collective-permute-start | bytes 516104 | tf_op jit(solution)/shard_map/ppermute | solution.py:35
  62.0 8.8 %collective-permute-start.17 = (f32[3,256]{1,0:T(4,128)S(1)}, f32[3,256]{1,0:T(4,128)S(1)}, u32[]{:S(2)}, u32[]{:S(2)}) collective-permute-start(f32[3,256]{1,0:T(4,128)S(1)} %bitcast.90), channel_id=1, source_target_pairs={{4,0},{8,4},{12,8},{16,12},{20,16},{24,20},{28,24},{32,28},{36,32}... | collective-permute-start | bytes 9224 | tf_op jit(solution)/shard_map/ppermute | solution.py:39
  63.3 8.2 %collective-permute-start.16 = (f32[3,256]{1,0:T(4,128)S(1)}, f32[3,256]{1,0:T(4,128)S(1)}, u32[]{:S(2)}, u32[]{:S(2)}) collective-permute-start(f32[3,256]{1,0:T(4,128)S(1)} %bitcast.86), channel_id=1, source_target_pairs={{0,4},{4,8},{8,12},{12,16},{16,20},{20,24},{24,28},{28,32},{32,36}... | collective-permute-start | bytes 9224 | tf_op jit(solution)/shard_map/ppermute | solution.py:39
  71.6 1.5 collective-permute-start.18
  73.2 10.0 %collective-permute-start.19 = (f32[3,56,256]{2,1,0:T(8,128)S(1)}, f32[3,56,256]{2,1,0:T(8,128)S(1)}, u32[]{:S(2)}, u32[]{:S(2)}) collective-permute-start(f32[3,56,256]{2,1,0:T(8,128)S(1)} %fusion.15.p_ref), channel_id=1, source_target_pairs={{0,2},{1,3},{2,0},{3,1},{4,6},{5,7},{6,4},{7,5},{8,10},{9,11},{10,... | collective-permute-start | bytes 516104 | tf_op jit(solution)/shard_map/ppermute | solution.py:35
  84.5 3.8 %collective-permute-start.20 = (f32[8,128]{1,0:T(8,128)S(1)}, f32[8,128]{1,0:T(8,128)S(1)}, u32[]{:S(2)}, u32[]{:S(2)}) collective-permute-start(f32[8,128]{1,0:T(8,128)S(1)} %pad_maximum_fusion.13), channel_id=1, source_target_pairs={{0,4},{1,5},{2,6},{3,7},{4,0},{5,1},{6,2},{7,3},{8,12},{9,13},{10,... | collective-permute-start | bytes 12296 | tf_op jit(solution)/shard_map/ppermute | solution.py:35
  88.3 12.0 %collective-permute-start.21 = (f32[8,128]{1,0:T(8,128)S(1)}, f32[8,128]{1,0:T(8,128)S(1)}, u32[]{:S(2)}, u32[]{:S(2)}) collective-permute-start(f32[8,128]{1,0:T(8,128)S(1)} %fusion.5), channel_id=1, source_target_pairs={{0,12},{1,13},{2,14},{3,15},{4,8},{5,9},{6,10},{7,11},{8,4},{9,5},... | collective-permute-start | bytes 12296 | tf_op jit(solution)/shard_map/ppermute | solution.py:35
  100.3 5.4 %collective-permute-start.22 = (f32[8,128]{1,0:T(8,128)S(1)}, f32[8,128]{1,0:T(8,128)S(1)}, u32[]{:S(2)}, u32[]{:S(2)}) collective-permute-start(f32[8,128]{1,0:T(8,128)S(1)} %add.95), channel_id=1, source_target_pairs={{0,16},{1,17},{2,18},{3,19},{4,20},{5,21},{6,22},{7,23},{8,24},{9,... | collective-permute-start | bytes 12296 | tf_op jit(solution)/shard_map/ppermute | solution.py:35
  105.7 2.5 %collective-permute-start.23 = (f32[8,128]{1,0:T(8,128)S(1)}, f32[8,128]{1,0:T(8,128)S(1)}, u32[]{:S(2)}, u32[]{:S(2)}) collective-permute-start(f32[8,128]{1,0:T(8,128)S(1)} %add.96), channel_id=1, source_target_pairs={{0,32},{1,33},{2,34},{3,35},{4,36},{5,37},{6,38},{7,39},{8,40},{9,... | collective-permute-start | bytes 12296 | tf_op jit(solution)/shard_map/ppermute | solution.py:35
  108.2 9.0 %collective-permute-start.24 = (f32[8,128]{1,0:T(8,128)S(1)}, f32[8,128]{1,0:T(8,128)S(1)}, u32[]{:S(2)}, u32[]{:S(2)}) collective-permute-start(f32[8,128]{1,0:T(8,128)S(1)} %add.97), channel_id=1, source_target_pairs={{0,96},{1,97},{2,98},{3,99},{4,100},{5,101},{6,102},{7,103},{8,104... | collective-permute-start | bytes 12296 | tf_op jit(solution)/shard_map/ppermute | solution.py:35
  117.8 5.3 %collective-permute-start.26 = (f32[1,128]{1,0:T(1,128)S(1)}, f32[1,128]{1,0:T(1,128)S(1)}, u32[]{:S(2)}, u32[]{:S(2)}) collective-permute-start(f32[1,128]{1,0:T(1,128)S(1)} %get-tuple-element.38), channel_id=1, source_target_pairs={{4,0},{8,4},{12,8},{16,12},{20,16},{24,20},{28,24},{32,28},{36,32}... | collective-permute-start | bytes 1544 | tf_op jit(solution)/shard_map/ppermute | solution.py:39
  119.1 4.7 %collective-permute-start.25 = (f32[1,128]{1,0:T(1,128)S(1)}, f32[1,128]{1,0:T(1,128)S(1)}, u32[]{:S(2)}, u32[]{:S(2)}) collective-permute-start(f32[1,128]{1,0:T(1,128)S(1)} %get-tuple-element.39), channel_id=1, source_target_pairs={{0,4},{4,8},{8,12},{12,16},{16,20},{20,24},{24,28},{28,32},{32,36}... | collective-permute-start | bytes 1544 | tf_op jit(solution)/shard_map/ppermute | solution.py:39
  125.1 4.6 %collective-permute-start.27 = (f32[3,256]{1,0:T(4,128)S(1)}, f32[3,256]{1,0:T(4,128)S(1)}, u32[]{:S(2)}, u32[]{:S(2)}) collective-permute-start(f32[3,256]{1,0:T(4,128)S(1)} %bitcast.93), channel_id=1, source_target_pairs={{4,0},{8,4},{12,8},{16,12},{20,16},{24,20},{28,24},{32,28},{36,32}... | collective-permute-start | bytes 9224 | tf_op jit(solution)/shard_map/ppermute | solution.py:39
  132.3 7.6 %collective-permute-start.29 = (f32[3,256]{1,0:T(4,128)S(1)}, f32[3,256]{1,0:T(4,128)S(1)}, u32[]{:S(2)}, u32[]{:S(2)}) collective-permute-start(f32[3,256]{1,0:T(4,128)S(1)} %bitcast.91), channel_id=1, source_target_pairs={{4,0},{8,4},{12,8},{16,12},{20,16},{24,20},{28,24},{32,28},{36,32}... | collective-permute-start | bytes 9224 | tf_op jit(solution)/shard_map/ppermute | solution.py:39
  133.6 7.0 %collective-permute-start.28 = (f32[3,256]{1,0:T(4,128)S(1)}, f32[3,256]{1,0:T(4,128)S(1)}, u32[]{:S(2)}, u32[]{:S(2)}) collective-permute-start(f32[3,256]{1,0:T(4,128)S(1)} %bitcast.87), channel_id=1, source_target_pairs={{0,4},{4,8},{8,12},{12,16},{16,20},{20,24},{24,28},{28,32},{32,36}... | collective-permute-start | bytes 9224 | tf_op jit(solution)/shard_map/ppermute | solution.py:39
  140.8 8.3 %collective-permute-start.30 = (f32[3,56,256]{2,1,0:T(8,128)S(1)}, f32[3,56,256]{2,1,0:T(8,128)S(1)}, u32[]{:S(2)}, u32[]{:S(2)}) collective-permute-start(f32[3,56,256]{2,1,0:T(8,128)S(1)} %select_add_fusion.1), channel_id=1, source_target_pairs={{0,1},{1,0},{2,3},{3,2},{4,5},{5,4},{6,7},{7,6},{8,9},{9,8},{10,11... | collective-permute-start | bytes 516104 | tf_op jit(solution)/shard_map/ppermute | solution.py:35
  149.2 12.1 %collective-permute-start.31 = (f32[3,56,256]{2,1,0:T(8,128)S(1)}, f32[3,56,256]{2,1,0:T(8,128)S(1)}, u32[]{:S(2)}, u32[]{:S(2)}) collective-permute-start(f32[3,56,256]{2,1,0:T(8,128)S(1)} %fusion.14.p_ref), channel_id=1, source_target_pairs={{0,2},{1,3},{2,0},{3,1},{4,6},{5,7},{6,4},{7,5},{8,10},{9,11},{10,... | collective-permute-start | bytes 516104 | tf_op jit(solution)/shard_map/ppermute | solution.py:35
  161.9 12.1 %copy-start = (f32[8,32,512]{2,1,0:T(8,128)S(1)}, f32[8,32,512]{2,1,0:T(8,128)}, u32[]{:S(2)}) copy-start(f32[8,32,512]{2,1,0:T(8,128)} %fs_ref.1) | copy-start | bytes 1572868
  161.9 12.1 %copy-start.1 = (f32[8,32,512]{2,1,0:T(8,128)S(1)}, f32[8,32,512]{2,1,0:T(8,128)}, u32[]{:S(2)}) copy-start(f32[8,32,512]{2,1,0:T(8,128)} %fd_ref.1) | copy-start | bytes 1572868
  164.3 8.2 %collective-permute-start.33 = (f32[3,256]{1,0:T(4,128)S(1)}, f32[3,256]{1,0:T(4,128)S(1)}, u32[]{:S(2)}, u32[]{:S(2)}) collective-permute-start(f32[3,256]{1,0:T(4,128)S(1)} %bitcast.92), channel_id=1, source_target_pairs={{4,0},{8,4},{12,8},{16,12},{20,16},{24,20},{28,24},{32,28},{36,32}... | collective-permute-start | bytes 9224 | tf_op jit(solution)/shard_map/ppermute | solution.py:39
  165.6 7.6 %collective-permute-start.32 = (f32[3,256]{1,0:T(4,128)S(1)}, f32[3,256]{1,0:T(4,128)S(1)}, u32[]{:S(2)}, u32[]{:S(2)}) collective-permute-start(f32[3,256]{1,0:T(4,128)S(1)} %bitcast.88), channel_id=1, source_target_pairs={{0,4},{4,8},{8,12},{12,16},{16,20},{20,24},{24,28},{28,32},{32,36}... | collective-permute-start | bytes 9224 | tf_op jit(solution)/shard_map/ppermute | solution.py:39
  174.0 7.5 %collective-permute-start.34 = (f32[3,56,256]{2,1,0:T(8,128)}, f32[3,56,256]{2,1,0:T(8,128)S(1)}, u32[]{:S(2)}, u32[]{:S(2)}) collective-permute-start(f32[3,56,256]{2,1,0:T(8,128)} %select_add_fusion), channel_id=1, source_target_pairs={{0,1},{1,0},{2,3},{3,2},{4,5},{5,4},{6,7},{7,6},{8,9},{9,8},{10,11... | collective-permute-start | bytes 516104 | tf_op jit(solution)/shard_map/ppermute | solution.py:35
  174.8 14.4 %collective-permute-start.1 = (f32[2,3,32,512]{3,2,1,0:T(8,128)}, f32[2,3,32,512]{3,2,1,0:T(8,128)S(1)}, u32[]{:S(2)}, u32[]{:S(2)}) collective-permute-start(f32[2,3,32,512]{3,2,1,0:T(8,128)} %get-tuple-element.16), channel_id=1, source_target_pairs={{4,0},{8,4},{12,8},{16,12},{20,16},{24,20},{28,24},{32,28},{36,32}... | collective-permute-start | bytes 1179656 | tf_op jit(solution)/shard_map/ppermute | solution.py:39
  176.1 13.9 %collective-permute-start = (f32[2,3,32,512]{3,2,1,0:T(8,128)S(1)}, f32[2,3,32,512]{3,2,1,0:T(8,128)S(1)}, u32[]{:S(2)}, u32[]{:S(2)}) collective-permute-start(f32[2,3,32,512]{3,2,1,0:T(8,128)S(1)} %get-tuple-element.17), channel_id=1, source_target_pairs={{0,4},{4,8},{8,12},{12,16},{16,20},{20,24},{24,28},{28,32},{32,36}... | collective-permute-start | bytes 1179656 | tf_op jit(solution)/shard_map/ppermute | solution.py:39
  181.6 18.9 %collective-permute-start.35 = (f32[3,56,256]{2,1,0:T(8,128)S(1)}, f32[3,56,256]{2,1,0:T(8,128)S(1)}, u32[]{:S(2)}, u32[]{:S(2)}) collective-permute-start(f32[3,56,256]{2,1,0:T(8,128)S(1)} %fusion.13.p_ref), channel_id=1, source_target_pairs={{0,2},{1,3},{2,0},{3,1},{4,6},{5,7},{6,4},{7,5},{8,10},{9,11},{10,... | collective-permute-start | bytes 516104 | tf_op jit(solution)/shard_map/ppermute | solution.py:35
  190.0 30.4 %collective-permute-start.3 = (f32[2,14,8,512]{3,2,1,0:T(8,128)S(1)}, f32[2,14,8,512]{3,2,1,0:T(8,128)S(1)}, u32[]{:S(2)}, u32[]{:S(2)}) collective-permute-start(f32[2,14,8,512]{3,2,1,0:T(8,128)S(1)} %get-tuple-element.14), channel_id=1, source_target_pairs={{1,0},{2,1},{3,2},{5,4},{6,5},{7,6},{9,8},{10,9},{11,10},{13,12},{... | collective-permute-start | bytes 1376264 | tf_op jit(solution)/shard_map/ppermute | solution.py:43
  192.7 27.8 %collective-permute-start.2 = (f32[2,14,8,512]{3,2,1,0:T(8,128)S(1)}, f32[2,14,8,512]{3,2,1,0:T(8,128)S(1)}, u32[]{:S(2)}, u32[]{:S(2)}) collective-permute-start(f32[2,14,8,512]{3,2,1,0:T(8,128)S(1)} %get-tuple-element.15), channel_id=1, source_target_pairs={{0,1},{1,2},{2,3},{4,5},{5,6},{6,7},{8,9},{9,10},{10,11},{12,13},{... | collective-permute-start | bytes 1376264 | tf_op jit(solution)/shard_map/ppermute | solution.py:43
  201.8 4.2 %collective-permute-start.36 = (f32[8,128]{1,0:T(8,128)S(1)}, f32[8,128]{1,0:T(8,128)S(1)}, u32[]{:S(2)}, u32[]{:S(2)}) collective-permute-start(f32[8,128]{1,0:T(8,128)S(1)} %pad_maximum_fusion.12), channel_id=1, source_target_pairs={{0,4},{1,5},{2,6},{3,7},{4,0},{5,1},{6,2},{7,3},{8,12},{9,13},{10,... | collective-permute-start | bytes 12296 | tf_op jit(solution)/shard_map/ppermute | solution.py:35
  206.0 9.7 %collective-permute-start.37 = (f32[8,128]{1,0:T(8,128)S(1)}, f32[8,128]{1,0:T(8,128)S(1)}, u32[]{:S(2)}, u32[]{:S(2)}) collective-permute-start(f32[8,128]{1,0:T(8,128)S(1)} %fusion.6), channel_id=1, source_target_pairs={{0,12},{1,13},{2,14},{3,15},{4,8},{5,9},{6,10},{7,11},{8,4},{9,5},... | collective-permute-start | bytes 12296 | tf_op jit(solution)/shard_map/ppermute | solution.py:35
  215.7 10.4 %collective-permute-start.38 = (f32[8,128]{1,0:T(8,128)S(1)}, f32[8,128]{1,0:T(8,128)S(1)}, u32[]{:S(2)}, u32[]{:S(2)}) collective-permute-start(f32[8,128]{1,0:T(8,128)S(1)} %add.107), channel_id=1, source_target_pairs={{0,16},{1,17},{2,18},{3,19},{4,20},{5,21},{6,22},{7,23},{8,24},{9,... | collective-permute-start | bytes 12296 | tf_op jit(solution)/shard_map/ppermute | solution.py:35
  226.1 2.5 %collective-permute-start.39 = (f32[8,128]{1,0:T(8,128)S(1)}, f32[8,128]{1,0:T(8,128)S(1)}, u32[]{:S(2)}, u32[]{:S(2)}) collective-permute-start(f32[8,128]{1,0:T(8,128)S(1)} %add.108), channel_id=1, source_target_pairs={{0,32},{1,33},{2,34},{3,35},{4,36},{5,37},{6,38},{7,39},{8,40},{9,... | collective-permute-start | bytes 12296 | tf_op jit(solution)/shard_map/ppermute | solution.py:35
  228.5 7.3 %collective-permute-start.40 = (f32[8,128]{1,0:T(8,128)S(1)}, f32[8,128]{1,0:T(8,128)S(1)}, u32[]{:S(2)}, u32[]{:S(2)}) collective-permute-start(f32[8,128]{1,0:T(8,128)S(1)} %add.109), channel_id=1, source_target_pairs={{0,96},{1,97},{2,98},{3,99},{4,100},{5,101},{6,102},{7,103},{8,104... | collective-permute-start | bytes 12296 | tf_op jit(solution)/shard_map/ppermute | solution.py:35
  (5 other events, 4.4 us)

commit v2 on v1

v2 whole, which is shorter than its diff:
```python
import functools

import jax
import jax.numpy as jnp
from jax import lax
from jax.experimental import pallas as pl
from jax.experimental.pallas import tpu as pltpu
from jax.sharding import PartitionSpec as P

F32 = jnp.float32
BF = jnp.bfloat16
AXES = ("gx", "gy")
N_GX = 32
N_DEV = 128
LR = 64
VR = 56
OWN = 48
CORE = 1
YHI = 2

pseudo_weight = 0.8
traction_scale = 30.0
motion_scale = 2.0
relax_weight = 0.5

VM = pl.BlockSpec(memory_space=pltpu.VMEM)
SM = pl.BlockSpec(memory_space=pltpu.SMEM)


def params(mib=40):
    return pltpu.CompilerParams(vmem_limit_bytes=mib << 20)


def swap(x, mask):
    return lax.ppermute(x, AXES, [(i, i ^ mask) for i in range(N_DEV)])


def from_gx(x, by):
    return lax.ppermute(x, "gx", [(i, i + by) for i in range(N_GX) if 0 <= i + by < N_GX])


def from_gy(x, by):
    return lax.ppermute(x, "gy", [(i, i + by) for i in range(4) if 0 <= i + by < 4])


def split(v):
    hi = v.astype(BF)
    return hi, (v - hi.astype(F32)).astype(BF)


def scale_of(stiff_ref):
    r = lax.broadcasted_iota(jnp.int32, (81, 81), 0)
    c = lax.broadcasted_iota(jnp.int32, (81, 81), 1)
    diag = jnp.where(r == c, stiff_ref[...], 0.0)
    trace = diag.sum(axis=1, keepdims=True).sum(axis=0, keepdims=True)
    return 1.0 / jnp.maximum(1.0, trace)


def fill_stiff(stiff_ref, s_scr):
    s_scr[...] = jnp.zeros_like(s_scr)
    hi, lo = split(jnp.pad(stiff_ref[...] * scale_of(stiff_ref), ((0, 15), (0, 7))))
    s_scr[0:96, :] = hi
    s_scr[96:192, :] = lo


def fill_table(v_ref, t_scr):
    for c in range(3):
        v = jnp.concatenate([v_ref[c], jnp.zeros((LR - VR, 256), F32)], axis=0)
        hi, lo = split(v)
        t_scr[c * LR : (c + 1) * LR, 0:256] = hi
        t_scr[c * LR : (c + 1) * LR, 256:512] = lo


def block_of(b):
    return pl.ds(pl.multiple_of(b * 128, 128), 128)


def forces_of(x, s_scr, coef_ref, live, b):
    xh, xl = split(x)
    r = jnp.dot(s_scr[...], xh, preferred_element_type=F32)
    prod = r[:88] + r[96:184] + jnp.dot(s_scr[0:96, :], xl, preferred_element_type=F32)[:88]
    slot = lax.broadcasted_iota(jnp.int32, (1, 128), 1) + b * 128
    return prod * jnp.where(slot < live, coef_ref[:, block_of(b)], 0.0)


def apply_body(live_ref, v_ref, conn_ref, coef_ref, stiff_ref, out_ref, t_scr, s_scr, oh_scr, ml_scr, x_scr, a_scr, acc):
    fill_table(v_ref, t_scr)
    fill_stiff(stiff_ref, s_scr)
    x_scr[80:88, :] = jnp.zeros((8, 128), F32)
    acc[...] = jnp.zeros_like(acc)
    i256 = lax.broadcasted_iota(jnp.int32, (256, 128), 0)
    i64 = lax.broadcasted_iota(jnp.int32, (LR, 128), 0)
    oh_scr[:, 27 * 128 :] = jnp.zeros((256, 128), BF)
    ml_scr[:, 27 * 128 :] = jnp.zeros((LR, 128), BF)
    a_scr[:, 27 * 128 :] = jnp.zeros((384, 128), BF)
    live = live_ref[0]

    def block(b, carry):
        for p in range(14):
            for h in range(2):
                k = 2 * p + h
                if k < 27:
                    sl = slice(k * 128, k * 128 + 128)
                    idx = conn_ref[k : k + 1, block_of(b)]
                    oh_scr[:, sl] = (i256 == (idx & 255)).astype(F32).astype(BF)
                    ml_scr[:, sl] = (i64 == (idx >> 8)).astype(F32).astype(BF)
            sp = slice(p * 256, p * 256 + 256)
            oh = oh_scr[:, sp]
            g = jnp.dot(t_scr[...], jnp.concatenate([oh, oh], axis=0), preferred_element_type=F32)
            m = ml_scr[:, sp].astype(F32)
            for c in range(3):
                s = (g[c * LR : (c + 1) * LR] * m).sum(axis=0, keepdims=True)
                for h in range(2):
                    k = 2 * p + h
                    if k < 27:
                        x_scr[c * 27 + k : c * 27 + k + 1, :] = s[:, h * 128 : h * 128 + 128]
        prod = forces_of(x_scr[...], s_scr, coef_ref, live, b)
        ph = prod.astype(BF).astype(F32)
        parts = (ph, prod - ph)
        for k in range(27):
            sl = slice(k * 128, k * 128 + 128)
            m = ml_scr[:, sl].reshape(4, 16, 128)
            for c in range(3):
                row = c * 27 + k
                for j, src in enumerate(parts):
                    r16 = jnp.broadcast_to(src[row : row + 1, :], (16, 128)).astype(BF)
                    at = j * 192 + c * LR
                    a_scr[at : at + LR, sl] = (m * r16[None]).reshape(LR, 128)
        acc[...] += lax.dot_general(
            a_scr[...], oh_scr[...], (((1,), (1,)), ((), ())), preferred_element_type=F32
        )
        return carry

    lax.fori_loop(0, (live + 127) // 128, block, 0)
    for c in range(3):
        s = acc[c * LR : (c + 1) * LR, :] + acc[192 + c * LR : 192 + (c + 1) * LR, :]
        out_ref[c] = s[:VR]


def stiff_apply(live, v, conn, coef, stiff):
    return pl.pallas_call(
        apply_body,
        out_shape=jax.ShapeDtypeStruct((3, VR, 256), F32),
        in_specs=[SM] + [VM] * 4,
        out_specs=VM,
        scratch_shapes=[
            pltpu.VMEM((192, 512), BF),
            pltpu.VMEM((192, 88), BF),
            pltpu.VMEM((256, 3584), BF),
            pltpu.VMEM((LR, 3584), BF),
            pltpu.VMEM((88, 128), F32),
            pltpu.VMEM((384, 3584), BF),
            pltpu.VMEM((384, 256), F32),
        ],
        compiler_params=params(),
    )(live, v, conn, coef, stiff)


def pack_parts_body(stiff_ref, load_ref, mass_ref, face_ref, tw_ref, normal_ref, out_ref):
    def put(at, row):
        out_ref[at : at + 1, :] = row[:, :128]
        out_ref[64 + at : 65 + at, :] = row[:, 128:]

    scale = scale_of(stiff_ref)
    for r in range(12):
        sl = slice(r * 256, r * 256 + 256)
        for c in range(3):
            put(c * 12 + r, load_ref[c : c + 1, sl])
        put(36 + r, mass_ref[:, sl] * scale)
    for k in range(4):
        put(48 + k, face_ref[k : k + 1, :].astype(F32))
        put(52 + k, tw_ref[k : k + 1, :])
    for c in range(3):
        put(56 + c, normal_ref[c : c + 1, :])
    zero = jnp.zeros((1, 256), F32)
    for r in range(59, 64):
        put(r, zero)


def pack_parts(stiff, load, mass, face, weight, normal):
    return pl.pallas_call(
        pack_parts_body,
        out_shape=jax.ShapeDtypeStruct((128, 128), F32),
        in_specs=[VM] * 6,
        out_specs=VM,
        compiler_params=params(),
    )(stiff, load, mass, face, weight, normal)


def pack_wall_body(at_ref, fs_ref, fd_ref, xa_ref, xb_ref, node_ref, ww_ref, out_ref):
    out_ref[...] = jnp.zeros_like(out_ref)
    even = jnp.full((32, 128), at_ref[0] & 1, jnp.int32) == 0
    for j, ref in enumerate((fs_ref, fd_ref)):
        for x in range(14):
            if x < 3:
                v = jnp.where(even, xb_ref[j, x], xa_ref[j, x])
            elif x < 11:
                v = ref[x - 3]
            else:
                v = jnp.where(even, xa_ref[j, x - 11], xb_ref[j, x - 11])
            t = v.T
            for z in range(4):
                at = j * 64 + z * 16 + x
                out_ref[at : at + 1, 0:32] = t[z : z + 1, :]
    for k in range(4):
        out_ref[128 + k * 8 : 136 + k * 8, 0:32] = node_ref[k].astype(F32)
        out_ref[160 + k * 8 : 168 + k * 8, 0:32] = ww_ref[k]
    out_ref[...] = pltpu.roll(out_ref[...], at_ref[1] * 32, 1)


def pack_wall(at, fs, fd, xa, xb, node, weight):
    def block(*shape):
        return pl.BlockSpec(shape, lambda i: (0,) * len(shape))

    return pl.pallas_call(
        pack_wall_body,
        grid=(1,),
        out_shape=jax.ShapeDtypeStruct((192, 128), F32),
        in_specs=[
            SM,
            block(8, 32, 128),
            block(8, 32, 128),
            block(2, 3, 32, 128),
            block(2, 3, 32, 128),
            block(4, 8, 32),
            block(4, 8, 32),
        ],
        out_specs=block(192, 128),
        compiler_params=params(),
    )(at, fs, fd, xa, xb, node, weight)


def source_of(vec_ref, seg_ref, pick_ref):
    rows = []
    for g in range(4):
        total = jnp.zeros((1, 256), F32)
        for c in range(3):
            total = total + seg_ref[g, 8 + c : 9 + c, :] * vec_ref[c, 12 * g : 12 * g + 1, :]
        rows.append(total)
    return split(jnp.concatenate(rows + [jnp.zeros((4, 256), F32)], axis=0))


def settle_body(*refs, first):
    at_ref, live_ref, p_ref, q_ref, mass_ref, v_ref, conn_ref, coef_ref, stiff_ref = refs[:9]
    if first:
        seg_ref, pick_ref, w_ref, out_ref, ws_ref = refs[9:14]
    else:
        w_ref, out_ref = refs[9:11]
    t_scr, s_scr, x_scr, acc = refs[-4:]
    keep = lax.broadcasted_iota(jnp.int32, (VR, 256), 0)
    end = jnp.where(at_ref[0] == N_GX - 1, OWN, OWN + 1)
    mask = (keep < end).astype(F32)
    mass = mass_ref[...]
    dots = [jnp.zeros((8, 256), F32) for _ in range(4)]
    for c in range(3):
        v = v_ref[c]
        w = (p_ref[c] + q_ref[c] + mass * v) * mask
        w_ref[c] = w
        for i, (x, y) in enumerate(((v, v), (v, w), (w, w), (w, mass * w))):
            dots[i] = dots[i] + (x[:OWN] * y[:OWN]).reshape(6, 8, 256).sum(axis=0)
    dots = [0.25 * d.sum(axis=0, keepdims=True).sum(axis=1, keepdims=True) for d in dots]

    if first:
        hf, lf = source_of(v_ref, seg_ref, pick_ref)
        hw, lw = source_of(w_ref, seg_ref, pick_ref)
        table = jnp.concatenate([hf, lf, hw, lw], axis=0)
        n256 = lax.broadcasted_iota(jnp.int32, (256, 128), 0)
        n8 = lax.broadcasted_iota(jnp.int32, (8, 128), 0)
        for x in range(8):
            tf = jnp.zeros((8, 128), F32)
            tw = jnp.zeros((8, 128), F32)
            for k in range(4):
                row = k * 8 + x
                node = pick_ref[row : row + 1, :].astype(jnp.int32)
                oh = (n256 == (node & 255)).astype(F32).astype(BF)
                r = jnp.dot(table, oh, preferred_element_type=F32)
                u = jnp.where(n8 == (node >> 8), pick_ref[32 + row : 33 + row, :], 0.0)
                tf = tf + (r[0:8] + r[8:16]) * u
                tw = tw + (r[16:24] + r[24:32]) * u
            ws_ref[x : x + 1, :] = (motion_scale * relax_weight) * tf.sum(axis=0, keepdims=True)
            ws_ref[8 + x : 9 + x, :] = (motion_scale * relax_weight) * tw.sum(axis=0, keepdims=True)

    fill_table(w_ref, t_scr)
    fill_stiff(stiff_ref, s_scr)
    acc[...] = jnp.zeros_like(acc)
    x_scr[80:88, :] = jnp.zeros((8, 128), F32)
    i256 = lax.broadcasted_iota(jnp.int32, (256, 128), 0)
    i64 = lax.broadcasted_iota(jnp.int32, (LR, 128), 0)
    live = live_ref[0]

    def block(b, carry):
        for p in range(14):
            pieces, masks = [], []
            for k in (2 * p, 2 * p + 1):
                idx = conn_ref[min(k, 26) : min(k, 26) + 1, block_of(b)]
                pieces.append((i256 == (idx & 255)).astype(F32).astype(BF))
                masks.append((i64 == (idx >> 8)).astype(F32))
            oh = jnp.concatenate(pieces, axis=1)
            g = jnp.dot(t_scr[...], jnp.concatenate([oh, oh], axis=0), preferred_element_type=F32)
            m = jnp.concatenate(masks, axis=1)
            for c in range(3):
                s = (g[c * LR : (c + 1) * LR] * m).sum(axis=0, keepdims=True)
                for h in range(2):
                    k = 2 * p + h
                    if k < 27:
                        x_scr[c * 27 + k : c * 27 + k + 1, :] = s[:, h * 128 : h * 128 + 128]
        x = x_scr[...]
        acc[...] += (forces_of(x, s_scr, coef_ref, live, b) * x).sum(axis=0, keepdims=True)
        return carry

    lax.fori_loop(0, (live + 127) // 128, block, 0)
    dots[3] = dots[3] + acc[...].sum(axis=1, keepdims=True)
    lane = lax.broadcasted_iota(jnp.int32, (1, 128), 1)
    row = jnp.zeros((1, 128), F32)
    for i in range(4):
        row = jnp.where(lane == i, dots[i], row)
    row = jnp.broadcast_to(row, (N_DEV, 128))
    if first:
        peer = lax.broadcasted_iota(jnp.int32, (N_DEV, 128), 0) >> 2
        after = peer > at_ref[0]
        out_ref[pl.ds(0, N_DEV, 4), :] = row
        out_ref[pl.ds(1, N_DEV, 4), :] = jnp.where(after, ws_ref[7:8, :], ws_ref[0:1, :])
        out_ref[pl.ds(2, N_DEV, 4), :] = jnp.where(after, ws_ref[15:16, :], ws_ref[8:9, :])
        out_ref[pl.ds(3, N_DEV, 4), :] = jnp.zeros((N_DEV, 128), F32)
    else:
        out_ref[...] = row


def settle(at, live, p, q, mass, v, conn, coef, stiff, wall=()):
    first = bool(wall)
    shapes = [(3, VR, 256), (4 * N_DEV, 128), (16, 128)] if first else [(3, VR, 256), (N_DEV, 128)]
    return pl.pallas_call(
        functools.partial(settle_body, first=first),
        out_shape=tuple(jax.ShapeDtypeStruct(x, F32) for x in shapes),
        in_specs=[SM, SM] + [VM] * (7 + len(wall)),
        out_specs=(VM,) * len(shapes),
        scratch_shapes=[
            pltpu.VMEM((192, 512), BF),
            pltpu.VMEM((192, 88), BF),
            pltpu.VMEM((88, 128), F32),
            pltpu.VMEM((1, 128), F32),
        ],
        compiler_params=params(),
    )(at, live, p, q, mass, v, conn, coef, stiff, *wall)


def rows_in(at_ref):
    x = lax.broadcasted_iota(jnp.int32, (16, 128), 0) + at_ref[0] * 8 - 3
    return ((x >= 0) & (x < N_GX * 8)).astype(F32)


def wall_step(p, gain, force, inside, depth):
    lane = lax.broadcasted_iota(jnp.int32, (16, 128), 1)
    out = []
    for z in range(depth):
        c = p[z]
        n = pltpu.roll(c, 1, 0) + pltpu.roll(c, 15, 0)
        n = n + jnp.where(lane == 0, 0.0, pltpu.roll(c, 1, 1))
        n = n + jnp.where(lane == 127, 0.0, pltpu.roll(c, 127, 1))
        n = n + p[z + 1]
        if z > 0:
            n = n + p[z - 1]
        out.append(((1.0 - pseudo_weight) * c + gain[z] * (force[z] + n)) * inside)
    return out


def wall_front(at_ref, slab_ref):
    inside = rows_in(at_ref)
    fs = [slab_ref[z * 16 : z * 16 + 16, :] for z in range(4)]
    gain = [pseudo_weight / (6.0 + slab_ref[64 + z * 16 : 64 + z * 16 + 16, :]) for z in range(4)]
    p1 = [gain[z] * fs[z] * inside for z in range(4)]
    p2 = wall_step(p1, gain, fs, inside, 3)
    return inside, fs, gain, p2


def push(wall16, load_ref, seg_ref, f_ref):
    wall = pltpu.roll(wall16, 13, 0)[0:8]
    hi, lo = split(wall)
    table = jnp.concatenate([hi, lo], axis=0)
    i128 = lax.broadcasted_iota(jnp.int32, (128, 256), 0)
    i8 = lax.broadcasted_iota(jnp.int32, (8, 256), 0)
    f_ref[...] = load_ref[...]
    for g in range(4):
        total = jnp.zeros((8, 256), F32)
        for k in range(4):
            face = seg_ref[g, k : k + 1, :].astype(jnp.int32)
            oh = (i128 == ((face >> 8) * 32 + (face & 31))).astype(F32).astype(BF)
            r = jnp.dot(table, oh, preferred_element_type=F32)
            w = jnp.where(i8 == ((face >> 5) & 7), seg_ref[g, 4 + k : 5 + k, :], 0.0)
            total = total + (r[:8] + r[8:]) * w
        traction = total.sum(axis=0, keepdims=True)
        for c in range(3):
            f_ref[c, 12 * g : 12 * g + 1, :] = (
                f_ref[c, 12 * g : 12 * g + 1, :]
                + traction_scale * traction * seg_ref[g, 8 + c : 9 + c, :]
            )


def first_body(at_ref, slab_ref, load_ref, seg_ref, f_ref):
    inside, fs, gain, p2 = wall_front(at_ref, slab_ref)
    push(p2[0], load_ref, seg_ref, f_ref)


def first_force(at, slab, load, seg):
    return pl.pallas_call(
        first_body,
        out_shape=jax.ShapeDtypeStruct((3, VR, 256), F32),
        in_specs=[SM, VM, VM, VM],
        out_specs=VM,
        compiler_params=params(),
    )(at, slab, load, seg)


def weights_of(sums, stiff_ref):
    lane = lax.broadcasted_iota(jnp.int32, (1, 128), 1)
    a, b, c, d = [jnp.where(lane == i, sums, 0.0).sum(axis=1, keepdims=True) for i in range(4)]
    inv = scale_of(stiff_ref)
    alpha = a / b
    beta = (c - b * (b / a)) / (d - c * (c / b))
    return (alpha + beta * (alpha * (c / b))) * inv, -(alpha * beta) * inv


def second_body(at_ref, got_ref, stiff_ref, ws_ref, slab_ref, load_ref, seg_ref, f_ref, wall_ref, sums_ref):
    inside, fs, gain, p2 = wall_front(at_ref, slab_ref)
    sums = got_ref[pl.ds(0, N_DEV, 4), :].sum(axis=0, keepdims=True)
    sums_ref[...] = jnp.broadcast_to(sums, (8, 128))
    c0, c1 = weights_of(sums, stiff_ref)
    gx = at_ref[0]
    wall_ref[...] = jnp.zeros_like(wall_ref)
    wall_ref[3:11, :] = c0 * ws_ref[0:8, :] + c1 * ws_ref[8:16, :]
    for row, by, edge in ((2, -1, 0), (11, 1, N_GX - 1)):
        peer = jnp.clip(gx + by, 0, N_GX - 1) * 4 + at_ref[1]
        got = c0 * got_ref[pl.ds(peer * 4 + 1, 1), :] + c1 * got_ref[pl.ds(peer * 4 + 2, 1), :]
        wall_ref[row : row + 1, :] = jnp.where(jnp.full((1, 128), gx, jnp.int32) == edge, 0.0, got)
    force = [fs[0] + wall_ref[...], fs[1]]
    p3 = wall_step(p2, gain, force, inside, 2)
    p4 = wall_step(p3, gain, force, inside, 1)
    push(p4[0], load_ref, seg_ref, f_ref)


def second_force(at, got, stiff, ws, slab, load, seg):
    return pl.pallas_call(
        second_body,
        out_shape=(
            jax.ShapeDtypeStruct((3, VR, 256), F32),
            jax.ShapeDtypeStruct((16, 128), F32),
            jax.ShapeDtypeStruct((8, 128), F32),
        ),
        in_specs=[SM] + [VM] * 6,
        out_specs=(VM, VM, VM),
        compiler_params=params(),
    )(at, got, stiff, ws, slab, load, seg)


def fluid_body(at_ref, fs_ref, fd_ref, xa_ref, xb_ref, sib_ref, mid_ref, ws_ref, out_ref, src, gain, pa, pb):
    odd = jnp.full((4, 512), at_ref[1] & 1, jnp.int32) == 1
    even = jnp.full((32, 512), at_ref[0] & 1, jnp.int32) == 0
    zero = jnp.zeros((4, 512), F32)
    for j, (ref, dst) in enumerate(((fs_ref, src), (fd_ref, gain))):
        for x in range(14):
            if x < 3:
                own = jnp.where(even, xb_ref[j, x], xa_ref[j, x])
            elif x < 11:
                own = ref[x - 3]
            else:
                own = jnp.where(even, xa_ref[j, x - 11], xb_ref[j, x - 11])
            dst[x, 8:40, :] = own
            sib, mid = sib_ref[j, x], mid_ref[j, x]
            dst[x, 0:8, :] = jnp.concatenate([zero, jnp.where(odd, sib, mid)], axis=0)
            dst[x, 40:48, :] = jnp.concatenate([jnp.where(odd, mid, sib), zero], axis=0)
    lane = lax.broadcasted_iota(jnp.int32, (48, 512), 1)
    y = lax.broadcasted_iota(jnp.int32, (48, 512), 0) + at_ref[1] * 32 - 8
    y_in = ((y >= 0) & (y < 128)).astype(F32)

    def x_in(x):
        gx = at_ref[0] * 8 + x - 3
        return jnp.where((gx >= 0) & (gx < N_GX * 8), 1.0, 0.0).astype(F32)

    def start(x, carry):
        g = pseudo_weight / (6.0 + gain[x]) * (y_in * x_in(x))
        gain[x] = g
        pa[x] = g * src[x]
        return carry

    lax.fori_loop(0, 14, start, 0)

    def new_row(p, x):
        c = p[x]
        n = p[x - 1] + p[x + 1] + pltpu.roll(c, 1, 0) + pltpu.roll(c, 47, 0)
        n = n + jnp.where(lane == 0, 0.0, pltpu.roll(c, 1, 1))
        n = n + jnp.where(lane == 511, 0.0, pltpu.roll(c, 511, 1))
        return (1.0 - pseudo_weight) * c + gain[x] * (src[x] + n)

    def second(x, carry):
        pb[x] = new_row(pa, x)
        return carry

    lax.fori_loop(1, 13, second, 0)

    def add_source(x, carry):
        src[x, :, 0:128] = src[x, :, 0:128] + ws_ref[x]
        return carry

    lax.fori_loop(2, 12, add_source, 0)

    def third(x, carry):
        pa[x] = new_row(pb, x)
        return carry

    lax.fori_loop(2, 12, third, 0)

    def fourth(x, carry):
        out_ref[x - 3] = new_row(pa, x)[8:40]
        return carry

    lax.fori_loop(3, 11, fourth, 0)


def fluid(at, fs, fd, xa, xb, sib, mid, ws):
    return pl.pallas_call(
        fluid_body,
        out_shape=jax.ShapeDtypeStruct((8, 32, 512), F32),
        in_specs=[SM] + [VM] * 7,
        out_specs=VM,
        scratch_shapes=[pltpu.VMEM((14, 48, 512), F32)] * 4,
        compiler_params=params(),
    )(at, fs, fd, xa, xb, sib, mid, ws)


def last_body(s1_ref, got_ref, stiff_ref, f1_ref, w1_ref, f2_ref, w2_ref, out_ref):
    c0, c1 = weights_of(s1_ref[0:1, :], stiff_ref)
    d0, d1 = weights_of(got_ref[...].sum(axis=0, keepdims=True), stiff_ref)
    for c in range(3):
        before = relax_weight * (c0 * f1_ref[c] + c1 * w1_ref[c])
        solved = d0 * f2_ref[c] + d1 * w2_ref[c]
        out_ref[c] = before + relax_weight * (solved - before)


def last(s1, got, stiff, f1, w1, f2, w2):
    return pl.pallas_call(
        last_body,
        out_shape=jax.ShapeDtypeStruct((3, 12, 256), F32),
        in_specs=[VM] * 7,
        out_specs=VM,
        compiler_params=params(),
    )(s1, got, stiff, f1, w1, f2, w2)


def local(
    fluid_source,
    fluid_diag,
    stiff_ref,
    elem_coef,
    connect,
    live_count,
    node_mass,
    solid_load,
    wet_normal,
    trac_face,
    trac_weight,
    wall_node,
    wall_weight,
):
    gx = lax.axis_index("gx")
    gy = lax.axis_index("gy")
    core = gy & 1
    yhi = gy >> 1
    at = jnp.stack([gx, gy]).astype(jnp.int32)

    def in_order(bit, own, other):
        return jnp.concatenate([jnp.where(bit == 0, own, other), jnp.where(bit == 0, other, own)], axis=0)

    even = gx % 2 == 0

    def beside(to_low, to_high):
        first = [(i, i ^ 1) for i in range(N_GX)]
        second = [(i, i + 1) for i in range(1, N_GX - 1, 2)] + [(i + 1, i) for i in range(1, N_GX - 1, 2)]
        a = lax.ppermute(jnp.where(even, to_high, to_low), "gx", first)
        b = lax.ppermute(jnp.where(even, to_low, to_high), "gx", second)
        return a, b

    both = jnp.stack([fluid_source, fluid_diag])
    xa, xb = beside(both[:, 0:3], both[:, 5:8])

    own = pack_parts(
        stiff_ref, solid_load, node_mass.reshape(1, 3072), trac_face, trac_weight, wet_normal
    )
    wide = pack_wall(at, fluid_source, fluid_diag, xa, xb, wall_node, wall_weight)
    near = swap(jnp.concatenate([own, wide], axis=0), CORE)
    pair = jnp.concatenate([in_order(core, own, near[:128]), wide + near[128:]], axis=0)
    far = swap(pair, YHI)
    wide = pair[256:] + far[256:]
    slab, pick = wide[:128], wide[128:]
    parts = in_order(yhi, pair[:256], far[:256]).reshape(4, 2, 64, 128)
    parts = jnp.concatenate([parts[:, 0], parts[:, 1]], axis=2)
    seg = parts[:, 48:64]
    load = parts[:, :36].reshape(4, 3, 12, 256).transpose(1, 0, 2, 3).reshape(3, OWN, 256)
    load = jnp.pad(load, ((0, 0), (0, VR - OWN), (0, 0)))
    mass = jnp.pad(parts[:, 36:48].reshape(OWN, 256), ((0, VR - OWN), (0, 0)))
    coef = elem_coef.reshape(1, 384)
    row = lax.broadcasted_iota(jnp.int32, (3, VR, 256), 1)

    def to_all(x):
        return lax.all_to_all(x, AXES, 0, 0, tiled=True)

    def pair_sum(v):
        s = stiff_apply(live_count, v, connect, coef, stiff_ref)
        a, b = beside(s[:, 0, :], s[:, OWN, :])
        below, above = jnp.where(even, b, a), jnp.where(even, a, b)
        s = s + jnp.where(row == 0, below[:, None, :], 0.0) + jnp.where(row == OWN, above[:, None, :], 0.0)
        return s + swap(s, CORE)

    f1 = first_force(at, slab, load, seg)
    following = from_gx(jnp.concatenate([f1[:, 0, :], mass[0:1]], axis=0), -1)
    f1 = jnp.where(row == OWN, following[0:3, None, :], f1)
    mass = jnp.where(row[0] == OWN, following[3:4], mass)
    pair1 = pair_sum(f1)

    xlo, xhi = jnp.where(even, xb, xa), jnp.where(even, xa, xb)
    low = jnp.concatenate([xlo[:, :, 0:4], both[:, :, 0:4], xhi[:, :, 0:4]], axis=1)
    high = jnp.concatenate([xlo[:, :, 28:32], both[:, :, 28:32], xhi[:, :, 28:32]], axis=1)
    sides = (jnp.where(core == 0, high, low), jnp.where(core == 0, low, high))
    sides, pair1 = lax.optimization_barrier((sides, pair1))
    other1 = swap(pair1, YHI)
    sib = swap(sides[0], CORE)
    mid = lax.ppermute(sides[1], "gy", [(1, 2), (2, 1)])
    pair1, sib, mid = lax.optimization_barrier((pair1, sib, mid))
    w1, out1, wsb = settle(at, live_count, pair1, other1, mass, f1, connect, coef, stiff_ref, (seg, pick))
    f2, ws, s1 = second_force(at, to_all(out1), stiff_ref, wsb, slab, load, seg)
    following = from_gx(f2[:, 0, :], -1)
    f2 = jnp.where(row == OWN, following[:, None, :], f2)
    pair2 = pair_sum(f2)

    padded = jnp.pad(ws, ((0, 0), (8, 8)))
    wall = lax.dynamic_slice_in_dim(padded, gy * 32, 48, axis=1)
    lane = lax.broadcasted_iota(jnp.int32, (16, 48, 128), 2)
    wall = jnp.where(lane == 0, wall[:, :, None], 0.0)
    wall, pair2 = lax.optimization_barrier((wall, pair2))
    other2 = swap(pair2, YHI)
    pressure = fluid(at, fluid_source, fluid_diag, xa, xb, sib, mid, wall)
    pair2, pressure = lax.optimization_barrier((pair2, pressure))
    w2, out2 = settle(at, live_count, pair2, other2, mass, f2, connect, coef, stiff_ref)

    def mine(x):
        return lax.dynamic_slice_in_dim(x, gy * 12, 12, axis=1)

    displacement = last(s1, to_all(out2), stiff_ref, mine(f1), mine(w1), mine(f2), mine(w2)).reshape(3, 3072)
    return pressure, displacement


def solution(mesh):
    in_specs = (
        P("gx", "gy", None),
        P("gx", "gy", None),
        P(),
        P(("gx", "gy")),
        P(None, ("gx", "gy")),
        P(("gx", "gy")),
        P(("gx", "gy")),
        P(None, ("gx", "gy")),
        P(None, ("gx", "gy")),
        P(None, ("gx", "gy")),
        P(None, ("gx", "gy")),
        P(None, "gx", "gy"),
        P(None, "gx", "gy"),
    )
    out_specs = (P("gx", "gy", None), P(None, ("gx", "gy")))
    return jax.shard_map(local, mesh=mesh, in_specs=in_specs, out_specs=out_specs, check_vma=False)
```

time: 239 us -> 153 us (0.64); the launches traced: 237 us -> 155 us
  starting transfers between devices: 155 us -> 66.6 us
  Pallas kernels: 21.8 us -> 28.1 us
  waiting for transfers between devices: 46.3 us -> 49.9 us
    ppermute x22 -> x7, starting transfers between devices: 92.3 us -> 10 us  [swap(): return lax.ppermute(x, AXES, [(i, i ^ mask) for i in range(N_DEV)])]
    ppermute x17 -> x2, starting transfers between devices: 52.3 us -> 2.57 us  [from_gx(): lax.ppermute(x, 'gx', [(i, i + by) for i in range(N_GX) if 0 <= i + by <...]
    all_to_all x0 -> x2, starting transfers between devices: none -> 31.6 us  [to_all(): return lax.all_to_all(x, AXES, 0, 0, tiled=True)]
    ppermute x22 -> x7, waiting for transfers between devices: 32.9 us -> 10.6 us  [swap(): return lax.ppermute(x, AXES, [(i, i ^ mask) for i in range(N_DEV)])]
    all_to_all x0 -> x2, waiting for transfers between devices: none -> 20.4 us  [to_all(): return lax.all_to_all(x, AXES, 0, 0, tiled=True)]
    ppermute x2 -> x7, waiting for transfers between devices: 0.01 us -> 13.9 us  [the longest x3 9.39 us: beside(): a = lax.ppermute(jnp.where(even, to_high, to_low), 'gx', first)]
    ppermute x2 -> x7, starting transfers between devices: 10.5 us -> 22.5 us  [the longest x3 14.2 us: beside(): a = lax.ppermute(jnp.where(even, to_high, to_low), 'gx', first)]
    ppermute x17 -> x2, waiting for transfers between devices: 13.4 us -> 5 us  [from_gx(): lax.ppermute(x, 'gx', [(i, i + by) for i in range(N_GX) if 0 <= i + by <...]
  transfers between devices with their start and end apart: 41 -> 18, of which waited for: 27 -> 14; matrix products, arithmetic and copies ran while one was open for 1% -> 2% of each run, Pallas kernels for 3% -> 4%
where the time goes in v2:
time: 153 us; the launch traced here: 155 us
  starting transfers between devices  66.6 us (44%)
  waiting for transfers between devices  49.9 us (33%)
  Pallas kernels  28.1 us (18%)
  local copies, waits for them, and re-layouts  4.07 us (3%)
  other arithmetic  3.94 us (3%)
  between operations  1.93 us (1%)
    all_to_all x2, starting transfers between devices, to_all(): return lax.all_to_all(x, AXES, 0, 0, tiled=True)  31.6 us
    all_to_all x2, waiting for transfers between devices, to_all(): return lax.all_to_all(x, AXES, 0, 0, tiled=True)  20.4 us
    ppermute x3, starting transfers between devices, beside(): a = lax.ppermute(jnp.where(even, to_high, to_low), 'gx', first)  14.2 us
    ppermute x7, waiting for transfers between devices, swap(): return lax.ppermute(x, AXES, [(i, i ^ mask) for i in range(N_DEV)])  10.6 us
    ppermute x7, starting transfers between devices, swap(): return lax.ppermute(x, AXES, [(i, i ^ mask) for i in range(N_DEV)])  10 us
    pallas_call x2, Pallas kernels, settle(): pl.pallas_call(functools.partial(settle_body, first=first), out_shape=tup...  9.85 us
    pallas_call x2, Pallas kernels, stiff_apply(): pl.pallas_call(apply_body, out_shape=jax.ShapeDtypeStruct((3, VR, 256), F...  9.54 us
    ppermute x3, waiting for transfers between devices, beside(): a = lax.ppermute(jnp.where(even, to_high, to_low), 'gx', first)  9.39 us
  transfers between devices with their start and end apart: 18, of which 14 were waited for; matrix products, arithmetic and copies ran while one was open for 2% of the time, Pallas kernels for 4%

profile of v2, /device:TPU:1, one launch (start us, length us, event | category | flops | bytes accessed | tf_op | source)
XLA Modules:
  0.0 154.6 jit_solution(4558791995229121500)
XLA Ops:
  0.7 1.7 %broadcast_select_fusion.4 = (f32[2,3,32,512]{3,2,1,0:T(8,128)S(1)}, f32[2,3,32,512]{3,2,1,0:T(8,128)S(1)}) fusion(pred[]{:T(512)S(6)} %eq.50, f32[1,8,32,512]{3,2,1,0:T(8,128)} %bitcast.45, f32[1,8,32,512]{3,2,1,0:T(8,128)} %bitcast.42), kind=kLoop, calls=%fused_computation.22 | loop fusion | flops 589824 | bytes 1835009 | tf_op jit(solution)/shard_map/jit(_where)/select_n | solution.py:579
  2.4 0.7 collective-permute-start
  3.1 4.6 %collective-permute-start.1 = (f32[2,3,32,512]{3,2,1,0:T(8,128)S(1)}, f32[2,3,32,512]{3,2,1,0:T(8,128)S(1)}, u32[]{:S(2)}, u32[]{:S(2)}) collective-permute-start(f32[2,3,32,512]{3,2,1,0:T(8,128)S(1)} %get-tuple-element.41), channel_id=1, source_target_pairs={{0,4},{4,0},{8,12},{12,8},{16,20},{20,16},{24,28},{28,24},{32,36},... | collective-permute-start | bytes 1179656 | tf_op jit(solution)/shard_map/ppermute | solution.py:578
  7.7 0.1 shard_map.141
  7.9 8.3 %collective-permute-done.1.xa_ref = f32[2,3,32,512]{3,2,1,0:T(8,128)S(1)} collective-permute-done((f32[2,3,32,512]{3,2,1,0:T(8,128)S(1)}, f32[2,3,32,512]{3,2,1,0:T(8,128)S(1)}, u32[]{:S(2)}, u32[]{:S(2)}) %collective-permute-start.1) | collective-permute-done | bytes 393248 | tf_op jit(solution)/shard_map/ppermute | solution.py:578
  16.2 0.8 shard_map.140
  17.0 1.6 %collective-permute-start.2 = (f32[320,128]{1,0:T(8,128)S(1)}, f32[320,128]{1,0:T(8,128)S(1)}, u32[]{:S(2)}, u32[]{:S(2)}) collective-permute-start(f32[320,128]{1,0:T(8,128)S(1)} %pad_maximum_fusion.4), channel_id=1, source_target_pairs={{0,1},{1,0},{2,3},{3,2},{4,5},{5,4},{6,7},{7,6},{8,9},{9,8},{10,11... | collective-permute-start | bytes 491528 | tf_op jit(solution)/shard_map/ppermute | solution.py:35
  19.4 0.3 collective-permute-done.2
  19.8 3.0 %collective-permute-start.3 = (f32[448,128]{1,0:T(8,128)S(1)}, f32[448,128]{1,0:T(8,128)S(1)}, u32[]{:S(2)}, u32[]{:S(2)}) collective-permute-start(f32[448,128]{1,0:T(8,128)S(1)} %pad_maximum_fusion.3), channel_id=1, source_target_pairs={{0,2},{1,3},{2,0},{3,1},{4,6},{5,7},{6,4},{7,5},{8,10},{9,11},{10,... | collective-permute-start | bytes 688136 | tf_op jit(solution)/shard_map/ppermute | solution.py:35
  22.7 1.0 broadcast_select_fusion.2
  23.7 4.4 %collective-permute-done.3 = f32[448,128]{1,0:T(8,128)S(1)} collective-permute-done((f32[448,128]{1,0:T(8,128)S(1)}, f32[448,128]{1,0:T(8,128)S(1)}, u32[]{:S(2)}, u32[]{:S(2)}) %collective-permute-start.3) | collective-permute-done | bytes 229408 | tf_op jit(solution)/shard_map/ppermute | solution.py:35
  28.4 0.5 copy-done.11
  29.0 1.0 shard_map.142
  30.0 0.7 slice-done
  30.7 1.3 collective-permute-start.4
  32.0 1.1 fusion.11
  33.1 2.0 %collective-permute-done.4 = f32[4,256]{1,0:T(4,128)S(1)} collective-permute-done((f32[4,256]{1,0:T(4,128)S(1)}, f32[4,256]{1,0:T(4,128)S(1)}, u32[]{:S(2)}, u32[]{:S(2)}) %collective-permute-start.4) | collective-permute-done | bytes 4128 | tf_op jit(solution)/shard_map/ppermute | solution.py:39
  35.2 0.7 copy-done.3
  35.9 4.8 %shard_map.143 = f32[3,56,256]{2,1,0:T(8,128)S(1)} custom-call(s32[1]{0:T(128)S(6)} %copy.74.live_ref.refs_1_, f32[3,56,256]{2,1,0:T(8,128)S(1)} %broadcast_select_fusion.8.v_ref.refs_5_, s32[27,384]{1,0:T(8,128)S(1)} %copy-done.3, f32[1,384]{1,0:T(1,128)S(1)} %reshape.49.coef_ref.refs_7_, f32[81,81]{1,0:T(8,128)S(1)} %copy-done.2), custom_call_target="tpu_custom_call" | custom-call | tf_op jit(solution)/shard_map/pallas_call | solution.py:141
  40.7 0.7 collective-permute-start.5
  41.3 6.6 %collective-permute-start.6 = (f32[3,256]{1,0:T(4,128)S(1)}, f32[3,256]{1,0:T(4,128)S(1)}, u32[]{:S(2)}, u32[]{:S(2)}) collective-permute-start(f32[3,256]{1,0:T(4,128)S(1)} %get-tuple-element.64), channel_id=1, source_target_pairs={{0,4},{4,0},{8,12},{12,8},{16,20},{20,16},{24,28},{28,24},{32,36},... | collective-permute-start | bytes 9224 | tf_op jit(solution)/shard_map/ppermute | solution.py:578
  48.0 0.9 collective-permute-done.6
  49.0 1.8 %collective-permute-start.7 = (f32[3,56,256]{2,1,0:T(8,128)S(1)}, f32[3,56,256]{2,1,0:T(8,128)S(1)}, u32[]{:S(2)}, u32[]{:S(2)}) collective-permute-start(f32[3,56,256]{2,1,0:T(8,128)S(1)} %select_add_fusion.1), channel_id=1, source_target_pairs={{0,1},{1,0},{2,3},{3,2},{4,5},{5,4},{6,7},{7,6},{8,9},{9,8},{10,11... | collective-permute-start | bytes 516104 | tf_op jit(solution)/shard_map/ppermute | solution.py:35
  50.9 1.0 collective-permute-done.7
  52.0 0.4 collective-permute-start.8
  52.5 6.3 %collective-permute-start.9 = (f32[2,14,4,512]{3,2,1,0:T(4,128)S(1)}, f32[2,14,4,512]{3,2,1,0:T(4,128)S(1)}, u32[]{:S(2)}, u32[]{:S(2)}) collective-permute-start(f32[2,14,4,512]{3,2,1,0:T(4,128)S(1)} %get-tuple-element.22), channel_id=1, source_target_pairs={{1,2},{2,1},{5,6},{6,5},{9,10},{10,9},{13,14},{14,13},{17,18},{18,... | collective-permute-start | bytes 688136 | tf_op jit(solution)/shard_map/ppermute | solution.py:626
  59.0 4.5 %collective-permute-done.9.mid_ref = f32[2,14,4,512]{3,2,1,0:T(4,128)S(1)} collective-permute-done((f32[2,14,4,512]{3,2,1,0:T(4,128)S(1)}, f32[2,14,4,512]{3,2,1,0:T(4,128)S(1)}, u32[]{:S(2)}, u32[]{:S(2)}) %collective-permute-start.9) | collective-permute-done | bytes 229408 | tf_op jit(solution)/shard_map/ppermute | solution.py:626
  63.5 2.6 %collective-permute-done.10.refs_3_ = f32[3,56,256]{2,1,0:T(8,128)S(1)} collective-permute-done((f32[3,56,256]{2,1,0:T(8,128)S(1)}, f32[3,56,256]{2,1,0:T(8,128)S(1)}, u32[]{:S(2)}, u32[]{:S(2)}) %collective-permute-start.10) | collective-permute-done | bytes 172064 | tf_op jit(solution)/shard_map/ppermute | solution.py:35
  66.2 5.3 %shard_map.144 = (f32[3,56,256]{2,1,0:T(8,128)S(1)}, f32[512,128]{1,0:T(8,128)}, f32[16,128]{1,0:T(8,128)S(1)}) custom-call(s32[2]{0:T(128)S(1)} %pad_add_fusion.at_ref.refs_0_, s32[1]{0:T(128)S(6)} %copy.74.live_ref.refs_1_, f32[3,56,256]{2,1,0:T(8,128)S(1)} %fusion.16.refs_2_, f32[3,56,256]{2,1,0:T(8,128)S(1)} %collective-permute-done.10.refs_3_, ...), custom_call_target="tpu_custom_call" | custom-call | tf_op jit(solution)/shard_map/pallas_call | solution.py:332
  71.5 16.7 %all-to-all-start = ((f32[128,4,128]{2,1,0:T(4,128)}), f32[128,4,128]{2,1,0:T(4,128)S(1)}, u32[]{:S(2)}, u32[]{:S(2)}) async-start(f32[128,4,128]{2,1,0:T(4,128)} %bitcast.13), calls=%async_computation | async-start | bytes 524288 | tf_op jit(solution)/shard_map/all_to_all | solution.py:604
  88.2 10.9 %all-to-all-done = f32[128,4,128]{2,1,0:T(4,128)S(1)} async-done(((f32[128,4,128]{2,1,0:T(4,128)}), f32[128,4,128]{2,1,0:T(4,128)S(1)}, u32[]{:S(2)}, u32[]{:S(2)}) %all-to-all-start) | async-done | bytes 262176 | tf_op jit(solution)/shard_map/all_to_all | solution.py:604
  99.1 1.1 shard_map.145
  100.3 1.3 collective-permute-start.11
  101.6 3.0 %collective-permute-done.11 = f32[3,256]{1,0:T(4,128)S(1)} collective-permute-done((f32[3,256]{1,0:T(4,128)S(1)}, f32[3,256]{1,0:T(4,128)S(1)}, u32[]{:S(2)}, u32[]{:S(2)}) %collective-permute-start.11) | collective-permute-done | bytes 3104 | tf_op jit(solution)/shard_map/ppermute | solution.py:39
  104.7 4.8 %shard_map.146 = f32[3,56,256]{2,1,0:T(8,128)S(1)} custom-call(s32[1]{0:T(128)S(6)} %copy.74.live_ref.refs_1_, f32[3,56,256]{2,1,0:T(8,128)S(1)} %broadcast_select_fusion.7.v_ref.refs_5_, s32[27,384]{1,0:T(8,128)S(1)} %copy-done.3, f32[1,384]{1,0:T(1,128)S(1)} %reshape.49.coef_ref.refs_7_, f32[81,81]{1,0:T(8,128)S(1)} %copy-done.2), custom_call_target="tpu_custom_call" | custom-call | tf_op jit(solution)/shard_map/pallas_call | solution.py:141
  109.5 3.0 %collective-permute-start.13 = (f32[3,256]{1,0:T(4,128)S(1)}, f32[3,256]{1,0:T(4,128)S(1)}, u32[]{:S(2)}, u32[]{:S(2)}) collective-permute-start(f32[3,256]{1,0:T(4,128)S(1)} %bitcast.58), channel_id=1, source_target_pairs={{0,4},{4,0},{8,12},{12,8},{16,20},{20,16},{24,28},{28,24},{32,36},... | collective-permute-start | bytes 9224 | tf_op jit(solution)/shard_map/ppermute | solution.py:578
  112.6 0.6 collective-permute-start.12
  113.3 0.3 collective-permute-done.13
  113.7 2.9 %collective-permute-start.14 = (f32[3,56,256]{2,1,0:T(8,128)S(1)}, f32[3,56,256]{2,1,0:T(8,128)S(1)}, u32[]{:S(2)}, u32[]{:S(2)}) collective-permute-start(f32[3,56,256]{2,1,0:T(8,128)S(1)} %select_add_fusion), channel_id=1, source_target_pairs={{0,1},{1,0},{2,3},{3,2},{4,5},{5,4},{6,7},{7,6},{8,9},{9,8},{10,11... | collective-permute-start | bytes 516104 | tf_op jit(solution)/shard_map/ppermute | solution.py:35
  116.6 0.2 broadcast_select_fusion.ws_ref
  116.8 0.9 collective-permute-done.14
  117.9 5.6 %shard_map.147 = f32[8,32,512]{2,1,0:T(8,128)} custom-call(s32[2]{0:T(128)S(1)} %pad_add_fusion.at_ref.refs_0_, f32[8,32,512]{2,1,0:T(8,128)S(1)} %copy-done, f32[8,32,512]{2,1,0:T(8,128)S(1)} %copy-done.1, f32[2,3,32,512]{3,2,1,0:T(8,128)S(1)} %collective-permute-done.1.xa_ref, f32[2,3,32,512]{3,2,1,0:T(8,128)S(1)} %collective-permute-done.xb_ref, ...), custom_call_target="tpu_custom_call" | custom-call | tf_op jit(solution)/shard_map/pallas_call | solution.py:520
  123.5 1.4 collective-permute-done.15.refs_3_
  125.0 4.5 %shard_map.148 = (f32[3,56,256]{2,1,0:T(8,128)S(1)}, f32[128,128]{1,0:T(8,128)}) custom-call(s32[2]{0:T(128)S(1)} %pad_add_fusion.at_ref.refs_0_, s32[1]{0:T(128)S(6)} %copy.74.live_ref.refs_1_, f32[3,56,256]{2,1,0:T(8,128)S(1)} %fusion.15.refs_2_, f32[3,56,256]{2,1,0:T(8,128)S(1)} %collective-permute-done.15.refs_3_, f32[56,256]{1,0:T(8,128)S(1)} %pad_select_fusion.refs_4_, ...), custom_call_target="tpu_custom_call" | custom-call | tf_op jit(solution)/shard_map/pallas_call | solution.py:332
  129.5 14.9 %all-to-all-start.1 = ((f32[128,1,128]{2,1,0:T(1,128)}), f32[128,1,128]{2,1,0:T(1,128)S(1)}, u32[]{:S(2)}, u32[]{:S(2)}) async-start(f32[128,1,128]{2,1,0:T(1,128)} %bitcast.17), calls=%async_computation.1 | async-start | bytes 131072 | tf_op jit(solution)/shard_map/all_to_all | solution.py:604
  144.4 9.4 %all-to-all-done.1 = f32[128,1,128]{2,1,0:T(1,128)S(1)} async-done(((f32[128,1,128]{2,1,0:T(1,128)}), f32[128,1,128]{2,1,0:T(1,128)S(1)}, u32[]{:S(2)}, u32[]{:S(2)}) %all-to-all-start.1) | async-done | bytes 65568 | tf_op jit(solution)/shard_map/all_to_all | solution.py:604
  153.8 0.1 shard_map.149
  153.9 0.6 copy.51
  (84 shorter events, 1.7 us)
Async XLA Ops:
  0.6 7.0 %copy-start.2 = (f32[81,81]{1,0:T(8,128)S(1)}, f32[81,81]{1,0:T(8,128)}, u32[]{:S(2)}) copy-start(f32[81,81]{1,0:T(8,128)} %stiff_ref.9) | copy-start | bytes 78736
  0.7 7.0 %copy-start.4 = (f32[3,3072]{1,0:T(4,128)S(1)}, f32[3,3072]{1,0:T(4,128)}, u32[]{:S(2)}) copy-start(f32[3,3072]{1,0:T(4,128)} %load_ref.1) | copy-start | bytes 110596
  0.7 7.0 %copy-start.7 = (f32[3072]{0:T(1024)S(1)}, f32[3072]{0:T(1024)}, u32[]{:S(2)}) copy-start(f32[3072]{0:T(1024)} %param.19) | copy-start | bytes 36868
  0.7 7.0 %copy-start.10 = (f32[3,256]{1,0:T(4,128)S(1)}, f32[3,256]{1,0:T(4,128)}, u32[]{:S(2)}) copy-start(f32[3,256]{1,0:T(4,128)} %normal_ref.1) | copy-start | bytes 9220
  0.7 15.5 %copy-start = (f32[8,32,512]{2,1,0:T(8,128)S(1)}, f32[8,32,512]{2,1,0:T(8,128)}, u32[]{:S(2)}) copy-start(f32[8,32,512]{2,1,0:T(8,128)} %fs_ref.3) | copy-start | bytes 1572868
  0.7 15.5 %copy-start.1 = (f32[8,32,512]{2,1,0:T(8,128)S(1)}, f32[8,32,512]{2,1,0:T(8,128)}, u32[]{:S(2)}) copy-start(f32[8,32,512]{2,1,0:T(8,128)} %fd_ref.3) | copy-start | bytes 1572868
  2.4 5.3 %copy-start.9 = (f32[4,256]{1,0:T(4,128)S(1)}, f32[4,256]{1,0:T(4,128)}, u32[]{:S(2)}) copy-start(f32[4,256]{1,0:T(4,128)} %tw_ref.1) | copy-start | bytes 12292
  2.4 5.3 %copy-start.8 = (s32[4,256]{1,0:T(4,128)S(1)}, s32[4,256]{1,0:T(4,128)}, u32[]{:S(2)}) copy-start(s32[4,256]{1,0:T(4,128)} %face_ref.1) | copy-start | bytes 12292
  2.4 5.5 %collective-permute-start = (f32[2,3,32,512]{3,2,1,0:T(8,128)S(1)}, f32[2,3,32,512]{3,2,1,0:T(8,128)S(1)}, u32[]{:S(2)}, u32[]{:S(2)}) collective-permute-start(f32[2,3,32,512]{3,2,1,0:T(8,128)S(1)} %get-tuple-element.40), channel_id=1, source_target_pairs={{4,8},{12,16},{20,24},{28,32},{36,40},{44,48},{52,56},{60,64},{68,... | collective-permute-start | bytes 1179656 | tf_op jit(solution)/shard_map/ppermute | solution.py:579
  3.1 13.1 %collective-permute-start.1 = (f32[2,3,32,512]{3,2,1,0:T(8,128)S(1)}, f32[2,3,32,512]{3,2,1,0:T(8,128)S(1)}, u32[]{:S(2)}, u32[]{:S(2)}) collective-permute-start(f32[2,3,32,512]{3,2,1,0:T(8,128)S(1)} %get-tuple-element.41), channel_id=1, source_target_pairs={{0,4},{4,0},{8,12},{12,8},{16,20},{20,16},{24,28},{28,24},{32,36},... | collective-permute-start | bytes 1179656 | tf_op jit(solution)/shard_map/ppermute | solution.py:578
  7.7 8.5 %copy-start.5 = (s32[4,8,32]{2,1,0:T(8,128)S(1)}, s32[4,8,32]{2,1,0:T(8,128)}, u32[]{:S(2)}) copy-start(s32[4,8,32]{2,1,0:T(8,128)} %node_ref.1) | copy-start | bytes 12292
  7.7 8.5 %copy-start.6 = (f32[4,8,32]{2,1,0:T(8,128)S(1)}, f32[4,8,32]{2,1,0:T(8,128)}, u32[]{:S(2)}) copy-start(f32[4,8,32]{2,1,0:T(8,128)} %ww_ref.1) | copy-start | bytes 12292
  17.0 2.7 %collective-permute-start.2 = (f32[320,128]{1,0:T(8,128)S(1)}, f32[320,128]{1,0:T(8,128)S(1)}, u32[]{:S(2)}, u32[]{:S(2)}) collective-permute-start(f32[320,128]{1,0:T(8,128)S(1)} %pad_maximum_fusion.4), channel_id=1, source_target_pairs={{0,1},{1,0},{2,3},{3,2},{4,5},{5,4},{6,7},{7,6},{8,9},{9,8},{10,11... | collective-permute-start | bytes 491528 | tf_op jit(solution)/shard_map/ppermute | solution.py:35
  18.7 0.7 copy-start.13
  19.8 8.4 %collective-permute-start.3 = (f32[448,128]{1,0:T(8,128)S(1)}, f32[448,128]{1,0:T(8,128)S(1)}, u32[]{:S(2)}, u32[]{:S(2)}) collective-permute-start(f32[448,128]{1,0:T(8,128)S(1)} %pad_maximum_fusion.3), channel_id=1, source_target_pairs={{0,2},{1,3},{2,0},{3,1},{4,6},{5,7},{6,4},{7,5},{8,10},{9,11},{10,... | collective-permute-start | bytes 688136 | tf_op jit(solution)/shard_map/ppermute | solution.py:35
  28.3 0.6 copy-start.11
  30.0 0.7 slice-start
  30.7 4.3 %collective-permute-start.4 = (f32[4,256]{1,0:T(4,128)S(1)}, f32[4,256]{1,0:T(4,128)S(1)}, u32[]{:S(2)}, u32[]{:S(2)}) collective-permute-start(f32[4,256]{1,0:T(4,128)S(1)} %pad_maximum_fusion.7), channel_id=1, source_target_pairs={{4,0},{8,4},{12,8},{16,12},{20,16},{24,20},{28,24},{32,28},{36,32}... | collective-permute-start | bytes 12296 | tf_op jit(solution)/shard_map/ppermute | solution.py:39
  35.1 0.8 copy-start.3
  40.7 7.4 %collective-permute-start.5 = (f32[3,256]{1,0:T(4,128)S(1)}, f32[3,256]{1,0:T(4,128)S(1)}, u32[]{:S(2)}, u32[]{:S(2)}) collective-permute-start(f32[3,256]{1,0:T(4,128)S(1)} %get-tuple-element.63), channel_id=1, source_target_pairs={{4,8},{12,16},{20,24},{28,32},{36,40},{44,48},{52,56},{60,64},{68,... | collective-permute-start | bytes 9224 | tf_op jit(solution)/shard_map/ppermute | solution.py:579
  41.3 7.6 %collective-permute-start.6 = (f32[3,256]{1,0:T(4,128)S(1)}, f32[3,256]{1,0:T(4,128)S(1)}, u32[]{:S(2)}, u32[]{:S(2)}) collective-permute-start(f32[3,256]{1,0:T(4,128)S(1)} %get-tuple-element.64), channel_id=1, source_target_pairs={{0,4},{4,0},{8,12},{12,8},{16,20},{20,16},{24,28},{28,24},{32,36},... | collective-permute-start | bytes 9224 | tf_op jit(solution)/shard_map/ppermute | solution.py:578
  49.0 2.9 %collective-permute-start.7 = (f32[3,56,256]{2,1,0:T(8,128)S(1)}, f32[3,56,256]{2,1,0:T(8,128)S(1)}, u32[]{:S(2)}, u32[]{:S(2)}) collective-permute-start(f32[3,56,256]{2,1,0:T(8,128)S(1)} %select_add_fusion.1), channel_id=1, source_target_pairs={{0,1},{1,0},{2,3},{3,2},{4,5},{5,4},{6,7},{7,6},{8,9},{9,8},{10,11... | collective-permute-start | bytes 516104 | tf_op jit(solution)/shard_map/ppermute | solution.py:35
  52.0 6.9 %copy-start.12 = (f32[48,256]{1,0:T(8,128)S(1)}, f32[48,256]{1,0:T(8,128)}, u32[]{:S(2)}) copy-start(f32[48,256]{1,0:T(8,128)} %copy-done.11) | copy-start | bytes 147460
  52.0 7.0 %collective-permute-start.8 = (f32[2,14,4,512]{3,2,1,0:T(4,128)S(1)}, f32[2,14,4,512]{3,2,1,0:T(4,128)S(1)}, u32[]{:S(2)}, u32[]{:S(2)}) collective-permute-start(f32[2,14,4,512]{3,2,1,0:T(4,128)S(1)} %broadcast_select_fusion.6), channel_id=1, source_target_pairs={{0,1},{1,0},{2,3},{3,2},{4,5},{5,4},{6,7},{7,6},{8,9},{9,8},{10,11... | collective-permute-start | bytes 688136 | tf_op jit(solution)/shard_map/ppermute | solution.py:35
  52.5 11.0 %collective-permute-start.9 = (f32[2,14,4,512]{3,2,1,0:T(4,128)S(1)}, f32[2,14,4,512]{3,2,1,0:T(4,128)S(1)}, u32[]{:S(2)}, u32[]{:S(2)}) collective-permute-start(f32[2,14,4,512]{3,2,1,0:T(4,128)S(1)} %get-tuple-element.22), channel_id=1, source_target_pairs={{1,2},{2,1},{5,6},{6,5},{9,10},{10,9},{13,14},{14,13},{17,18},{18,... | collective-permute-start | bytes 688136 | tf_op jit(solution)/shard_map/ppermute | solution.py:626
  58.8 7.4 %collective-permute-start.10 = (f32[3,56,256]{2,1,0:T(8,128)S(1)}, f32[3,56,256]{2,1,0:T(8,128)S(1)}, u32[]{:S(2)}, u32[]{:S(2)}) collective-permute-start(f32[3,56,256]{2,1,0:T(8,128)S(1)} %fusion.16.refs_2_), channel_id=1, source_target_pairs={{0,2},{1,3},{2,0},{3,1},{4,6},{5,7},{6,4},{7,5},{8,10},{9,11},{10,... | collective-permute-start | bytes 516104 | tf_op jit(solution)/shard_map/ppermute | solution.py:35
  71.5 27.7 %all-to-all-start = ((f32[128,4,128]{2,1,0:T(4,128)}), f32[128,4,128]{2,1,0:T(4,128)S(1)}, u32[]{:S(2)}, u32[]{:S(2)}) async-start(f32[128,4,128]{2,1,0:T(4,128)} %bitcast.13), calls=%async_computation | async-start | bytes 524288 | tf_op jit(solution)/shard_map/all_to_all | solution.py:604
  100.3 4.4 %collective-permute-start.11 = (f32[3,256]{1,0:T(4,128)S(1)}, f32[3,256]{1,0:T(4,128)S(1)}, u32[]{:S(2)}, u32[]{:S(2)}) collective-permute-start(f32[3,256]{1,0:T(4,128)S(1)} %bitcast.59), channel_id=1, source_target_pairs={{4,0},{8,4},{12,8},{16,12},{20,16},{24,20},{28,24},{32,28},{36,32}... | collective-permute-start | bytes 9224 | tf_op jit(solution)/shard_map/ppermute | solution.py:39
  109.5 4.0 %collective-permute-start.13 = (f32[3,256]{1,0:T(4,128)S(1)}, f32[3,256]{1,0:T(4,128)S(1)}, u32[]{:S(2)}, u32[]{:S(2)}) collective-permute-start(f32[3,256]{1,0:T(4,128)S(1)} %bitcast.58), channel_id=1, source_target_pairs={{0,4},{4,0},{8,12},{12,8},{16,20},{20,16},{24,28},{28,24},{32,36},... | collective-permute-start | bytes 9224 | tf_op jit(solution)/shard_map/ppermute | solution.py:578
  112.6 1.0 collective-permute-start.12
  113.7 4.0 %collective-permute-start.14 = (f32[3,56,256]{2,1,0:T(8,128)S(1)}, f32[3,56,256]{2,1,0:T(8,128)S(1)}, u32[]{:S(2)}, u32[]{:S(2)}) collective-permute-start(f32[3,56,256]{2,1,0:T(8,128)S(1)} %select_add_fusion), channel_id=1, source_target_pairs={{0,1},{1,0},{2,3},{3,2},{4,5},{5,4},{6,7},{7,6},{8,9},{9,8},{10,11... | collective-permute-start | bytes 516104 | tf_op jit(solution)/shard_map/ppermute | solution.py:35
  117.8 7.2 %collective-permute-start.15 = (f32[3,56,256]{2,1,0:T(8,128)S(1)}, f32[3,56,256]{2,1,0:T(8,128)S(1)}, u32[]{:S(2)}, u32[]{:S(2)}) collective-permute-start(f32[3,56,256]{2,1,0:T(8,128)S(1)} %fusion.15.refs_2_), channel_id=1, source_target_pairs={{0,2},{1,3},{2,0},{3,1},{4,6},{5,7},{6,4},{7,5},{8,10},{9,11},{10,... | collective-permute-start | bytes 516104 | tf_op jit(solution)/shard_map/ppermute | solution.py:35
  129.5 24.3 %all-to-all-start.1 = ((f32[128,1,128]{2,1,0:T(1,128)}), f32[128,1,128]{2,1,0:T(1,128)S(1)}, u32[]{:S(2)}, u32[]{:S(2)}) async-start(f32[128,1,128]{2,1,0:T(1,128)} %bitcast.17), calls=%async_computation.1 | async-start | bytes 131072 | tf_op jit(solution)/shard_map/all_to_all | solution.py:604

commit v3 on v2

--- a/solution.py
+++ b/solution.py
@@ -153,6 +153,7 @@
             pltpu.VMEM((384, 256), F32),
         ],
         compiler_params=params(),
+        cost_estimate=pl.CostEstimate(flops=6 * 10**9, bytes_accessed=24 * 10**6, transcendentals=0),
     )(live, v, conn, coef, stiff)
 
 
@@ -241,11 +242,11 @@
 
 
 def settle_body(*refs, first):
-    at_ref, live_ref, p_ref, q_ref, mass_ref, v_ref, conn_ref, coef_ref, stiff_ref = refs[:9]
+    at_ref, live_ref, p_ref, q_ref, edge_ref, mass_ref, v_ref, conn_ref, coef_ref, stiff_ref = refs[:10]
     if first:
-        seg_ref, pick_ref, w_ref, out_ref, ws_ref = refs[9:14]
+        seg_ref, pick_ref, w_ref, out_ref, ws_ref = refs[10:15]
     else:
-        w_ref, out_ref = refs[9:11]
+        w_ref, out_ref = refs[10:12]
     t_scr, s_scr, x_scr, acc = refs[-4:]
     keep = lax.broadcasted_iota(jnp.int32, (VR, 256), 0)
     end = jnp.where(at_ref[0] == N_GX - 1, OWN, OWN + 1)
@@ -254,7 +255,9 @@
     dots = [jnp.zeros((8, 256), F32) for _ in range(4)]
     for c in range(3):
         v = v_ref[c]
-        w = (p_ref[c] + q_ref[c] + mass * v) * mask
+        w = p_ref[c] + q_ref[c]
+        w = w + jnp.where(keep == 0, edge_ref[0, c : c + 1, :], jnp.where(keep == OWN, edge_ref[1, c : c + 1, :], 0.0))
+        w = (w + mass * v) * mask
         w_ref[c] = w
         for i, (x, y) in enumerate(((v, v), (v, w), (w, w), (w, mass * w))):
             dots[i] = dots[i] + (x[:OWN] * y[:OWN]).reshape(6, 8, 256).sum(axis=0)
@@ -326,13 +329,13 @@
         out_ref[...] = row
 
 
-def settle(at, live, p, q, mass, v, conn, coef, stiff, wall=()):
+def settle(at, live, p, q, edge, mass, v, conn, coef, stiff, wall=()):
     first = bool(wall)
     shapes = [(3, VR, 256), (4 * N_DEV, 128), (16, 128)] if first else [(3, VR, 256), (N_DEV, 128)]
     return pl.pallas_call(
         functools.partial(settle_body, first=first),
         out_shape=tuple(jax.ShapeDtypeStruct(x, F32) for x in shapes),
-        in_specs=[SM, SM] + [VM] * (7 + len(wall)),
+        in_specs=[SM, SM] + [VM] * (8 + len(wall)),
         out_specs=(VM,) * len(shapes),
         scratch_shapes=[
             pltpu.VMEM((192, 512), BF),
@@ -341,7 +344,8 @@
             pltpu.VMEM((1, 128), F32),
         ],
         compiler_params=params(),
-    )(at, live, p, q, mass, v, conn, coef, stiff, *wall)
+        cost_estimate=pl.CostEstimate(flops=6 * 10**9, bytes_accessed=24 * 10**6, transcendentals=0),
+    )(at, live, p, q, edge, mass, v, conn, coef, stiff, *wall)
 
 
 def rows_in(at_ref):
@@ -524,6 +528,7 @@
         out_specs=VM,
         scratch_shapes=[pltpu.VMEM((14, 48, 512), F32)] * 4,
         compiler_params=params(),
+        cost_estimate=pl.CostEstimate(flops=10**8, bytes_accessed=20 * 10**6, transcendentals=0),
     )(at, fs, fd, xa, xb, sib, mid, ws)
 
 
@@ -571,21 +576,30 @@
         return jnp.concatenate([jnp.where(bit == 0, own, other), jnp.where(bit == 0, other, own)], axis=0)
 
     even = gx % 2 == 0
-
-    def beside(to_low, to_high):
-        first = [(i, i ^ 1) for i in range(N_GX)]
-        second = [(i, i + 1) for i in range(1, N_GX - 1, 2)] + [(i + 1, i) for i in range(1, N_GX - 1, 2)]
-        a = lax.ppermute(jnp.where(even, to_high, to_low), "gx", first)
-        b = lax.ppermute(jnp.where(even, to_low, to_high), "gx", second)
-        return a, b
-
-    both = jnp.stack([fluid_source, fluid_diag])
-    xa, xb = beside(both[:, 0:3], both[:, 5:8])
+    low_pairs = [(i, i ^ 1) for i in range(N_GX)]
+    high_pairs = [(i, i + 1) for i in range(1, N_GX - 1, 2)]
+    high_pairs = high_pairs + [(j, i) for i, j in high_pairs]
+
+    def beside(to_low, to_high, cross=False):
+        sends = jnp.where(even, to_high, to_low), jnp.where(even, to_low, to_high)
+        got = []
+        for send, pairs in zip(sends, (low_pairs, high_pairs)):
+            if cross:
+                both_ends = [(4 * i + g, 4 * j + (g ^ (2 * (g & 1)))) for i, j in pairs for g in range(4)]
+                got.append(lax.ppermute(send, AXES, both_ends))
+            else:
+                got.append(lax.ppermute(send, "gx", pairs))
+        return got
+
+    def three(part):
+        return jnp.stack([fluid_source[part], fluid_diag[part]])
+
+    sa, sb = beside(three(slice(0, 3))[..., :128], three(slice(5, 8))[..., :128])
 
     own = pack_parts(
         stiff_ref, solid_load, node_mass.reshape(1, 3072), trac_face, trac_weight, wet_normal
     )
-    wide = pack_wall(at, fluid_source, fluid_diag, xa, xb, wall_node, wall_weight)
+    wide = pack_wall(at, fluid_source, fluid_diag, sa, sb, wall_node, wall_weight)
     near = swap(jnp.concatenate([own, wide], axis=0), CORE)
     pair = jnp.concatenate([in_order(core, own, near[:128]), wide + near[128:]], axis=0)
     far = swap(pair, YHI)
@@ -603,48 +617,62 @@
     def to_all(x):
         return lax.all_to_all(x, AXES, 0, 0, tiled=True)
 
-    def pair_sum(v):
-        s = stiff_apply(live_count, v, connect, coef, stiff_ref)
-        a, b = beside(s[:, 0, :], s[:, OWN, :])
-        below, above = jnp.where(even, b, a), jnp.where(even, a, b)
-        s = s + jnp.where(row == 0, below[:, None, :], 0.0) + jnp.where(row == OWN, above[:, None, :], 0.0)
-        return s + swap(s, CORE)
+    def exchange(s):
+        pair = s + swap(s, CORE)
+        far = swap(pair, YHI)
+        ab = beside(pair[:, 0, :], pair[:, OWN, :], cross=True)
+        return pair, far, ab
+
+    def edges(far, ab):
+        far, (a, b) = lax.optimization_barrier((far, ab))
+        got = jnp.stack([jnp.where(even, b, a), jnp.where(even, a, b)])
+        return far, got + swap(got, CORE)
 
     f1 = first_force(at, slab, load, seg)
     following = from_gx(jnp.concatenate([f1[:, 0, :], mass[0:1]], axis=0), -1)
     f1 = jnp.where(row == OWN, following[0:3, None, :], f1)
     mass = jnp.where(row[0] == OWN, following[3:4], mass)
-    pair1 = pair_sum(f1)
-
-    xlo, xhi = jnp.where(even, xb, xa), jnp.where(even, xa, xb)
-    low = jnp.concatenate([xlo[:, :, 0:4], both[:, :, 0:4], xhi[:, :, 0:4]], axis=1)
-    high = jnp.concatenate([xlo[:, :, 28:32], both[:, :, 28:32], xhi[:, :, 28:32]], axis=1)
-    sides = (jnp.where(core == 0, high, low), jnp.where(core == 0, low, high))
-    sides, pair1 = lax.optimization_barrier((sides, pair1))
-    other1 = swap(pair1, YHI)
-    sib = swap(sides[0], CORE)
-    mid = lax.ppermute(sides[1], "gy", [(1, 2), (2, 1)])
-    pair1, sib, mid = lax.optimization_barrier((pair1, sib, mid))
-    w1, out1, wsb = settle(at, live_count, pair1, other1, mass, f1, connect, coef, stiff_ref, (seg, pick))
-    f2, ws, s1 = second_force(at, to_all(out1), stiff_ref, wsb, slab, load, seg)
+
+    pair1, far1, ab = exchange(stiff_apply(live_count, f1, connect, coef, stiff_ref))
+    far1, edge1 = edges(far1, ab)
+    w1, out1, wsb = settle(
+        at, live_count, pair1, far1, edge1, mass, f1, connect, coef, stiff_ref, (seg, pick)
+    )
+    rows, out1 = lax.optimization_barrier(((three(slice(0, 3)), three(slice(5, 8))), out1))
+    got1 = to_all(out1)
+    xa, xb = beside(*rows)
+    f2, ws, s1 = second_force(at, got1, stiff_ref, wsb, slab, load, seg)
     following = from_gx(f2[:, 0, :], -1)
     f2 = jnp.where(row == OWN, following[:, None, :], f2)
-    pair2 = pair_sum(f2)
-
+    f2, xa, xb = lax.optimization_barrier((f2, xa, xb))
+    pair2, far2, ab = exchange(stiff_apply(live_count, f2, connect, coef, stiff_ref))
+
+    xlo, xhi = jnp.where(even, xb, xa), jnp.where(even, xa, xb)
+
+    def columns(part):
+        middle = jnp.stack([fluid_source[:, part], fluid_diag[:, part]])
+        return jnp.concatenate([xlo[:, :, part], middle, xhi[:, :, part]], axis=1)
+
+    low, high = columns(slice(0, 4)), columns(slice(28, 32))
+    sides = (jnp.where(core == 0, high, low), jnp.where(core == 0, low, high))
     padded = jnp.pad(ws, ((0, 0), (8, 8)))
     wall = lax.dynamic_slice_in_dim(padded, gy * 32, 48, axis=1)
     lane = lax.broadcasted_iota(jnp.int32, (16, 48, 128), 2)
     wall = jnp.where(lane == 0, wall[:, :, None], 0.0)
-    wall, pair2 = lax.optimization_barrier((wall, pair2))
-    other2 = swap(pair2, YHI)
+    sides, wall, pair2 = lax.optimization_barrier((sides, wall, pair2))
+    far2, edge2 = edges(far2, ab)
+    sides, far2, edge2 = lax.optimization_barrier((sides, far2, edge2))
+    sib = swap(sides[0], CORE)
+    mid = lax.ppermute(sides[1], "gy", [(1, 2), (2, 1)])
+    w2, out2 = settle(at, live_count, pair2, far2, edge2, mass, f2, connect, coef, stiff_ref)
+    out2, sib, mid = lax.optimization_barrier((out2, sib, mid))
+    got2 = to_all(out2)
     pressure = fluid(at, fluid_source, fluid_diag, xa, xb, sib, mid, wall)
-    pair2, pressure = lax.optimization_barrier((pair2, pressure))
-    w2, out2 = settle(at, live_count, pair2, other2, mass, f2, connect, coef, stiff_ref)
 
     def mine(x):
         return lax.dynamic_slice_in_dim(x, gy * 12, 12, axis=1)
 
-    displacement = last(s1, to_all(out2), stiff_ref, mine(f1), mine(w1), mine(f2), mine(w2)).reshape(3, 3072)
+    displacement = last(s1, got2, stiff_ref, mine(f1), mine(w1), mine(f2), mine(w2)).reshape(3, 3072)
     return pressure, displacement
 
 

time: 153 us -> 137 us (0.90); the launches traced: 155 us -> 135 us
  waiting for transfers between devices: 49.9 us -> 37.6 us
  Pallas kernels: 28.1 us -> 20.6 us
    ppermute x7 -> x9, starting transfers between devices: 10 us -> 25 us  [swap(): return lax.ppermute(x, AXES, [(i, i ^ mask) for i in range(N_DEV)])]
    all_to_all x2, waiting for transfers between devices: 20.4 us -> 11.7 us  [to_all(): return lax.all_to_all(x, AXES, 0, 0, tiled=True)]
    ppermute x6 -> x8, starting transfers between devices: 16.2 us -> 7.94 us  [the longest x4 4.83 us: beside(): got.append(lax.ppermute(send, 'gx', pairs))]
    pallas_call x2, Pallas kernels: 9.54 us -> 5.08 us  [stiff_apply(): pl.pallas_call(apply_body, out_shape=jax.ShapeDtypeStruct((3, VR, 256), F...]
    all_to_all x2, starting transfers between devices: 31.6 us -> 27.4 us  [to_all(): return lax.all_to_all(x, AXES, 0, 0, tiled=True)]
    ppermute x1, waiting for transfers between devices: 4.52 us -> 0.91 us  [local(): mid = lax.ppermute(sides[1], 'gy', [(1, 2), (2, 1)])]
    pallas_call x2, Pallas kernels: 9.85 us -> 6.79 us  [settle(): pl.pallas_call(functools.partial(settle_body, first=first), out_shape=tup...]
    another operation x0 -> x3, local copies, waits for them, and re-layouts: none -> 1.84 us  [the longest x2 1.13 us: three(): return jnp.stack([fluid_source[part], fluid_diag[part]])]
  transfers between devices with their start and end apart: 18 -> 22, of which waited for: 14 -> 16; matrix products, arithmetic and copies ran while one was open for 2% -> 3% of each run, Pallas kernels for 4% -> 7%
where the time goes in v3:
time: 137 us; the launch traced here: 135 us
  starting transfers between devices  67.9 us (50%)
  waiting for transfers between devices  37.6 us (27%)
  Pallas kernels  20.6 us (15%)
  local copies, waits for them, and re-layouts  4.06 us (3%)
  other arithmetic  3.02 us (2%)
  between operations  1.97 us (1%)
    all_to_all x2, starting transfers between devices, to_all(): return lax.all_to_all(x, AXES, 0, 0, tiled=True)  27.4 us
    ppermute x9, starting transfers between devices, swap(): return lax.ppermute(x, AXES, [(i, i ^ mask) for i in range(N_DEV)])  25 us
    all_to_all x2, waiting for transfers between devices, to_all(): return lax.all_to_all(x, AXES, 0, 0, tiled=True)  11.7 us
    ppermute x9, waiting for transfers between devices, swap(): return lax.ppermute(x, AXES, [(i, i ^ mask) for i in range(N_DEV)])  11.4 us
    pallas_call x2, Pallas kernels, settle(): pl.pallas_call(functools.partial(settle_body, first=first), out_shape=tup...  6.79 us
    ppermute x4, waiting for transfers between devices, beside(): got.append(lax.ppermute(send, AXES, both_ends))  6.58 us
    ppermute x2, waiting for transfers between devices, from_gx(): lax.ppermute(x, 'gx', [(i, i + by) for i in range(N_GX) if 0 <= i + by <...  5.98 us
    pallas_call x1, Pallas kernels, fluid(): pl.pallas_call(fluid_body, out_shape=jax.ShapeDtypeStruct((8, 32, 512), F...  5.61 us
  transfers between devices with their start and end apart: 22, of which 16 were waited for; matrix products, arithmetic and copies ran while one was open for 3% of the time, Pallas kernels for 7%

profile of v3, /device:TPU:1, one launch (start us, length us, event | category | flops | bytes accessed | tf_op | source)
XLA Modules:
  0.0 135.1 jit_solution(3213049266470871879)
XLA Ops:
  0.7 1.1 slice_bitcast_fusion.1
  2.0 2.1 %collective-permute-start = (f32[2,3,32,128]{3,2,1,0:T(8,128)S(1)}, f32[2,3,32,128]{3,2,1,0:T(8,128)S(1)}, u32[]{:S(2)}, u32[]{:S(2)}) collective-permute-start(f32[2,3,32,128]{3,2,1,0:T(8,128)S(1)} %get-tuple-element.69), channel_id=1, source_target_pairs={{0,4},{4,0},{8,12},{12,8},{16,20},{20,16},{24,28},{28,24},{32,36},... | collective-permute-start | bytes 294920 | tf_op jit(solution)/shard_map/ppermute | solution.py:591
  4.1 0.7 collective-permute-start.1
  5.1 1.1 collective-permute-done.xa_ref
  6.2 0.8 shard_map.140
  7.0 2.1 %collective-permute-start.2 = (f32[320,128]{1,0:T(8,128)S(1)}, f32[320,128]{1,0:T(8,128)S(1)}, u32[]{:S(2)}, u32[]{:S(2)}) collective-permute-start(f32[320,128]{1,0:T(8,128)S(1)} %pad_maximum_fusion.6), channel_id=1, source_target_pairs={{0,1},{1,0},{2,3},{3,2},{4,5},{5,4},{6,7},{7,6},{8,9},{9,8},{10,11... | collective-permute-start | bytes 491528 | tf_op jit(solution)/shard_map/ppermute | solution.py:35
  9.1 1.0 collective-permute-done.2
  10.2 3.1 %collective-permute-start.3 = (f32[448,128]{1,0:T(8,128)S(1)}, f32[448,128]{1,0:T(8,128)S(1)}, u32[]{:S(2)}, u32[]{:S(2)}) collective-permute-start(f32[448,128]{1,0:T(8,128)S(1)} %pad_maximum_fusion.3), channel_id=1, source_target_pairs={{0,2},{1,3},{2,0},{3,1},{4,6},{5,7},{6,4},{7,5},{8,10},{9,11},{10,... | collective-permute-start | bytes 688136 | tf_op jit(solution)/shard_map/ppermute | solution.py:35
  13.2 0.7 slice_bitcast_fusion.8
  13.9 6.2 %collective-permute-done.3 = f32[448,128]{1,0:T(8,128)S(1)} collective-permute-done((f32[448,128]{1,0:T(8,128)S(1)}, f32[448,128]{1,0:T(8,128)S(1)}, u32[]{:S(2)}, u32[]{:S(2)}) %collective-permute-start.3) | collective-permute-done | bytes 229408 | tf_op jit(solution)/shard_map/ppermute | solution.py:35
  20.5 1.0 shard_map.142
  21.5 1.3 collective-permute-start.4
  23.5 3.2 %collective-permute-done.4 = f32[4,256]{1,0:T(4,128)S(1)} collective-permute-done((f32[4,256]{1,0:T(4,128)S(1)}, f32[4,256]{1,0:T(4,128)S(1)}, u32[]{:S(2)}, u32[]{:S(2)}) %collective-permute-start.4) | collective-permute-done | bytes 4128 | tf_op jit(solution)/shard_map/ppermute | solution.py:39
  26.7 0.7 copy-done.10
  27.5 2.5 %shard_map.143 = f32[3,56,256]{2,1,0:T(8,128)S(1)} custom-call(s32[1]{0:T(128)S(6)} %copy.60.live_ref.refs_1_, f32[3,56,256]{2,1,0:T(8,128)S(1)} %broadcast_select_fusion.8.v_ref.refs_6_, s32[27,384]{1,0:T(8,128)S(1)} %copy-done.10, f32[1,384]{1,0:T(1,128)S(1)} %reshape.45.coef_ref.refs_8_, f32[81,81]{1,0:T(8,128)S(1)} %copy-done.2), custom_call_target="tpu_custom_call" | custom-call | flops 6000000000 | bytes 24000000 | tf_op jit(solution)/shard_map/pallas_call | solution.py:141
  30.0 2.1 %collective-permute-start.5 = (f32[3,56,256]{2,0,1:T(4,128)S(1)}, f32[3,56,256]{2,0,1:T(4,128)S(1)}, u32[]{:S(2)}, u32[]{:S(2)}) collective-permute-start(f32[3,56,256]{2,0,1:T(4,128)S(1)} %copy.41), channel_id=1, source_target_pairs={{0,1},{1,0},{2,3},{3,2},{4,5},{5,4},{6,7},{7,6},{8,9},{9,8},{10,11... | collective-permute-start | bytes 516104 | tf_op jit(solution)/shard_map/ppermute | solution.py:35
  32.2 0.9 pad_maximum_fusion
  33.4 7.6 %collective-permute-start.6 = (f32[3,56,256]{2,0,1:T(4,128)S(1)}, f32[3,56,256]{2,0,1:T(4,128)S(1)}, u32[]{:S(2)}, u32[]{:S(2)}) collective-permute-start(f32[3,56,256]{2,0,1:T(4,128)S(1)} %copy_add_fusion.1), channel_id=1, source_target_pairs={{0,2},{1,3},{2,0},{3,1},{4,6},{5,7},{6,4},{7,5},{8,10},{9,11},{10,... | collective-permute-start | bytes 516104 | tf_op jit(solution)/shard_map/ppermute | solution.py:35
  41.0 1.5 %collective-permute-start.7 = (f32[3,256]{1,0:T(4,128)S(1)}, f32[3,256]{1,0:T(4,128)S(1)}, u32[]{:S(2)}, u32[]{:S(2)}) collective-permute-start(f32[3,256]{1,0:T(4,128)S(1)} %get-tuple-element.91), channel_id=1, source_target_pairs={{0,4},{1,7},{2,6},{3,5},{4,0},{5,3},{6,2},{7,1},{8,12},{9,15},{10,... | collective-permute-start | bytes 9224 | tf_op jit(solution)/shard_map/ppermute | solution.py:589
  42.6 0.6 collective-permute-start.8
  43.3 2.7 %collective-permute-done.7 = f32[3,256]{1,0:T(4,128)S(1)} collective-permute-done((f32[3,256]{1,0:T(4,128)S(1)}, f32[3,256]{1,0:T(4,128)S(1)}, u32[]{:S(2)}, u32[]{:S(2)}) %collective-permute-start.7) | collective-permute-done | bytes 3104 | tf_op jit(solution)/shard_map/ppermute | solution.py:589
  46.0 0.7 collective-permute-done.6
  46.8 1.0 collective-permute-start.9
  47.8 0.7 collective-permute-done.9
  48.6 3.8 %shard_map.144 = (f32[3,56,256]{2,1,0:T(8,128)S(1)}, f32[512,128]{1,0:T(8,128)}, f32[16,128]{1,0:T(8,128)S(1)}) custom-call(s32[2]{0:T(128)S(1)} %pad_add_fusion.at_ref.refs_0_, s32[1]{0:T(128)S(6)} %copy.60.live_ref.refs_1_, f32[3,56,256]{2,1,0:T(8,128)S(1)} %copy.42.refs_2_, f32[3,56,256]{2,1,0:T(8,128)S(1)} %copy.43.refs_3_, ...), custom_call_target="tpu_custom_call" | custom-call | flops 6000000000 | bytes 24000000 | tf_op jit(solution)/shard_map/pallas_call | solution.py:335
  52.4 16.9 %all-to-all-start = ((f32[128,4,128]{2,1,0:T(4,128)}), f32[128,4,128]{2,1,0:T(4,128)S(1)}, u32[]{:S(2)}, u32[]{:S(2)}) async-start(f32[128,4,128]{2,1,0:T(4,128)} %bitcast.17), calls=%async_computation | async-start | bytes 524288 | tf_op jit(solution)/shard_map/all_to_all | solution.py:618
  69.3 1.0 broadcast_select_fusion.3
  70.3 1.4 %collective-permute-start.11 = (f32[2,3,32,512]{3,2,1,0:T(8,128)}, f32[2,3,32,512]{3,2,1,0:T(8,128)S(1)}, u32[]{:S(2)}, u32[]{:S(2)}) collective-permute-start(f32[2,3,32,512]{3,2,1,0:T(8,128)} %get-tuple-element.67), channel_id=1, source_target_pairs={{0,4},{4,0},{8,12},{12,8},{16,20},{20,16},{24,28},{28,24},{32,36},... | collective-permute-start | bytes 1179656 | tf_op jit(solution)/shard_map/ppermute | solution.py:591
  71.7 0.7 collective-permute-start.12
  72.4 7.9 %all-to-all-done = f32[128,4,128]{2,1,0:T(4,128)S(1)} async-done(((f32[128,4,128]{2,1,0:T(4,128)}), f32[128,4,128]{2,1,0:T(4,128)S(1)}, u32[]{:S(2)}, u32[]{:S(2)}) %all-to-all-start) | async-done | bytes 262176 | tf_op jit(solution)/shard_map/all_to_all | solution.py:618
  80.3 1.1 shard_map.145
  81.4 1.3 collective-permute-start.10
  83.0 2.8 %collective-permute-done.10 = f32[3,256]{1,0:T(4,128)S(1)} collective-permute-done((f32[3,256]{1,0:T(4,128)S(1)}, f32[3,256]{1,0:T(4,128)S(1)}, u32[]{:S(2)}, u32[]{:S(2)}) %collective-permute-start.10) | collective-permute-done | bytes 3104 | tf_op jit(solution)/shard_map/ppermute | solution.py:39
  85.9 2.6 %shard_map.146 = f32[3,56,256]{2,1,0:T(8,128)S(1)} custom-call(s32[1]{0:T(128)S(6)} %copy.60.live_ref.refs_1_, f32[3,56,256]{2,1,0:T(8,128)S(1)} %broadcast_select_fusion.7.v_ref.refs_6_, s32[27,384]{1,0:T(8,128)S(1)} %copy-done.10, f32[1,384]{1,0:T(1,128)S(1)} %reshape.45.coef_ref.refs_8_, f32[81,81]{1,0:T(8,128)S(1)} %copy-done.2), custom_call_target="tpu_custom_call" | custom-call | flops 6000000000 | bytes 24000000 | tf_op jit(solution)/shard_map/pallas_call | solution.py:141
  88.6 2.2 %collective-permute-start.13 = (f32[3,56,256]{2,0,1:T(4,128)S(1)}, f32[3,56,256]{2,0,1:T(4,128)S(1)}, u32[]{:S(2)}, u32[]{:S(2)}) collective-permute-start(f32[3,56,256]{2,0,1:T(4,128)S(1)} %copy.45), channel_id=1, source_target_pairs={{0,1},{1,0},{2,3},{3,2},{4,5},{5,4},{6,7},{7,6},{8,9},{9,8},{10,11... | collective-permute-start | bytes 516104 | tf_op jit(solution)/shard_map/ppermute | solution.py:35
  91.0 1.0 collective-permute-done.13
  92.1 5.5 %collective-permute-start.14 = (f32[3,56,256]{2,0,1:T(4,128)S(1)}, f32[3,56,256]{2,0,1:T(4,128)S(1)}, u32[]{:S(2)}, u32[]{:S(2)}) collective-permute-start(f32[3,56,256]{2,0,1:T(4,128)S(1)} %copy_add_fusion), channel_id=1, source_target_pairs={{0,2},{1,3},{2,0},{3,1},{4,6},{5,7},{6,4},{7,5},{8,10},{9,11},{10,... | collective-permute-start | bytes 516104 | tf_op jit(solution)/shard_map/ppermute | solution.py:35
  97.9 0.6 collective-permute-start.16
  98.7 3.9 %collective-permute-done.15 = f32[3,256]{1,0:T(4,128)S(1)} collective-permute-done((f32[3,256]{1,0:T(4,128)S(1)}, f32[3,256]{1,0:T(4,128)S(1)}, u32[]{:S(2)}, u32[]{:S(2)}) %collective-permute-start.15) | collective-permute-done | bytes 3104 | tf_op jit(solution)/shard_map/ppermute | solution.py:589
  102.6 0.7 collective-permute-done.14
  103.3 1.0 collective-permute-start.17
  104.3 0.8 collective-permute-done.17
  105.6 5.0 %collective-permute-start.19 = (f32[2,14,4,512]{3,2,1,0:T(4,128)S(1)}, f32[2,14,4,512]{3,2,1,0:T(4,128)S(1)}, u32[]{:S(2)}, u32[]{:S(2)}) collective-permute-start(f32[2,14,4,512]{3,2,1,0:T(4,128)S(1)} %get-tuple-element.56), channel_id=1, source_target_pairs={{1,2},{2,1},{5,6},{6,5},{9,10},{10,9},{13,14},{14,13},{17,18},{18,... | collective-permute-start | bytes 688136 | tf_op jit(solution)/shard_map/ppermute | solution.py:666
  110.5 3.0 %shard_map.147 = (f32[3,56,256]{2,1,0:T(8,128)S(1)}, f32[128,128]{1,0:T(8,128)}) custom-call(s32[2]{0:T(128)S(1)} %pad_add_fusion.at_ref.refs_0_, s32[1]{0:T(128)S(6)} %copy.60.live_ref.refs_1_, f32[3,56,256]{2,1,0:T(8,128)S(1)} %copy.46.refs_2_, f32[3,56,256]{2,1,0:T(8,128)S(1)} %copy.47.refs_3_, f32[2,3,256]{2,1,0:T(4,128)S(1)} %fusion.4.refs_4_, ...), custom_call_target="tpu_custom_call" | custom-call | flops 6000000000 | bytes 24000000 | tf_op jit(solution)/shard_map/pallas_call | solution.py:335
  113.5 0.9 collective-permute-done.19.mid_ref
  114.4 10.5 %all-to-all-start.1 = ((f32[128,1,128]{2,1,0:T(1,128)}), f32[128,1,128]{2,1,0:T(1,128)S(1)}, u32[]{:S(2)}, u32[]{:S(2)}) async-start(f32[128,1,128]{2,1,0:T(1,128)} %bitcast.28), calls=%async_computation.1 | async-start | bytes 131072 | tf_op jit(solution)/shard_map/all_to_all | solution.py:618
  124.9 5.6 %shard_map.148 = f32[8,32,512]{2,1,0:T(8,128)} custom-call(s32[2]{0:T(128)S(1)} %pad_add_fusion.at_ref.refs_0_, f32[8,32,512]{2,1,0:T(8,128)S(1)} %copy-done, f32[8,32,512]{2,1,0:T(8,128)S(1)} %copy-done.1, f32[2,3,32,512]{3,2,1,0:T(8,128)S(1)} %collective-permute-done.11.xa_ref, f32[2,3,32,512]{3,2,1,0:T(8,128)S(1)} %collective-permute-done.12.xb_ref, ...), custom_call_target="tpu_custom_call" | custom-call | flops 100000000 | bytes 20000000 | tf_op jit(solution)/shard_map/pallas_call | solution.py:524
  130.5 3.8 %all-to-all-done.1 = f32[128,1,128]{2,1,0:T(1,128)S(1)} async-done(((f32[128,1,128]{2,1,0:T(1,128)}), f32[128,1,128]{2,1,0:T(1,128)S(1)}, u32[]{:S(2)}, u32[]{:S(2)}) %all-to-all-start.1) | async-done | bytes 65568 | tf_op jit(solution)/shard_map/all_to_all | solution.py:618
  (107 shorter events, 3.8 us)
Async XLA Ops:
  0.6 1.2 copy-start.1
  1.9 2.9 %copy-start.2 = (f32[81,81]{1,0:T(8,128)S(1)}, f32[81,81]{1,0:T(8,128)}, u32[]{:S(2)}) copy-start(f32[81,81]{1,0:T(8,128)} %stiff_ref.9) | copy-start | bytes 78736
  1.9 2.9 %copy-start.3 = (f32[3,3072]{1,0:T(4,128)S(1)}, f32[3,3072]{1,0:T(4,128)}, u32[]{:S(2)}) copy-start(f32[3,3072]{1,0:T(4,128)} %load_ref.1) | copy-start | bytes 110596
  1.9 2.9 %copy-start.6 = (f32[3072]{0:T(1024)S(1)}, f32[3072]{0:T(1024)}, u32[]{:S(2)}) copy-start(f32[3072]{0:T(1024)} %param.19) | copy-start | bytes 36868
  1.9 2.9 %copy-start.9 = (f32[3,256]{1,0:T(4,128)S(1)}, f32[3,256]{1,0:T(4,128)}, u32[]{:S(2)}) copy-start(f32[3,256]{1,0:T(4,128)} %normal_ref.1) | copy-start | bytes 9220
  1.9 4.2 %copy-start = (f32[8,32,512]{2,1,0:T(8,128)S(1)}, f32[8,32,512]{2,1,0:T(8,128)}, u32[]{:S(2)}) copy-start(f32[8,32,512]{2,1,0:T(8,128)} %fs_ref.3) | copy-start | bytes 1572868
  2.0 2.9 %copy-start.8 = (f32[4,256]{1,0:T(4,128)S(1)}, f32[4,256]{1,0:T(4,128)}, u32[]{:S(2)}) copy-start(f32[4,256]{1,0:T(4,128)} %tw_ref.1) | copy-start | bytes 12292
  2.0 2.9 %copy-start.7 = (s32[4,256]{1,0:T(4,128)S(1)}, s32[4,256]{1,0:T(4,128)}, u32[]{:S(2)}) copy-start(s32[4,256]{1,0:T(4,128)} %face_ref.1) | copy-start | bytes 12292
  2.0 4.1 %collective-permute-start = (f32[2,3,32,128]{3,2,1,0:T(8,128)S(1)}, f32[2,3,32,128]{3,2,1,0:T(8,128)S(1)}, u32[]{:S(2)}, u32[]{:S(2)}) collective-permute-start(f32[2,3,32,128]{3,2,1,0:T(8,128)S(1)} %get-tuple-element.69), channel_id=1, source_target_pairs={{0,4},{4,0},{8,12},{12,8},{16,20},{20,16},{24,28},{28,24},{32,36},... | collective-permute-start | bytes 294920 | tf_op jit(solution)/shard_map/ppermute | solution.py:591
  4.1 2.0 %collective-permute-start.1 = (f32[2,3,32,128]{3,2,1,0:T(8,128)S(1)}, f32[2,3,32,128]{3,2,1,0:T(8,128)S(1)}, u32[]{:S(2)}, u32[]{:S(2)}) collective-permute-start(f32[2,3,32,128]{3,2,1,0:T(8,128)S(1)} %get-tuple-element.68), channel_id=1, source_target_pairs={{4,8},{12,16},{20,24},{28,32},{36,40},{44,48},{52,56},{60,64},{68,... | collective-permute-start | bytes 294920 | tf_op jit(solution)/shard_map/ppermute | solution.py:591
  4.9 1.3 copy-start.4
  4.9 1.3 copy-start.5
  7.0 3.1 %collective-permute-start.2 = (f32[320,128]{1,0:T(8,128)S(1)}, f32[320,128]{1,0:T(8,128)S(1)}, u32[]{:S(2)}, u32[]{:S(2)}) collective-permute-start(f32[320,128]{1,0:T(8,128)S(1)} %pad_maximum_fusion.6), channel_id=1, source_target_pairs={{0,1},{1,0},{2,3},{3,2},{4,5},{5,4},{6,7},{7,6},{8,9},{9,8},{10,11... | collective-permute-start | bytes 491528 | tf_op jit(solution)/shard_map/ppermute | solution.py:35
  10.2 10.0 %collective-permute-start.3 = (f32[448,128]{1,0:T(8,128)S(1)}, f32[448,128]{1,0:T(8,128)S(1)}, u32[]{:S(2)}, u32[]{:S(2)}) collective-permute-start(f32[448,128]{1,0:T(8,128)S(1)} %pad_maximum_fusion.3), channel_id=1, source_target_pairs={{0,2},{1,3},{2,0},{3,1},{4,6},{5,7},{6,4},{7,5},{8,10},{9,11},{10,... | collective-permute-start | bytes 688136 | tf_op jit(solution)/shard_map/ppermute | solution.py:35
  21.5 1.3 copy-start.17
  21.5 5.2 %collective-permute-start.4 = (f32[4,256]{1,0:T(4,128)S(1)}, f32[4,256]{1,0:T(4,128)S(1)}, u32[]{:S(2)}, u32[]{:S(2)}) collective-permute-start(f32[4,256]{1,0:T(4,128)S(1)} %pad_maximum_fusion.11), channel_id=1, source_target_pairs={{4,0},{8,4},{12,8},{16,12},{20,16},{24,20},{28,24},{32,28},{36,32}... | collective-permute-start | bytes 12296 | tf_op jit(solution)/shard_map/ppermute | solution.py:39
  26.7 0.8 copy-start.10
  30.0 3.3 %collective-permute-start.5 = (f32[3,56,256]{2,0,1:T(4,128)S(1)}, f32[3,56,256]{2,0,1:T(4,128)S(1)}, u32[]{:S(2)}, u32[]{:S(2)}) collective-permute-start(f32[3,56,256]{2,0,1:T(4,128)S(1)} %copy.41), channel_id=1, source_target_pairs={{0,1},{1,0},{2,3},{3,2},{4,5},{5,4},{6,7},{7,6},{8,9},{9,8},{10,11... | collective-permute-start | bytes 516104 | tf_op jit(solution)/shard_map/ppermute | solution.py:35
  33.4 13.4 %collective-permute-start.6 = (f32[3,56,256]{2,0,1:T(4,128)S(1)}, f32[3,56,256]{2,0,1:T(4,128)S(1)}, u32[]{:S(2)}, u32[]{:S(2)}) collective-permute-start(f32[3,56,256]{2,0,1:T(4,128)S(1)} %copy_add_fusion.1), channel_id=1, source_target_pairs={{0,2},{1,3},{2,0},{3,1},{4,6},{5,7},{6,4},{7,5},{8,10},{9,11},{10,... | collective-permute-start | bytes 516104 | tf_op jit(solution)/shard_map/ppermute | solution.py:35
  41.0 5.0 %collective-permute-start.7 = (f32[3,256]{1,0:T(4,128)S(1)}, f32[3,256]{1,0:T(4,128)S(1)}, u32[]{:S(2)}, u32[]{:S(2)}) collective-permute-start(f32[3,256]{1,0:T(4,128)S(1)} %get-tuple-element.91), channel_id=1, source_target_pairs={{0,4},{1,7},{2,6},{3,5},{4,0},{5,3},{6,2},{7,1},{8,12},{9,15},{10,... | collective-permute-start | bytes 9224 | tf_op jit(solution)/shard_map/ppermute | solution.py:589
  42.6 3.4 %collective-permute-start.8 = (f32[3,256]{1,0:T(4,128)S(1)}, f32[3,256]{1,0:T(4,128)S(1)}, u32[]{:S(2)}, u32[]{:S(2)}) collective-permute-start(f32[3,256]{1,0:T(4,128)S(1)} %get-tuple-element.90), channel_id=1, source_target_pairs={{4,8},{5,11},{6,10},{7,9},{12,16},{13,19},{14,18},{15,17},{20,24},... | collective-permute-start | bytes 9224 | tf_op jit(solution)/shard_map/ppermute | solution.py:589
  46.8 1.8 %collective-permute-start.9 = (f32[2,3,256]{2,1,0:T(4,128)S(1)}, f32[2,3,256]{2,1,0:T(4,128)S(1)}, u32[]{:S(2)}, u32[]{:S(2)}) collective-permute-start(f32[2,3,256]{2,1,0:T(4,128)S(1)} %pad_maximum_fusion.9), channel_id=1, source_target_pairs={{0,1},{1,0},{2,3},{3,2},{4,5},{5,4},{6,7},{7,6},{8,9},{9,8},{10,11... | collective-permute-start | bytes 18440 | tf_op jit(solution)/shard_map/ppermute | solution.py:35
  48.6 20.8 %copy-start.12 = (f32[2,3,32,512]{3,2,1,0:T(8,128)S(1)}, f32[2,3,32,512]{3,2,1,0:T(8,128)}, u32[]{:S(2)}) copy-start(f32[2,3,32,512]{3,2,1,0:T(8,128)} %get-tuple-element.40) | copy-start | bytes 1179652
  52.4 16.9 %copy-start.11 = (f32[2,3,32,512]{3,2,1,0:T(8,128)S(1)}, f32[2,3,32,512]{3,2,1,0:T(8,128)}, u32[]{:S(2)}) copy-start(f32[2,3,32,512]{3,2,1,0:T(8,128)} %get-tuple-element.41) | copy-start | bytes 1179652
  52.4 27.9 %all-to-all-start = ((f32[128,4,128]{2,1,0:T(4,128)}), f32[128,4,128]{2,1,0:T(4,128)S(1)}, u32[]{:S(2)}, u32[]{:S(2)}) async-start(f32[128,4,128]{2,1,0:T(4,128)} %bitcast.17), calls=%async_computation | async-start | bytes 524288 | tf_op jit(solution)/shard_map/all_to_all | solution.py:618
  70.3 15.6 %collective-permute-start.11 = (f32[2,3,32,512]{3,2,1,0:T(8,128)}, f32[2,3,32,512]{3,2,1,0:T(8,128)S(1)}, u32[]{:S(2)}, u32[]{:S(2)}) collective-permute-start(f32[2,3,32,512]{3,2,1,0:T(8,128)} %get-tuple-element.67), channel_id=1, source_target_pairs={{0,4},{4,0},{8,12},{12,8},{16,20},{20,16},{24,28},{28,24},{32,36},... | collective-permute-start | bytes 1179656 | tf_op jit(solution)/shard_map/ppermute | solution.py:591
  71.7 14.2 %collective-permute-start.12 = (f32[2,3,32,512]{3,2,1,0:T(8,128)}, f32[2,3,32,512]{3,2,1,0:T(8,128)S(1)}, u32[]{:S(2)}, u32[]{:S(2)}) collective-permute-start(f32[2,3,32,512]{3,2,1,0:T(8,128)} %get-tuple-element.66), channel_id=1, source_target_pairs={{4,8},{12,16},{20,24},{28,32},{36,40},{44,48},{52,56},{60,64},{68,... | collective-permute-start | bytes 1179656 | tf_op jit(solution)/shard_map/ppermute | solution.py:591
  81.4 4.4 %collective-permute-start.10 = (f32[3,256]{1,0:T(4,128)S(1)}, f32[3,256]{1,0:T(4,128)S(1)}, u32[]{:S(2)}, u32[]{:S(2)}) collective-permute-start(f32[3,256]{1,0:T(4,128)S(1)} %bitcast.73), channel_id=1, source_target_pairs={{4,0},{8,4},{12,8},{16,12},{20,16},{24,20},{28,24},{32,28},{36,32}... | collective-permute-start | bytes 9224 | tf_op jit(solution)/shard_map/ppermute | solution.py:39
  88.6 3.3 %collective-permute-start.13 = (f32[3,56,256]{2,0,1:T(4,128)S(1)}, f32[3,56,256]{2,0,1:T(4,128)S(1)}, u32[]{:S(2)}, u32[]{:S(2)}) collective-permute-start(f32[3,56,256]{2,0,1:T(4,128)S(1)} %copy.45), channel_id=1, source_target_pairs={{0,1},{1,0},{2,3},{3,2},{4,5},{5,4},{6,7},{7,6},{8,9},{9,8},{10,11... | collective-permute-start | bytes 516104 | tf_op jit(solution)/shard_map/ppermute | solution.py:35
  92.0 6.6 %copy-start.13 = (f32[1,8,4,512]{3,2,1,0:T(4,128)S(1)}, f32[1,8,4,512]{3,2,1,0:T(4,128)}, u32[]{:S(2)}) copy-start(f32[1,8,4,512]{3,2,1,0:T(4,128)} %get-tuple-element.72) | copy-start | bytes 196612
  92.0 6.6 %copy-start.14 = (f32[1,8,4,512]{3,2,1,0:T(4,128)S(1)}, f32[1,8,4,512]{3,2,1,0:T(4,128)}, u32[]{:S(2)}) copy-start(f32[1,8,4,512]{3,2,1,0:T(4,128)} %get-tuple-element.73) | copy-start | bytes 196612
  92.0 6.6 %copy-start.15 = (f32[1,8,4,512]{3,2,1,0:T(4,128)S(1)}, f32[1,8,4,512]{3,2,1,0:T(4,128)}, u32[]{:S(2)}) copy-start(f32[1,8,4,512]{3,2,1,0:T(4,128)} %get-tuple-element.100) | copy-start | bytes 196612
  92.0 6.6 %copy-start.16 = (f32[1,8,4,512]{3,2,1,0:T(4,128)S(1)}, f32[1,8,4,512]{3,2,1,0:T(4,128)}, u32[]{:S(2)}) copy-start(f32[1,8,4,512]{3,2,1,0:T(4,128)} %get-tuple-element.101) | copy-start | bytes 196612
  92.1 11.2 %collective-permute-start.14 = (f32[3,56,256]{2,0,1:T(4,128)S(1)}, f32[3,56,256]{2,0,1:T(4,128)S(1)}, u32[]{:S(2)}, u32[]{:S(2)}) collective-permute-start(f32[3,56,256]{2,0,1:T(4,128)S(1)} %copy_add_fusion), channel_id=1, source_target_pairs={{0,2},{1,3},{2,0},{3,1},{4,6},{5,7},{6,4},{7,5},{8,10},{9,11},{10,... | collective-permute-start | bytes 516104 | tf_op jit(solution)/shard_map/ppermute | solution.py:35
  97.6 5.0 %collective-permute-start.15 = (f32[3,256]{1,0:T(4,128)S(1)}, f32[3,256]{1,0:T(4,128)S(1)}, u32[]{:S(2)}, u32[]{:S(2)}) collective-permute-start(f32[3,256]{1,0:T(4,128)S(1)} %get-tuple-element.89), channel_id=1, source_target_pairs={{0,4},{1,7},{2,6},{3,5},{4,0},{5,3},{6,2},{7,1},{8,12},{9,15},{10,... | collective-permute-start | bytes 9224 | tf_op jit(solution)/shard_map/ppermute | solution.py:589
  97.9 4.7 %collective-permute-start.16 = (f32[3,256]{1,0:T(4,128)S(1)}, f32[3,256]{1,0:T(4,128)S(1)}, u32[]{:S(2)}, u32[]{:S(2)}) collective-permute-start(f32[3,256]{1,0:T(4,128)S(1)} %get-tuple-element.88), channel_id=1, source_target_pairs={{4,8},{5,11},{6,10},{7,9},{12,16},{13,19},{14,18},{15,17},{20,24},... | collective-permute-start | bytes 9224 | tf_op jit(solution)/shard_map/ppermute | solution.py:589
  103.3 1.8 %collective-permute-start.17 = (f32[2,3,256]{2,1,0:T(4,128)S(1)}, f32[2,3,256]{2,1,0:T(4,128)S(1)}, u32[]{:S(2)}, u32[]{:S(2)}) collective-permute-start(f32[2,3,256]{2,1,0:T(4,128)S(1)} %pad_maximum_fusion.10), channel_id=1, source_target_pairs={{0,1},{1,0},{2,3},{3,2},{4,5},{5,4},{6,7},{7,6},{8,9},{9,8},{10,11... | collective-permute-start | bytes 18440 | tf_op jit(solution)/shard_map/ppermute | solution.py:35
  105.1 8.3 %collective-permute-start.18 = (f32[2,14,4,512]{3,2,1,0:T(4,128)S(1)}, f32[2,14,4,512]{3,2,1,0:T(4,128)S(1)}, u32[]{:S(2)}, u32[]{:S(2)}) collective-permute-start(f32[2,14,4,512]{3,2,1,0:T(4,128)S(1)} %get-tuple-element.55), channel_id=1, source_target_pairs={{0,1},{1,0},{2,3},{3,2},{4,5},{5,4},{6,7},{7,6},{8,9},{9,8},{10,11... | collective-permute-start | bytes 688136 | tf_op jit(solution)/shard_map/ppermute | solution.py:35
  105.6 8.8 %collective-permute-start.19 = (f32[2,14,4,512]{3,2,1,0:T(4,128)S(1)}, f32[2,14,4,512]{3,2,1,0:T(4,128)S(1)}, u32[]{:S(2)}, u32[]{:S(2)}) collective-permute-start(f32[2,14,4,512]{3,2,1,0:T(4,128)S(1)} %get-tuple-element.56), channel_id=1, source_target_pairs={{1,2},{2,1},{5,6},{6,5},{9,10},{10,9},{13,14},{14,13},{17,18},{18,... | collective-permute-start | bytes 688136 | tf_op jit(solution)/shard_map/ppermute | solution.py:666
  114.4 19.9 %all-to-all-start.1 = ((f32[128,1,128]{2,1,0:T(1,128)}), f32[128,1,128]{2,1,0:T(1,128)S(1)}, u32[]{:S(2)}, u32[]{:S(2)}) async-start(f32[128,1,128]{2,1,0:T(1,128)} %bitcast.28), calls=%async_computation.1 | async-start | bytes 131072 | tf_op jit(solution)/shard_map/all_to_all | solution.py:618

commit v4 on v3

--- a/solution.py
+++ b/solution.py
@@ -88,8 +88,9 @@
     fill_stiff(stiff_ref, s_scr)
     x_scr[80:88, :] = jnp.zeros((8, 128), F32)
     acc[...] = jnp.zeros_like(acc)
-    i256 = lax.broadcasted_iota(jnp.int32, (256, 128), 0)
-    i64 = lax.broadcasted_iota(jnp.int32, (LR, 128), 0)
+    b256 = lax.broadcasted_iota(jnp.int32, (256, 128), 0).astype(F32).astype(BF)
+    b64 = b256[:LR]
+    one, nil = jnp.ones((256, 128), BF), jnp.zeros((256, 128), BF)
     oh_scr[:, 27 * 128 :] = jnp.zeros((256, 128), BF)
     ml_scr[:, 27 * 128 :] = jnp.zeros((LR, 128), BF)
     a_scr[:, 27 * 128 :] = jnp.zeros((384, 128), BF)
@@ -102,8 +103,8 @@
                 if k < 27:
                     sl = slice(k * 128, k * 128 + 128)
                     idx = conn_ref[k : k + 1, block_of(b)]
-                    oh_scr[:, sl] = (i256 == (idx & 255)).astype(F32).astype(BF)
-                    ml_scr[:, sl] = (i64 == (idx >> 8)).astype(F32).astype(BF)
+                    oh_scr[:, sl] = jnp.where(b256 == (idx & 255).astype(F32).astype(BF), one, nil)
+                    ml_scr[:, sl] = jnp.where(b64 == (idx >> 8).astype(F32).astype(BF), one[:LR], nil[:LR])
             sp = slice(p * 256, p * 256 + 256)
             oh = oh_scr[:, sp]
             g = jnp.dot(t_scr[...], jnp.concatenate([oh, oh], axis=0), preferred_element_type=F32)
@@ -287,7 +288,8 @@
     fill_stiff(stiff_ref, s_scr)
     acc[...] = jnp.zeros_like(acc)
     x_scr[80:88, :] = jnp.zeros((8, 128), F32)
-    i256 = lax.broadcasted_iota(jnp.int32, (256, 128), 0)
+    b256 = lax.broadcasted_iota(jnp.int32, (256, 128), 0).astype(F32).astype(BF)
+    one, nil = jnp.ones((256, 128), BF), jnp.zeros((256, 128), BF)
     i64 = lax.broadcasted_iota(jnp.int32, (LR, 128), 0)
     live = live_ref[0]
 
@@ -296,7 +298,7 @@
             pieces, masks = [], []
             for k in (2 * p, 2 * p + 1):
                 idx = conn_ref[min(k, 26) : min(k, 26) + 1, block_of(b)]
-                pieces.append((i256 == (idx & 255)).astype(F32).astype(BF))
+                pieces.append(jnp.where(b256 == (idx & 255).astype(F32).astype(BF), one, nil))
                 masks.append((i64 == (idx >> 8)).astype(F32))
             oh = jnp.concatenate(pieces, axis=1)
             g = jnp.dot(t_scr[...], jnp.concatenate([oh, oh], axis=0), preferred_element_type=F32)
@@ -538,13 +540,15 @@
     for c in range(3):
         before = relax_weight * (c0 * f1_ref[c] + c1 * w1_ref[c])
         solved = d0 * f2_ref[c] + d1 * w2_ref[c]
-        out_ref[c] = before + relax_weight * (solved - before)
+        new = before + relax_weight * (solved - before)
+        for r in range(12):
+            out_ref[c : c + 1, r * 256 : r * 256 + 256] = new[r : r + 1, :]
 
 
 def last(s1, got, stiff, f1, w1, f2, w2):
     return pl.pallas_call(
         last_body,
-        out_shape=jax.ShapeDtypeStruct((3, 12, 256), F32),
+        out_shape=jax.ShapeDtypeStruct((3, 3072), F32),
         in_specs=[VM] * 7,
         out_specs=VM,
         compiler_params=params(),
@@ -672,7 +676,7 @@
     def mine(x):
         return lax.dynamic_slice_in_dim(x, gy * 12, 12, axis=1)
 
-    displacement = last(s1, got2, stiff_ref, mine(f1), mine(w1), mine(f2), mine(w2)).reshape(3, 3072)
+    displacement = last(s1, got2, stiff_ref, mine(f1), mine(w1), mine(f2), mine(w2))
     return pressure, displacement
 
 

time: 137 us -> 135 us (0.985)
  starting transfers between devices: 67.9 us -> 61.7 us
  Pallas kernels: 20.6 us -> 26.6 us
    ppermute x9, starting transfers between devices: 25 us -> 16.4 us  [swap(): return lax.ppermute(x, AXES, [(i, i ^ mask) for i in range(N_DEV)])]
    pallas_call x2, Pallas kernels: 5.08 us -> 9.14 us  [stiff_apply(): pl.pallas_call(apply_body, out_shape=jax.ShapeDtypeStruct((3, VR, 256), F...]
  transfers between devices with their start and end apart: 22 -> 22, of which waited for: 16 -> 16; matrix products, arithmetic and copies ran while one was open for 3% -> 3% of each run, Pallas kernels for 7% -> 8%
where the time goes in v4:
time: 135 us; the launch traced here: 133 us
  starting transfers between devices  61.7 us (46%)
  waiting for transfers between devices  36.7 us (27%)
  Pallas kernels  26.6 us (20%)
  local copies, waits for them, and re-layouts  3.42 us (3%)
  other arithmetic  3.02 us (2%)
  between operations  1.99 us (1%)
    all_to_all x2, starting transfers between devices, to_all(): return lax.all_to_all(x, AXES, 0, 0, tiled=True)  28.5 us
    ppermute x9, starting transfers between devices, swap(): return lax.ppermute(x, AXES, [(i, i ^ mask) for i in range(N_DEV)])  16.4 us
    ppermute x9, waiting for transfers between devices, swap(): return lax.ppermute(x, AXES, [(i, i ^ mask) for i in range(N_DEV)])  12.4 us
    all_to_all x2, waiting for transfers between devices, to_all(): return lax.all_to_all(x, AXES, 0, 0, tiled=True)  11.7 us
    pallas_call x2, Pallas kernels, stiff_apply(): pl.pallas_call(apply_body, out_shape=jax.ShapeDtypeStruct((3, VR, 256), F...  9.14 us
    pallas_call x2, Pallas kernels, settle(): pl.pallas_call(functools.partial(settle_body, first=first), out_shape=tup...  8.12 us
    ppermute x2, waiting for transfers between devices, from_gx(): lax.ppermute(x, 'gx', [(i, i + by) for i in range(N_GX) if 0 <= i + by <...  5.98 us
    pallas_call x1, Pallas kernels, fluid(): pl.pallas_call(fluid_body, out_shape=jax.ShapeDtypeStruct((8, 32, 512), F...  5.61 us
  transfers between devices with their start and end apart: 22, of which 16 were waited for; matrix products, arithmetic and copies ran while one was open for 3% of the time, Pallas kernels for 8%

profile of v4, /device:TPU:1, one launch (start us, length us, event | category | flops | bytes accessed | tf_op | source)
XLA Modules:
  0.0 133.4 jit_solution(938135818356753016)
XLA Ops:
  0.7 1.1 slice_bitcast_fusion.1
  2.0 2.1 %collective-permute-start = (f32[2,3,32,128]{3,2,1,0:T(8,128)S(1)}, f32[2,3,32,128]{3,2,1,0:T(8,128)S(1)}, u32[]{:S(2)}, u32[]{:S(2)}) collective-permute-start(f32[2,3,32,128]{3,2,1,0:T(8,128)S(1)} %get-tuple-element.69), channel_id=1, source_target_pairs={{0,4},{4,0},{8,12},{12,8},{16,20},{20,16},{24,28},{28,24},{32,36},... | collective-permute-start | bytes 294920 | tf_op jit(solution)/shard_map/ppermute | solution.py:595
  4.1 0.7 collective-permute-start.1
  5.1 1.1 collective-permute-done.xa_ref
  6.2 0.8 shard_map.140
  7.0 2.1 %collective-permute-start.2 = (f32[320,128]{1,0:T(8,128)S(1)}, f32[320,128]{1,0:T(8,128)S(1)}, u32[]{:S(2)}, u32[]{:S(2)}) collective-permute-start(f32[320,128]{1,0:T(8,128)S(1)} %pad_maximum_fusion.6), channel_id=1, source_target_pairs={{0,1},{1,0},{2,3},{3,2},{4,5},{5,4},{6,7},{7,6},{8,9},{9,8},{10,11... | collective-permute-start | bytes 491528 | tf_op jit(solution)/shard_map/ppermute | solution.py:35
  9.1 1.0 collective-permute-done.2
  10.2 3.1 %collective-permute-start.3 = (f32[448,128]{1,0:T(8,128)S(1)}, f32[448,128]{1,0:T(8,128)S(1)}, u32[]{:S(2)}, u32[]{:S(2)}) collective-permute-start(f32[448,128]{1,0:T(8,128)S(1)} %pad_maximum_fusion.3), channel_id=1, source_target_pairs={{0,2},{1,3},{2,0},{3,1},{4,6},{5,7},{6,4},{7,5},{8,10},{9,11},{10,... | collective-permute-start | bytes 688136 | tf_op jit(solution)/shard_map/ppermute | solution.py:35
  13.2 0.7 slice_bitcast_fusion.8
  13.9 6.2 %collective-permute-done.3 = f32[448,128]{1,0:T(8,128)S(1)} collective-permute-done((f32[448,128]{1,0:T(8,128)S(1)}, f32[448,128]{1,0:T(8,128)S(1)}, u32[]{:S(2)}, u32[]{:S(2)}) %collective-permute-start.3) | collective-permute-done | bytes 229408 | tf_op jit(solution)/shard_map/ppermute | solution.py:35
  20.5 1.0 shard_map.142
  21.5 1.3 collective-permute-start.4
  23.5 3.2 %collective-permute-done.4 = f32[4,256]{1,0:T(4,128)S(1)} collective-permute-done((f32[4,256]{1,0:T(4,128)S(1)}, f32[4,256]{1,0:T(4,128)S(1)}, u32[]{:S(2)}, u32[]{:S(2)}) %collective-permute-start.4) | collective-permute-done | bytes 4128 | tf_op jit(solution)/shard_map/ppermute | solution.py:39
  26.7 0.7 copy-done.10
  27.5 4.6 %shard_map.143 = f32[3,56,256]{2,1,0:T(8,128)S(1)} custom-call(s32[1]{0:T(128)S(6)} %copy.59.live_ref.refs_1_, f32[3,56,256]{2,1,0:T(8,128)S(1)} %broadcast_select_fusion.8.v_ref.refs_6_, s32[27,384]{1,0:T(8,128)S(1)} %copy-done.10, f32[1,384]{1,0:T(1,128)S(1)} %reshape.42.coef_ref.refs_8_, f32[81,81]{1,0:T(8,128)S(1)} %copy-done.2), custom_call_target="tpu_custom_call" | custom-call | flops 6000000000 | bytes 24000000 | tf_op jit(solution)/shard_map/pallas_call | solution.py:142
  32.2 0.9 pad_maximum_fusion
  33.2 0.5 collective-permute-done.5
  33.8 5.2 %collective-permute-start.6 = (f32[3,56,256]{2,0,1:T(4,128)S(1)}, f32[3,56,256]{2,0,1:T(4,128)S(1)}, u32[]{:S(2)}, u32[]{:S(2)}) collective-permute-start(f32[3,56,256]{2,0,1:T(4,128)S(1)} %copy_add_fusion.1), channel_id=1, source_target_pairs={{0,2},{1,3},{2,0},{3,1},{4,6},{5,7},{6,4},{7,5},{8,10},{9,11},{10,... | collective-permute-start | bytes 516104 | tf_op jit(solution)/shard_map/ppermute | solution.py:35
  39.0 1.5 %collective-permute-start.7 = (f32[3,256]{1,0:T(4,128)S(1)}, f32[3,256]{1,0:T(4,128)S(1)}, u32[]{:S(2)}, u32[]{:S(2)}) collective-permute-start(f32[3,256]{1,0:T(4,128)S(1)} %get-tuple-element.91), channel_id=1, source_target_pairs={{0,4},{1,7},{2,6},{3,5},{4,0},{5,3},{6,2},{7,1},{8,12},{9,15},{10,... | collective-permute-start | bytes 9224 | tf_op jit(solution)/shard_map/ppermute | solution.py:593
  40.5 0.6 collective-permute-start.8
  41.3 2.7 %collective-permute-done.7 = f32[3,256]{1,0:T(4,128)S(1)} collective-permute-done((f32[3,256]{1,0:T(4,128)S(1)}, f32[3,256]{1,0:T(4,128)S(1)}, u32[]{:S(2)}, u32[]{:S(2)}) %collective-permute-start.7) | collective-permute-done | bytes 3104 | tf_op jit(solution)/shard_map/ppermute | solution.py:593
  44.0 0.9 collective-permute-done.6
  44.9 0.8 collective-permute-start.9
  45.8 0.7 collective-permute-done.9
  46.5 4.5 %shard_map.144 = (f32[3,56,256]{2,1,0:T(8,128)S(1)}, f32[512,128]{1,0:T(8,128)}, f32[16,128]{1,0:T(8,128)S(1)}) custom-call(s32[2]{0:T(128)S(1)} %pad_add_fusion.at_ref.refs_0_, s32[1]{0:T(128)S(6)} %copy.59.live_ref.refs_1_, f32[3,56,256]{2,1,0:T(8,128)S(1)} %copy.42.refs_2_, f32[3,56,256]{2,1,0:T(8,128)S(1)} %copy.43.refs_3_, ...), custom_call_target="tpu_custom_call" | custom-call | flops 6000000000 | bytes 24000000 | tf_op jit(solution)/shard_map/pallas_call | solution.py:337
  51.0 17.2 %all-to-all-start = ((f32[128,4,128]{2,1,0:T(4,128)}), f32[128,4,128]{2,1,0:T(4,128)S(1)}, u32[]{:S(2)}, u32[]{:S(2)}) async-start(f32[128,4,128]{2,1,0:T(4,128)} %bitcast.17), calls=%async_computation | async-start | bytes 524288 | tf_op jit(solution)/shard_map/all_to_all | solution.py:622
  68.2 1.0 broadcast_select_fusion.3
  69.2 1.4 %collective-permute-start.11 = (f32[2,3,32,512]{3,2,1,0:T(8,128)}, f32[2,3,32,512]{3,2,1,0:T(8,128)S(1)}, u32[]{:S(2)}, u32[]{:S(2)}) collective-permute-start(f32[2,3,32,512]{3,2,1,0:T(8,128)} %get-tuple-element.67), channel_id=1, source_target_pairs={{0,4},{4,0},{8,12},{12,8},{16,20},{20,16},{24,28},{28,24},{32,36},... | collective-permute-start | bytes 1179656 | tf_op jit(solution)/shard_map/ppermute | solution.py:595
  70.6 0.7 collective-permute-start.12
  71.3 7.9 %all-to-all-done = f32[128,4,128]{2,1,0:T(4,128)S(1)} async-done(((f32[128,4,128]{2,1,0:T(4,128)}), f32[128,4,128]{2,1,0:T(4,128)S(1)}, u32[]{:S(2)}, u32[]{:S(2)}) %all-to-all-start) | async-done | bytes 262176 | tf_op jit(solution)/shard_map/all_to_all | solution.py:622
  79.2 1.1 shard_map.145
  80.3 1.3 collective-permute-start.10
  81.9 2.8 %collective-permute-done.10 = f32[3,256]{1,0:T(4,128)S(1)} collective-permute-done((f32[3,256]{1,0:T(4,128)S(1)}, f32[3,256]{1,0:T(4,128)S(1)}, u32[]{:S(2)}, u32[]{:S(2)}) %collective-permute-start.10) | collective-permute-done | bytes 3104 | tf_op jit(solution)/shard_map/ppermute | solution.py:39
  84.8 4.6 %shard_map.146 = f32[3,56,256]{2,1,0:T(8,128)S(1)} custom-call(s32[1]{0:T(128)S(6)} %copy.59.live_ref.refs_1_, f32[3,56,256]{2,1,0:T(8,128)S(1)} %broadcast_select_fusion.7.v_ref.refs_6_, s32[27,384]{1,0:T(8,128)S(1)} %copy-done.10, f32[1,384]{1,0:T(1,128)S(1)} %reshape.42.coef_ref.refs_8_, f32[81,81]{1,0:T(8,128)S(1)} %copy-done.2), custom_call_target="tpu_custom_call" | custom-call | flops 6000000000 | bytes 24000000 | tf_op jit(solution)/shard_map/pallas_call | solution.py:142
  89.9 1.3 %collective-permute-done.13 = f32[3,56,256]{2,0,1:T(4,128)S(1)} collective-permute-done((f32[3,56,256]{2,0,1:T(4,128)S(1)}, f32[3,56,256]{2,0,1:T(4,128)S(1)}, u32[]{:S(2)}, u32[]{:S(2)}) %collective-permute-start.13) | collective-permute-done | bytes 172064 | tf_op jit(solution)/shard_map/ppermute | solution.py:35
  91.4 3.7 %collective-permute-start.14 = (f32[3,56,256]{2,0,1:T(4,128)S(1)}, f32[3,56,256]{2,0,1:T(4,128)S(1)}, u32[]{:S(2)}, u32[]{:S(2)}) collective-permute-start(f32[3,56,256]{2,0,1:T(4,128)S(1)} %copy_add_fusion), channel_id=1, source_target_pairs={{0,2},{1,3},{2,0},{3,1},{4,6},{5,7},{6,4},{7,5},{8,10},{9,11},{10,... | collective-permute-start | bytes 516104 | tf_op jit(solution)/shard_map/ppermute | solution.py:35
  95.0 1.6 %collective-permute-start.15 = (f32[3,256]{1,0:T(4,128)S(1)}, f32[3,256]{1,0:T(4,128)S(1)}, u32[]{:S(2)}, u32[]{:S(2)}) collective-permute-start(f32[3,256]{1,0:T(4,128)S(1)} %get-tuple-element.89), channel_id=1, source_target_pairs={{0,4},{1,7},{2,6},{3,5},{4,0},{5,3},{6,2},{7,1},{8,12},{9,15},{10,... | collective-permute-start | bytes 9224 | tf_op jit(solution)/shard_map/ppermute | solution.py:593
  96.7 0.6 collective-permute-start.16
  97.5 2.5 %collective-permute-done.15 = f32[3,256]{1,0:T(4,128)S(1)} collective-permute-done((f32[3,256]{1,0:T(4,128)S(1)}, f32[3,256]{1,0:T(4,128)S(1)}, u32[]{:S(2)}, u32[]{:S(2)}) %collective-permute-start.15) | collective-permute-done | bytes 3104 | tf_op jit(solution)/shard_map/ppermute | solution.py:593
  100.0 0.9 collective-permute-done.14
  100.9 0.8 collective-permute-start.17
  101.8 0.8 collective-permute-done.17
  103.0 4.9 %collective-permute-start.19 = (f32[2,14,4,512]{3,2,1,0:T(4,128)S(1)}, f32[2,14,4,512]{3,2,1,0:T(4,128)S(1)}, u32[]{:S(2)}, u32[]{:S(2)}) collective-permute-start(f32[2,14,4,512]{3,2,1,0:T(4,128)S(1)} %get-tuple-element.56), channel_id=1, source_target_pairs={{1,2},{2,1},{5,6},{6,5},{9,10},{10,9},{13,14},{14,13},{17,18},{18,... | collective-permute-start | bytes 688136 | tf_op jit(solution)/shard_map/ppermute | solution.py:670
  107.9 3.6 %shard_map.147 = (f32[3,56,256]{2,1,0:T(8,128)S(1)}, f32[128,128]{1,0:T(8,128)}) custom-call(s32[2]{0:T(128)S(1)} %pad_add_fusion.at_ref.refs_0_, s32[1]{0:T(128)S(6)} %copy.59.live_ref.refs_1_, f32[3,56,256]{2,1,0:T(8,128)S(1)} %copy.46.refs_2_, f32[3,56,256]{2,1,0:T(8,128)S(1)} %copy.47.refs_3_, f32[2,3,256]{2,1,0:T(4,128)S(1)} %fusion.4.refs_4_, ...), custom_call_target="tpu_custom_call" | custom-call | flops 6000000000 | bytes 24000000 | tf_op jit(solution)/shard_map/pallas_call | solution.py:337
  111.9 11.3 %all-to-all-start.1 = ((f32[128,1,128]{2,1,0:T(1,128)}), f32[128,1,128]{2,1,0:T(1,128)S(1)}, u32[]{:S(2)}, u32[]{:S(2)}) async-start(f32[128,1,128]{2,1,0:T(1,128)} %bitcast.28), calls=%async_computation.1 | async-start | bytes 131072 | tf_op jit(solution)/shard_map/all_to_all | solution.py:622
  123.2 5.6 %shard_map.148 = f32[8,32,512]{2,1,0:T(8,128)} custom-call(s32[2]{0:T(128)S(1)} %pad_add_fusion.at_ref.refs_0_, f32[8,32,512]{2,1,0:T(8,128)S(1)} %copy-done, f32[8,32,512]{2,1,0:T(8,128)S(1)} %copy-done.1, f32[2,3,32,512]{3,2,1,0:T(8,128)S(1)} %collective-permute-done.11.xa_ref, f32[2,3,32,512]{3,2,1,0:T(8,128)S(1)} %collective-permute-done.12.xb_ref, ...), custom_call_target="tpu_custom_call" | custom-call | flops 100000000 | bytes 20000000 | tf_op jit(solution)/shard_map/pallas_call | solution.py:526
  128.8 3.8 %all-to-all-done.1 = f32[128,1,128]{2,1,0:T(1,128)S(1)} async-done(((f32[128,1,128]{2,1,0:T(1,128)}), f32[128,1,128]{2,1,0:T(1,128)S(1)}, u32[]{:S(2)}, u32[]{:S(2)}) %all-to-all-start.1) | async-done | bytes 65568 | tf_op jit(solution)/shard_map/all_to_all | solution.py:622
  132.7 0.8 shard_map.149
  (106 shorter events, 3.2 us)
Async XLA Ops:
  0.6 1.2 copy-start.1
  1.9 2.9 %copy-start.2 = (f32[81,81]{1,0:T(8,128)S(1)}, f32[81,81]{1,0:T(8,128)}, u32[]{:S(2)}) copy-start(f32[81,81]{1,0:T(8,128)} %stiff_ref.9) | copy-start | bytes 78736
  1.9 2.9 %copy-start.3 = (f32[3,3072]{1,0:T(4,128)S(1)}, f32[3,3072]{1,0:T(4,128)}, u32[]{:S(2)}) copy-start(f32[3,3072]{1,0:T(4,128)} %load_ref.1) | copy-start | bytes 110596
  1.9 2.9 %copy-start.6 = (f32[3072]{0:T(1024)S(1)}, f32[3072]{0:T(1024)}, u32[]{:S(2)}) copy-start(f32[3072]{0:T(1024)} %param.19) | copy-start | bytes 36868
  1.9 2.9 %copy-start.9 = (f32[3,256]{1,0:T(4,128)S(1)}, f32[3,256]{1,0:T(4,128)}, u32[]{:S(2)}) copy-start(f32[3,256]{1,0:T(4,128)} %normal_ref.1) | copy-start | bytes 9220
  1.9 4.2 %copy-start = (f32[8,32,512]{2,1,0:T(8,128)S(1)}, f32[8,32,512]{2,1,0:T(8,128)}, u32[]{:S(2)}) copy-start(f32[8,32,512]{2,1,0:T(8,128)} %fs_ref.3) | copy-start | bytes 1572868
  2.0 2.9 %copy-start.8 = (f32[4,256]{1,0:T(4,128)S(1)}, f32[4,256]{1,0:T(4,128)}, u32[]{:S(2)}) copy-start(f32[4,256]{1,0:T(4,128)} %tw_ref.1) | copy-start | bytes 12292
  2.0 2.9 %copy-start.7 = (s32[4,256]{1,0:T(4,128)S(1)}, s32[4,256]{1,0:T(4,128)}, u32[]{:S(2)}) copy-start(s32[4,256]{1,0:T(4,128)} %face_ref.1) | copy-start | bytes 12292
  2.0 4.1 %collective-permute-start = (f32[2,3,32,128]{3,2,1,0:T(8,128)S(1)}, f32[2,3,32,128]{3,2,1,0:T(8,128)S(1)}, u32[]{:S(2)}, u32[]{:S(2)}) collective-permute-start(f32[2,3,32,128]{3,2,1,0:T(8,128)S(1)} %get-tuple-element.69), channel_id=1, source_target_pairs={{0,4},{4,0},{8,12},{12,8},{16,20},{20,16},{24,28},{28,24},{32,36},... | collective-permute-start | bytes 294920 | tf_op jit(solution)/shard_map/ppermute | solution.py:595
  4.1 2.0 %collective-permute-start.1 = (f32[2,3,32,128]{3,2,1,0:T(8,128)S(1)}, f32[2,3,32,128]{3,2,1,0:T(8,128)S(1)}, u32[]{:S(2)}, u32[]{:S(2)}) collective-permute-start(f32[2,3,32,128]{3,2,1,0:T(8,128)S(1)} %get-tuple-element.68), channel_id=1, source_target_pairs={{4,8},{12,16},{20,24},{28,32},{36,40},{44,48},{52,56},{60,64},{68,... | collective-permute-start | bytes 294920 | tf_op jit(solution)/shard_map/ppermute | solution.py:595
  4.9 1.3 copy-start.4
  4.9 1.3 copy-start.5
  7.0 3.1 %collective-permute-start.2 = (f32[320,128]{1,0:T(8,128)S(1)}, f32[320,128]{1,0:T(8,128)S(1)}, u32[]{:S(2)}, u32[]{:S(2)}) collective-permute-start(f32[320,128]{1,0:T(8,128)S(1)} %pad_maximum_fusion.6), channel_id=1, source_target_pairs={{0,1},{1,0},{2,3},{3,2},{4,5},{5,4},{6,7},{7,6},{8,9},{9,8},{10,11... | collective-permute-start | bytes 491528 | tf_op jit(solution)/shard_map/ppermute | solution.py:35
  10.2 10.0 %collective-permute-start.3 = (f32[448,128]{1,0:T(8,128)S(1)}, f32[448,128]{1,0:T(8,128)S(1)}, u32[]{:S(2)}, u32[]{:S(2)}) collective-permute-start(f32[448,128]{1,0:T(8,128)S(1)} %pad_maximum_fusion.3), channel_id=1, source_target_pairs={{0,2},{1,3},{2,0},{3,1},{4,6},{5,7},{6,4},{7,5},{8,10},{9,11},{10,... | collective-permute-start | bytes 688136 | tf_op jit(solution)/shard_map/ppermute | solution.py:35
  21.5 1.3 %copy-start.17 = (f32[384]{0:T(512)S(1)}, f32[384]{0:T(512)}, u32[]{:S(2)}) copy-start(f32[384]{0:T(512)} %param.16) | copy-start | bytes 4612
  21.5 5.2 %collective-permute-start.4 = (f32[4,256]{1,0:T(4,128)S(1)}, f32[4,256]{1,0:T(4,128)S(1)}, u32[]{:S(2)}, u32[]{:S(2)}) collective-permute-start(f32[4,256]{1,0:T(4,128)S(1)} %pad_maximum_fusion.11), channel_id=1, source_target_pairs={{4,0},{8,4},{12,8},{16,12},{20,16},{24,20},{28,24},{32,28},{36,32}... | collective-permute-start | bytes 12296 | tf_op jit(solution)/shard_map/ppermute | solution.py:39
  26.7 0.8 copy-start.10
  32.1 1.6 %collective-permute-start.5 = (f32[3,56,256]{2,0,1:T(4,128)S(1)}, f32[3,56,256]{2,0,1:T(4,128)S(1)}, u32[]{:S(2)}, u32[]{:S(2)}) collective-permute-start(f32[3,56,256]{2,0,1:T(4,128)S(1)} %copy.41), channel_id=1, source_target_pairs={{0,1},{1,0},{2,3},{3,2},{4,5},{5,4},{6,7},{7,6},{8,9},{9,8},{10,11... | collective-permute-start | bytes 516104 | tf_op jit(solution)/shard_map/ppermute | solution.py:35
  33.8 11.1 %collective-permute-start.6 = (f32[3,56,256]{2,0,1:T(4,128)S(1)}, f32[3,56,256]{2,0,1:T(4,128)S(1)}, u32[]{:S(2)}, u32[]{:S(2)}) collective-permute-start(f32[3,56,256]{2,0,1:T(4,128)S(1)} %copy_add_fusion.1), channel_id=1, source_target_pairs={{0,2},{1,3},{2,0},{3,1},{4,6},{5,7},{6,4},{7,5},{8,10},{9,11},{10,... | collective-permute-start | bytes 516104 | tf_op jit(solution)/shard_map/ppermute | solution.py:35
  39.0 5.0 %collective-permute-start.7 = (f32[3,256]{1,0:T(4,128)S(1)}, f32[3,256]{1,0:T(4,128)S(1)}, u32[]{:S(2)}, u32[]{:S(2)}) collective-permute-start(f32[3,256]{1,0:T(4,128)S(1)} %get-tuple-element.91), channel_id=1, source_target_pairs={{0,4},{1,7},{2,6},{3,5},{4,0},{5,3},{6,2},{7,1},{8,12},{9,15},{10,... | collective-permute-start | bytes 9224 | tf_op jit(solution)/shard_map/ppermute | solution.py:593
  40.5 3.4 %collective-permute-start.8 = (f32[3,256]{1,0:T(4,128)S(1)}, f32[3,256]{1,0:T(4,128)S(1)}, u32[]{:S(2)}, u32[]{:S(2)}) collective-permute-start(f32[3,256]{1,0:T(4,128)S(1)} %get-tuple-element.90), channel_id=1, source_target_pairs={{4,8},{5,11},{6,10},{7,9},{12,16},{13,19},{14,18},{15,17},{20,24},... | collective-permute-start | bytes 9224 | tf_op jit(solution)/shard_map/ppermute | solution.py:593
  44.9 1.6 %collective-permute-start.9 = (f32[2,3,256]{2,1,0:T(4,128)S(1)}, f32[2,3,256]{2,1,0:T(4,128)S(1)}, u32[]{:S(2)}, u32[]{:S(2)}) collective-permute-start(f32[2,3,256]{2,1,0:T(4,128)S(1)} %pad_maximum_fusion.9), channel_id=1, source_target_pairs={{0,1},{1,0},{2,3},{3,2},{4,5},{5,4},{6,7},{7,6},{8,9},{9,8},{10,11... | collective-permute-start | bytes 18440 | tf_op jit(solution)/shard_map/ppermute | solution.py:35
  46.5 21.7 %copy-start.12 = (f32[2,3,32,512]{3,2,1,0:T(8,128)S(1)}, f32[2,3,32,512]{3,2,1,0:T(8,128)}, u32[]{:S(2)}) copy-start(f32[2,3,32,512]{3,2,1,0:T(8,128)} %get-tuple-element.40) | copy-start | bytes 1179652
  51.0 17.2 %copy-start.11 = (f32[2,3,32,512]{3,2,1,0:T(8,128)S(1)}, f32[2,3,32,512]{3,2,1,0:T(8,128)}, u32[]{:S(2)}) copy-start(f32[2,3,32,512]{3,2,1,0:T(8,128)} %get-tuple-element.41) | copy-start | bytes 1179652
  51.0 28.1 %all-to-all-start = ((f32[128,4,128]{2,1,0:T(4,128)}), f32[128,4,128]{2,1,0:T(4,128)S(1)}, u32[]{:S(2)}, u32[]{:S(2)}) async-start(f32[128,4,128]{2,1,0:T(4,128)} %bitcast.17), calls=%async_computation | async-start | bytes 524288 | tf_op jit(solution)/shard_map/all_to_all | solution.py:622
  69.2 15.6 %collective-permute-start.11 = (f32[2,3,32,512]{3,2,1,0:T(8,128)}, f32[2,3,32,512]{3,2,1,0:T(8,128)S(1)}, u32[]{:S(2)}, u32[]{:S(2)}) collective-permute-start(f32[2,3,32,512]{3,2,1,0:T(8,128)} %get-tuple-element.67), channel_id=1, source_target_pairs={{0,4},{4,0},{8,12},{12,8},{16,20},{20,16},{24,28},{28,24},{32,36},... | collective-permute-start | bytes 1179656 | tf_op jit(solution)/shard_map/ppermute | solution.py:595
  70.6 14.2 %collective-permute-start.12 = (f32[2,3,32,512]{3,2,1,0:T(8,128)}, f32[2,3,32,512]{3,2,1,0:T(8,128)S(1)}, u32[]{:S(2)}, u32[]{:S(2)}) collective-permute-start(f32[2,3,32,512]{3,2,1,0:T(8,128)} %get-tuple-element.66), channel_id=1, source_target_pairs={{4,8},{12,16},{20,24},{28,32},{36,40},{44,48},{52,56},{60,64},{68,... | collective-permute-start | bytes 1179656 | tf_op jit(solution)/shard_map/ppermute | solution.py:595
  80.3 4.4 %collective-permute-start.10 = (f32[3,256]{1,0:T(4,128)S(1)}, f32[3,256]{1,0:T(4,128)S(1)}, u32[]{:S(2)}, u32[]{:S(2)}) collective-permute-start(f32[3,256]{1,0:T(4,128)S(1)} %bitcast.69), channel_id=1, source_target_pairs={{4,0},{8,4},{12,8},{16,12},{20,16},{24,20},{28,24},{32,28},{36,32}... | collective-permute-start | bytes 9224 | tf_op jit(solution)/shard_map/ppermute | solution.py:39
  89.5 1.7 %collective-permute-start.13 = (f32[3,56,256]{2,0,1:T(4,128)S(1)}, f32[3,56,256]{2,0,1:T(4,128)S(1)}, u32[]{:S(2)}, u32[]{:S(2)}) collective-permute-start(f32[3,56,256]{2,0,1:T(4,128)S(1)} %copy.45), channel_id=1, source_target_pairs={{0,1},{1,0},{2,3},{3,2},{4,5},{5,4},{6,7},{7,6},{8,9},{9,8},{10,11... | collective-permute-start | bytes 516104 | tf_op jit(solution)/shard_map/ppermute | solution.py:35
  91.2 6.1 %copy-start.13 = (f32[1,8,4,512]{3,2,1,0:T(4,128)S(1)}, f32[1,8,4,512]{3,2,1,0:T(4,128)}, u32[]{:S(2)}) copy-start(f32[1,8,4,512]{3,2,1,0:T(4,128)} %get-tuple-element.72) | copy-start | bytes 196612
  91.2 6.1 %copy-start.14 = (f32[1,8,4,512]{3,2,1,0:T(4,128)S(1)}, f32[1,8,4,512]{3,2,1,0:T(4,128)}, u32[]{:S(2)}) copy-start(f32[1,8,4,512]{3,2,1,0:T(4,128)} %get-tuple-element.73) | copy-start | bytes 196612
  91.2 6.1 %copy-start.15 = (f32[1,8,4,512]{3,2,1,0:T(4,128)S(1)}, f32[1,8,4,512]{3,2,1,0:T(4,128)}, u32[]{:S(2)}) copy-start(f32[1,8,4,512]{3,2,1,0:T(4,128)} %get-tuple-element.100) | copy-start | bytes 196612
  91.2 6.1 %copy-start.16 = (f32[1,8,4,512]{3,2,1,0:T(4,128)S(1)}, f32[1,8,4,512]{3,2,1,0:T(4,128)}, u32[]{:S(2)}) copy-start(f32[1,8,4,512]{3,2,1,0:T(4,128)} %get-tuple-element.101) | copy-start | bytes 196612
  91.4 9.6 %collective-permute-start.14 = (f32[3,56,256]{2,0,1:T(4,128)S(1)}, f32[3,56,256]{2,0,1:T(4,128)S(1)}, u32[]{:S(2)}, u32[]{:S(2)}) collective-permute-start(f32[3,56,256]{2,0,1:T(4,128)S(1)} %copy_add_fusion), channel_id=1, source_target_pairs={{0,2},{1,3},{2,0},{3,1},{4,6},{5,7},{6,4},{7,5},{8,10},{9,11},{10,... | collective-permute-start | bytes 516104 | tf_op jit(solution)/shard_map/ppermute | solution.py:35
  95.0 5.0 %collective-permute-start.15 = (f32[3,256]{1,0:T(4,128)S(1)}, f32[3,256]{1,0:T(4,128)S(1)}, u32[]{:S(2)}, u32[]{:S(2)}) collective-permute-start(f32[3,256]{1,0:T(4,128)S(1)} %get-tuple-element.89), channel_id=1, source_target_pairs={{0,4},{1,7},{2,6},{3,5},{4,0},{5,3},{6,2},{7,1},{8,12},{9,15},{10,... | collective-permute-start | bytes 9224 | tf_op jit(solution)/shard_map/ppermute | solution.py:593
  96.7 3.3 %collective-permute-start.16 = (f32[3,256]{1,0:T(4,128)S(1)}, f32[3,256]{1,0:T(4,128)S(1)}, u32[]{:S(2)}, u32[]{:S(2)}) collective-permute-start(f32[3,256]{1,0:T(4,128)S(1)} %get-tuple-element.88), channel_id=1, source_target_pairs={{4,8},{5,11},{6,10},{7,9},{12,16},{13,19},{14,18},{15,17},{20,24},... | collective-permute-start | bytes 9224 | tf_op jit(solution)/shard_map/ppermute | solution.py:593
  100.9 1.6 %collective-permute-start.17 = (f32[2,3,256]{2,1,0:T(4,128)S(1)}, f32[2,3,256]{2,1,0:T(4,128)S(1)}, u32[]{:S(2)}, u32[]{:S(2)}) collective-permute-start(f32[2,3,256]{2,1,0:T(4,128)S(1)} %pad_maximum_fusion.10), channel_id=1, source_target_pairs={{0,1},{1,0},{2,3},{3,2},{4,5},{5,4},{6,7},{7,6},{8,9},{9,8},{10,11... | collective-permute-start | bytes 18440 | tf_op jit(solution)/shard_map/ppermute | solution.py:35
  102.6 9.0 %collective-permute-start.18 = (f32[2,14,4,512]{3,2,1,0:T(4,128)S(1)}, f32[2,14,4,512]{3,2,1,0:T(4,128)S(1)}, u32[]{:S(2)}, u32[]{:S(2)}) collective-permute-start(f32[2,14,4,512]{3,2,1,0:T(4,128)S(1)} %get-tuple-element.55), channel_id=1, source_target_pairs={{0,1},{1,0},{2,3},{3,2},{4,5},{5,4},{6,7},{7,6},{8,9},{9,8},{10,11... | collective-permute-start | bytes 688136 | tf_op jit(solution)/shard_map/ppermute | solution.py:35
  103.0 8.8 %collective-permute-start.19 = (f32[2,14,4,512]{3,2,1,0:T(4,128)S(1)}, f32[2,14,4,512]{3,2,1,0:T(4,128)S(1)}, u32[]{:S(2)}, u32[]{:S(2)}) collective-permute-start(f32[2,14,4,512]{3,2,1,0:T(4,128)S(1)} %get-tuple-element.56), channel_id=1, source_target_pairs={{1,2},{2,1},{5,6},{6,5},{9,10},{10,9},{13,14},{14,13},{17,18},{18,... | collective-permute-start | bytes 688136 | tf_op jit(solution)/shard_map/ppermute | solution.py:670
  111.9 20.8 %all-to-all-start.1 = ((f32[128,1,128]{2,1,0:T(1,128)}), f32[128,1,128]{2,1,0:T(1,128)S(1)}, u32[]{:S(2)}, u32[]{:S(2)}) async-start(f32[128,1,128]{2,1,0:T(1,128)} %bitcast.28), calls=%async_computation.1 | async-start | bytes 131072 | tf_op jit(solution)/shard_map/all_to_all | solution.py:622

commit v5 on v4

--- a/solution.py
+++ b/solution.py
@@ -64,11 +64,15 @@
 
 
 def fill_table(v_ref, t_scr):
-    for c in range(3):
-        v = jnp.concatenate([v_ref[c], jnp.zeros((LR - VR, 256), F32)], axis=0)
-        hi, lo = split(v)
-        t_scr[c * LR : (c + 1) * LR, 0:256] = hi
-        t_scr[c * LR : (c + 1) * LR, 256:512] = lo
+    blocks = [v_ref[c, 0:OWN, :] for c in range(3)] + [v_ref[c, OWN : OWN + 1, :] for c in range(3)]
+    hi, lo = split(jnp.concatenate(blocks + [jnp.zeros((13, 256), F32)], axis=0))
+    t_scr[:, 0:256] = hi
+    t_scr[:, 256:512] = lo
+
+
+def select_rows(g, m, c):
+    s = (g[c * OWN : (c + 1) * OWN] * m[:OWN]).sum(axis=0, keepdims=True)
+    return s + g[144 + c : 145 + c] * m[OWN : OWN + 1]
 
 
 def block_of(b):
@@ -93,7 +97,7 @@
     one, nil = jnp.ones((256, 128), BF), jnp.zeros((256, 128), BF)
     oh_scr[:, 27 * 128 :] = jnp.zeros((256, 128), BF)
     ml_scr[:, 27 * 128 :] = jnp.zeros((LR, 128), BF)
-    a_scr[:, 27 * 128 :] = jnp.zeros((384, 128), BF)
+    a_scr[:, 27 * 128 :] = jnp.zeros((320, 128), BF)
     live = live_ref[0]
 
     def block(b, carry):
@@ -110,7 +114,7 @@
             g = jnp.dot(t_scr[...], jnp.concatenate([oh, oh], axis=0), preferred_element_type=F32)
             m = ml_scr[:, sp].astype(F32)
             for c in range(3):
-                s = (g[c * LR : (c + 1) * LR] * m).sum(axis=0, keepdims=True)
+                s = select_rows(g, m, c)
                 for h in range(2):
                     k = 2 * p + h
                     if k < 27:
@@ -120,13 +124,16 @@
         parts = (ph, prod - ph)
         for k in range(27):
             sl = slice(k * 128, k * 128 + 128)
-            m = ml_scr[:, sl].reshape(4, 16, 128)
-            for c in range(3):
-                row = c * 27 + k
-                for j, src in enumerate(parts):
-                    r16 = jnp.broadcast_to(src[row : row + 1, :], (16, 128)).astype(BF)
-                    at = j * 192 + c * LR
-                    a_scr[at : at + LR, sl] = (m * r16[None]).reshape(LR, 128)
+            m = ml_scr[0:OWN, sl].reshape(3, 16, 128)
+            last_row = ml_scr[OWN : OWN + 16, sl].astype(F32)[0:1]
+            for j, src in enumerate(parts):
+                rows = [src[c * 27 + k : c * 27 + k + 1, :] for c in range(3)]
+                for c in range(3):
+                    r16 = jnp.broadcast_to(rows[c], (16, 128)).astype(BF)
+                    at = j * 160 + c * OWN
+                    a_scr[at : at + OWN, sl] = (m * r16[None]).reshape(OWN, 128)
+                tail = jnp.concatenate(rows + [jnp.zeros((13, 128), F32)], axis=0) * last_row
+                a_scr[j * 160 + 144 : j * 160 + 160, sl] = tail.astype(BF)
         acc[...] += lax.dot_general(
             a_scr[...], oh_scr[...], (((1,), (1,)), ((), ())), preferred_element_type=F32
         )
@@ -134,8 +141,10 @@
 
     lax.fori_loop(0, (live + 127) // 128, block, 0)
     for c in range(3):
-        s = acc[c * LR : (c + 1) * LR, :] + acc[192 + c * LR : 192 + (c + 1) * LR, :]
-        out_ref[c] = s[:VR]
+        at = c * OWN
+        out_ref[c, 0:OWN, :] = acc[at : at + OWN, :] + acc[160 + at : 160 + at + OWN, :]
+        tail = acc[144 + c : 145 + c, :] + acc[304 + c : 305 + c, :]
+        out_ref[c, OWN:VR, :] = jnp.concatenate([tail, jnp.zeros((VR - OWN - 1, 256), F32)], axis=0)
 
 
 def stiff_apply(live, v, conn, coef, stiff):
@@ -145,13 +154,13 @@
         in_specs=[SM] + [VM] * 4,
         out_specs=VM,
         scratch_shapes=[
-            pltpu.VMEM((192, 512), BF),
+            pltpu.VMEM((160, 512), BF),
             pltpu.VMEM((192, 88), BF),
             pltpu.VMEM((256, 3584), BF),
             pltpu.VMEM((LR, 3584), BF),
             pltpu.VMEM((88, 128), F32),
-            pltpu.VMEM((384, 3584), BF),
-            pltpu.VMEM((384, 256), F32),
+            pltpu.VMEM((320, 3584), BF),
+            pltpu.VMEM((320, 256), F32),
         ],
         compiler_params=params(),
         cost_estimate=pl.CostEstimate(flops=6 * 10**9, bytes_accessed=24 * 10**6, transcendentals=0),
@@ -304,7 +313,7 @@
             g = jnp.dot(t_scr[...], jnp.concatenate([oh, oh], axis=0), preferred_element_type=F32)
             m = jnp.concatenate(masks, axis=1)
             for c in range(3):
-                s = (g[c * LR : (c + 1) * LR] * m).sum(axis=0, keepdims=True)
+                s = select_rows(g, m, c)
                 for h in range(2):
                     k = 2 * p + h
                     if k < 27:
@@ -340,7 +349,7 @@
         in_specs=[SM, SM] + [VM] * (8 + len(wall)),
         out_specs=(VM,) * len(shapes),
         scratch_shapes=[
-            pltpu.VMEM((192, 512), BF),
+            pltpu.VMEM((160, 512), BF),
             pltpu.VMEM((192, 88), BF),
             pltpu.VMEM((88, 128), F32),
             pltpu.VMEM((1, 128), F32),

time: 135 us -> 133 us (0.985); the launches traced: 133 us -> 135 us
  Pallas kernels: 26.6 us -> 19.3 us
  starting transfers between devices: 61.7 us -> 69 us
  waiting for transfers between devices: 36.7 us -> 38.1 us
    pallas_call x2, Pallas kernels: 9.14 us -> 4.19 us  [stiff_apply(): pl.pallas_call(apply_body, out_shape=jax.ShapeDtypeStruct((3, VR, 256), F...]
    ppermute x9, starting transfers between devices: 16.4 us -> 20.4 us  [swap(): return lax.ppermute(x, AXES, [(i, i ^ mask) for i in range(N_DEV)])]
    ppermute x1, waiting for transfers between devices: 0.28 us -> 3.68 us  [local(): mid = lax.ppermute(sides[1], 'gy', [(1, 2), (2, 1)])]
    all_to_all x2, starting transfers between devices: 28.5 us -> 31.4 us  [to_all(): return lax.all_to_all(x, AXES, 0, 0, tiled=True)]
    ppermute x4, waiting for transfers between devices: 5.24 us -> 2.65 us  [beside(): got.append(lax.ppermute(send, AXES, both_ends))]
    ppermute x4, starting transfers between devices: 4.44 us -> 7.03 us  [beside(): got.append(lax.ppermute(send, AXES, both_ends))]
    pallas_call x2, Pallas kernels: 8.12 us -> 5.69 us  [settle(): pl.pallas_call(functools.partial(settle_body, first=first), out_shape=tup...]
    ppermute x1, starting transfers between devices: 4.91 us -> 2.72 us  [local(): mid = lax.ppermute(sides[1], 'gy', [(1, 2), (2, 1)])]
  transfers between devices with their start and end apart: 22 -> 22, of which waited for: 16 -> 16; matrix products, arithmetic and copies ran while one was open for 3% -> 3% of each run, Pallas kernels for 8% -> 7%
where the time goes in v5:
time: 133 us; the launch traced here: 135 us
  starting transfers between devices  69 us (52%)
  waiting for transfers between devices  38.1 us (29%)
  Pallas kernels  19.3 us (15%)
  local copies, waits for them, and re-layouts  3.42 us (3%)
  other arithmetic  3.02 us (2%)
  between operations  1.96 us (1%)
    all_to_all x2, starting transfers between devices, to_all(): return lax.all_to_all(x, AXES, 0, 0, tiled=True)  31.4 us
    ppermute x9, starting transfers between devices, swap(): return lax.ppermute(x, AXES, [(i, i ^ mask) for i in range(N_DEV)])  20.4 us
    ppermute x9, waiting for transfers between devices, swap(): return lax.ppermute(x, AXES, [(i, i ^ mask) for i in range(N_DEV)])  13 us
    all_to_all x2, waiting for transfers between devices, to_all(): return lax.all_to_all(x, AXES, 0, 0, tiled=True)  11.7 us
    ppermute x4, starting transfers between devices, beside(): got.append(lax.ppermute(send, AXES, both_ends))  7.03 us
    ppermute x2, waiting for transfers between devices, from_gx(): lax.ppermute(x, 'gx', [(i, i + by) for i in range(N_GX) if 0 <= i + by <...  5.98 us
    pallas_call x2, Pallas kernels, settle(): pl.pallas_call(functools.partial(settle_body, first=first), out_shape=tup...  5.69 us
    pallas_call x1, Pallas kernels, fluid(): pl.pallas_call(fluid_body, out_shape=jax.ShapeDtypeStruct((8, 32, 512), F...  5.61 us
  transfers between devices with their start and end apart: 22, of which 16 were waited for; matrix products, arithmetic and copies ran while one was open for 3% of the time, Pallas kernels for 7%

profile of v5, /device:TPU:1, one launch (start us, length us, event | category | flops | bytes accessed | tf_op | source)
XLA Modules:
  0.0 134.7 jit_solution(124997677786955488)
XLA Ops:
  0.7 1.1 slice_bitcast_fusion.1
  2.0 2.1 %collective-permute-start = (f32[2,3,32,128]{3,2,1,0:T(8,128)S(1)}, f32[2,3,32,128]{3,2,1,0:T(8,128)S(1)}, u32[]{:S(2)}, u32[]{:S(2)}) collective-permute-start(f32[2,3,32,128]{3,2,1,0:T(8,128)S(1)} %get-tuple-element.69), channel_id=1, source_target_pairs={{0,4},{4,0},{8,12},{12,8},{16,20},{20,16},{24,28},{28,24},{32,36},... | collective-permute-start | bytes 294920 | tf_op jit(solution)/shard_map/ppermute | solution.py:604
  4.1 0.7 collective-permute-start.1
  5.1 1.1 collective-permute-done.xa_ref
  6.2 0.8 shard_map.140
  7.0 2.1 %collective-permute-start.2 = (f32[320,128]{1,0:T(8,128)S(1)}, f32[320,128]{1,0:T(8,128)S(1)}, u32[]{:S(2)}, u32[]{:S(2)}) collective-permute-start(f32[320,128]{1,0:T(8,128)S(1)} %pad_maximum_fusion.6), channel_id=1, source_target_pairs={{0,1},{1,0},{2,3},{3,2},{4,5},{5,4},{6,7},{7,6},{8,9},{9,8},{10,11... | collective-permute-start | bytes 491528 | tf_op jit(solution)/shard_map/ppermute | solution.py:35
  9.1 1.0 collective-permute-done.2
  10.2 3.1 %collective-permute-start.3 = (f32[448,128]{1,0:T(8,128)S(1)}, f32[448,128]{1,0:T(8,128)S(1)}, u32[]{:S(2)}, u32[]{:S(2)}) collective-permute-start(f32[448,128]{1,0:T(8,128)S(1)} %pad_maximum_fusion.3), channel_id=1, source_target_pairs={{0,2},{1,3},{2,0},{3,1},{4,6},{5,7},{6,4},{7,5},{8,10},{9,11},{10,... | collective-permute-start | bytes 688136 | tf_op jit(solution)/shard_map/ppermute | solution.py:35
  13.2 0.7 slice_bitcast_fusion.8
  13.9 6.2 %collective-permute-done.3 = f32[448,128]{1,0:T(8,128)S(1)} collective-permute-done((f32[448,128]{1,0:T(8,128)S(1)}, f32[448,128]{1,0:T(8,128)S(1)}, u32[]{:S(2)}, u32[]{:S(2)}) %collective-permute-start.3) | collective-permute-done | bytes 229408 | tf_op jit(solution)/shard_map/ppermute | solution.py:35
  20.5 1.0 shard_map.142
  21.5 1.3 collective-permute-start.4
  23.5 3.2 %collective-permute-done.4 = f32[4,256]{1,0:T(4,128)S(1)} collective-permute-done((f32[4,256]{1,0:T(4,128)S(1)}, f32[4,256]{1,0:T(4,128)S(1)}, u32[]{:S(2)}, u32[]{:S(2)}) %collective-permute-start.4) | collective-permute-done | bytes 4128 | tf_op jit(solution)/shard_map/ppermute | solution.py:39
  26.7 0.7 copy-done.10
  27.5 2.1 %shard_map.143 = f32[3,56,256]{2,1,0:T(8,128)S(1)} custom-call(s32[1]{0:T(128)S(6)} %copy.59.live_ref.refs_1_, f32[3,56,256]{2,1,0:T(8,128)S(1)} %broadcast_select_fusion.8.v_ref.refs_6_, s32[27,384]{1,0:T(8,128)S(1)} %copy-done.10, f32[1,384]{1,0:T(1,128)S(1)} %reshape.42.coef_ref.refs_8_, f32[81,81]{1,0:T(8,128)S(1)} %copy-done.2), custom_call_target="tpu_custom_call" | custom-call | flops 6000000000 | bytes 24000000 | tf_op jit(solution)/shard_map/pallas_call | solution.py:151
  29.7 4.1 %collective-permute-start.5 = (f32[3,56,256]{2,0,1:T(4,128)S(1)}, f32[3,56,256]{2,0,1:T(4,128)S(1)}, u32[]{:S(2)}, u32[]{:S(2)}) collective-permute-start(f32[3,56,256]{2,0,1:T(4,128)S(1)} %copy.41), channel_id=1, source_target_pairs={{0,1},{1,0},{2,3},{3,2},{4,5},{5,4},{6,7},{7,6},{8,9},{9,8},{10,11... | collective-permute-start | bytes 516104 | tf_op jit(solution)/shard_map/ppermute | solution.py:35
  33.8 0.9 pad_maximum_fusion
  35.0 3.0 %collective-permute-start.6 = (f32[3,56,256]{2,0,1:T(4,128)S(1)}, f32[3,56,256]{2,0,1:T(4,128)S(1)}, u32[]{:S(2)}, u32[]{:S(2)}) collective-permute-start(f32[3,56,256]{2,0,1:T(4,128)S(1)} %copy_add_fusion.1), channel_id=1, source_target_pairs={{0,2},{1,3},{2,0},{3,1},{4,6},{5,7},{6,4},{7,5},{8,10},{9,11},{10,... | collective-permute-start | bytes 516104 | tf_op jit(solution)/shard_map/ppermute | solution.py:35
  38.0 3.5 %collective-permute-start.7 = (f32[3,256]{1,0:T(4,128)S(1)}, f32[3,256]{1,0:T(4,128)S(1)}, u32[]{:S(2)}, u32[]{:S(2)}) collective-permute-start(f32[3,256]{1,0:T(4,128)S(1)} %get-tuple-element.91), channel_id=1, source_target_pairs={{0,4},{1,7},{2,6},{3,5},{4,0},{5,3},{6,2},{7,1},{8,12},{9,15},{10,... | collective-permute-start | bytes 9224 | tf_op jit(solution)/shard_map/ppermute | solution.py:602
  42.2 0.7 collective-permute-done.7
  43.4 1.3 collective-permute-start.9
  44.8 0.7 collective-permute-done.9
  45.6 3.3 %shard_map.144 = (f32[3,56,256]{2,1,0:T(8,128)S(1)}, f32[512,128]{1,0:T(8,128)}, f32[16,128]{1,0:T(8,128)S(1)}) custom-call(s32[2]{0:T(128)S(1)} %pad_add_fusion.at_ref.refs_0_, s32[1]{0:T(128)S(6)} %copy.59.live_ref.refs_1_, f32[3,56,256]{2,1,0:T(8,128)S(1)} %copy.42.refs_2_, f32[3,56,256]{2,1,0:T(8,128)S(1)} %copy.43.refs_3_, ...), custom_call_target="tpu_custom_call" | custom-call | flops 6000000000 | bytes 24000000 | tf_op jit(solution)/shard_map/pallas_call | solution.py:346
  48.8 20.0 %all-to-all-start = ((f32[128,4,128]{2,1,0:T(4,128)}), f32[128,4,128]{2,1,0:T(4,128)S(1)}, u32[]{:S(2)}, u32[]{:S(2)}) async-start(f32[128,4,128]{2,1,0:T(4,128)} %bitcast.17), calls=%async_computation | async-start | bytes 524288 | tf_op jit(solution)/shard_map/all_to_all | solution.py:631
  68.9 1.0 broadcast_select_fusion.3
  69.8 1.4 %collective-permute-start.11 = (f32[2,3,32,512]{3,2,1,0:T(8,128)}, f32[2,3,32,512]{3,2,1,0:T(8,128)S(1)}, u32[]{:S(2)}, u32[]{:S(2)}) collective-permute-start(f32[2,3,32,512]{3,2,1,0:T(8,128)} %get-tuple-element.67), channel_id=1, source_target_pairs={{0,4},{4,0},{8,12},{12,8},{16,20},{20,16},{24,28},{28,24},{32,36},... | collective-permute-start | bytes 1179656 | tf_op jit(solution)/shard_map/ppermute | solution.py:604
  71.2 0.7 collective-permute-start.12
  71.9 7.9 %all-to-all-done = f32[128,4,128]{2,1,0:T(4,128)S(1)} async-done(((f32[128,4,128]{2,1,0:T(4,128)}), f32[128,4,128]{2,1,0:T(4,128)S(1)}, u32[]{:S(2)}, u32[]{:S(2)}) %all-to-all-start) | async-done | bytes 262176 | tf_op jit(solution)/shard_map/all_to_all | solution.py:631
  79.8 1.1 shard_map.145
  81.0 1.3 collective-permute-start.10
  82.5 2.8 %collective-permute-done.10 = f32[3,256]{1,0:T(4,128)S(1)} collective-permute-done((f32[3,256]{1,0:T(4,128)S(1)}, f32[3,256]{1,0:T(4,128)S(1)}, u32[]{:S(2)}, u32[]{:S(2)}) %collective-permute-start.10) | collective-permute-done | bytes 3104 | tf_op jit(solution)/shard_map/ppermute | solution.py:39
  85.4 2.1 %shard_map.146 = f32[3,56,256]{2,1,0:T(8,128)S(1)} custom-call(s32[1]{0:T(128)S(6)} %copy.59.live_ref.refs_1_, f32[3,56,256]{2,1,0:T(8,128)S(1)} %broadcast_select_fusion.7.v_ref.refs_6_, s32[27,384]{1,0:T(8,128)S(1)} %copy-done.10, f32[1,384]{1,0:T(1,128)S(1)} %reshape.42.coef_ref.refs_8_, f32[81,81]{1,0:T(8,128)S(1)} %copy-done.2), custom_call_target="tpu_custom_call" | custom-call | flops 6000000000 | bytes 24000000 | tf_op jit(solution)/shard_map/pallas_call | solution.py:151
  87.6 4.2 %collective-permute-start.13 = (f32[3,56,256]{2,0,1:T(4,128)S(1)}, f32[3,56,256]{2,0,1:T(4,128)S(1)}, u32[]{:S(2)}, u32[]{:S(2)}) collective-permute-start(f32[3,56,256]{2,0,1:T(4,128)S(1)} %copy.45), channel_id=1, source_target_pairs={{0,1},{1,0},{2,3},{3,2},{4,5},{5,4},{6,7},{7,6},{8,9},{9,8},{10,11... | collective-permute-start | bytes 516104 | tf_op jit(solution)/shard_map/ppermute | solution.py:35
  91.9 1.0 collective-permute-done.13
  93.0 1.0 collective-permute-start.14
  94.1 2.2 %collective-permute-start.15 = (f32[3,256]{1,0:T(4,128)S(1)}, f32[3,256]{1,0:T(4,128)S(1)}, u32[]{:S(2)}, u32[]{:S(2)}) collective-permute-start(f32[3,256]{1,0:T(4,128)S(1)} %get-tuple-element.89), channel_id=1, source_target_pairs={{0,4},{1,7},{2,6},{3,5},{4,0},{5,3},{6,2},{7,1},{8,12},{9,15},{10,... | collective-permute-start | bytes 9224 | tf_op jit(solution)/shard_map/ppermute | solution.py:602
  96.3 0.6 collective-permute-start.16
  97.1 1.9 %collective-permute-done.15 = f32[3,256]{1,0:T(4,128)S(1)} collective-permute-done((f32[3,256]{1,0:T(4,128)S(1)}, f32[3,256]{1,0:T(4,128)S(1)}, u32[]{:S(2)}, u32[]{:S(2)}) %collective-permute-start.15) | collective-permute-done | bytes 3104 | tf_op jit(solution)/shard_map/ppermute | solution.py:602
  99.0 2.6 %collective-permute-done.14 = f32[3,56,256]{2,0,1:T(4,128)S(1)} collective-permute-done((f32[3,56,256]{2,0,1:T(4,128)S(1)}, f32[3,56,256]{2,0,1:T(4,128)S(1)}, u32[]{:S(2)}, u32[]{:S(2)}) %collective-permute-start.14) | collective-permute-done | bytes 172064 | tf_op jit(solution)/shard_map/ppermute | solution.py:35
  101.7 1.3 collective-permute-start.17
  103.0 0.8 collective-permute-done.17
  104.3 2.7 %collective-permute-start.19 = (f32[2,14,4,512]{3,2,1,0:T(4,128)S(1)}, f32[2,14,4,512]{3,2,1,0:T(4,128)S(1)}, u32[]{:S(2)}, u32[]{:S(2)}) collective-permute-start(f32[2,14,4,512]{3,2,1,0:T(4,128)S(1)} %get-tuple-element.56), channel_id=1, source_target_pairs={{1,2},{2,1},{5,6},{6,5},{9,10},{10,9},{13,14},{14,13},{17,18},{18,... | collective-permute-start | bytes 688136 | tf_op jit(solution)/shard_map/ppermute | solution.py:679
  107.0 2.4 %shard_map.147 = (f32[3,56,256]{2,1,0:T(8,128)S(1)}, f32[128,128]{1,0:T(8,128)}) custom-call(s32[2]{0:T(128)S(1)} %pad_add_fusion.at_ref.refs_0_, s32[1]{0:T(128)S(6)} %copy.59.live_ref.refs_1_, f32[3,56,256]{2,1,0:T(8,128)S(1)} %copy.46.refs_2_, f32[3,56,256]{2,1,0:T(8,128)S(1)} %copy.47.refs_3_, f32[2,3,256]{2,1,0:T(4,128)S(1)} %fusion.4.refs_4_, ...), custom_call_target="tpu_custom_call" | custom-call | flops 6000000000 | bytes 24000000 | tf_op jit(solution)/shard_map/pallas_call | solution.py:346
  109.4 3.7 %collective-permute-done.19.mid_ref = f32[2,14,4,512]{3,2,1,0:T(4,128)S(1)} collective-permute-done((f32[2,14,4,512]{3,2,1,0:T(4,128)S(1)}, f32[2,14,4,512]{3,2,1,0:T(4,128)S(1)}, u32[]{:S(2)}, u32[]{:S(2)}) %collective-permute-start.19) | collective-permute-done | bytes 229408 | tf_op jit(solution)/shard_map/ppermute | solution.py:679
  113.1 11.4 %all-to-all-start.1 = ((f32[128,1,128]{2,1,0:T(1,128)}), f32[128,1,128]{2,1,0:T(1,128)S(1)}, u32[]{:S(2)}, u32[]{:S(2)}) async-start(f32[128,1,128]{2,1,0:T(1,128)} %bitcast.28), calls=%async_computation.1 | async-start | bytes 131072 | tf_op jit(solution)/shard_map/all_to_all | solution.py:631
  124.5 5.6 %shard_map.148 = f32[8,32,512]{2,1,0:T(8,128)} custom-call(s32[2]{0:T(128)S(1)} %pad_add_fusion.at_ref.refs_0_, f32[8,32,512]{2,1,0:T(8,128)S(1)} %copy-done, f32[8,32,512]{2,1,0:T(8,128)S(1)} %copy-done.1, f32[2,3,32,512]{3,2,1,0:T(8,128)S(1)} %collective-permute-done.11.xa_ref, f32[2,3,32,512]{3,2,1,0:T(8,128)S(1)} %collective-permute-done.12.xb_ref, ...), custom_call_target="tpu_custom_call" | custom-call | flops 100000000 | bytes 20000000 | tf_op jit(solution)/shard_map/pallas_call | solution.py:535
  130.1 3.8 %all-to-all-done.1 = f32[128,1,128]{2,1,0:T(1,128)S(1)} async-done(((f32[128,1,128]{2,1,0:T(1,128)}), f32[128,1,128]{2,1,0:T(1,128)S(1)}, u32[]{:S(2)}, u32[]{:S(2)}) %all-to-all-start.1) | async-done | bytes 65568 | tf_op jit(solution)/shard_map/all_to_all | solution.py:631
  133.9 0.8 shard_map.149
  (106 shorter events, 3.9 us)
Async XLA Ops:
  0.6 1.2 copy-start.1
  1.9 2.9 %copy-start.2 = (f32[81,81]{1,0:T(8,128)S(1)}, f32[81,81]{1,0:T(8,128)}, u32[]{:S(2)}) copy-start(f32[81,81]{1,0:T(8,128)} %stiff_ref.9) | copy-start | bytes 78736
  1.9 2.9 %copy-start.3 = (f32[3,3072]{1,0:T(4,128)S(1)}, f32[3,3072]{1,0:T(4,128)}, u32[]{:S(2)}) copy-start(f32[3,3072]{1,0:T(4,128)} %load_ref.1) | copy-start | bytes 110596
  1.9 2.9 %copy-start.6 = (f32[3072]{0:T(1024)S(1)}, f32[3072]{0:T(1024)}, u32[]{:S(2)}) copy-start(f32[3072]{0:T(1024)} %param.19) | copy-start | bytes 36868
  1.9 2.9 %copy-start.9 = (f32[3,256]{1,0:T(4,128)S(1)}, f32[3,256]{1,0:T(4,128)}, u32[]{:S(2)}) copy-start(f32[3,256]{1,0:T(4,128)} %normal_ref.1) | copy-start | bytes 9220
  1.9 4.2 %copy-start = (f32[8,32,512]{2,1,0:T(8,128)S(1)}, f32[8,32,512]{2,1,0:T(8,128)}, u32[]{:S(2)}) copy-start(f32[8,32,512]{2,1,0:T(8,128)} %fs_ref.3) | copy-start | bytes 1572868
  2.0 2.9 %copy-start.8 = (f32[4,256]{1,0:T(4,128)S(1)}, f32[4,256]{1,0:T(4,128)}, u32[]{:S(2)}) copy-start(f32[4,256]{1,0:T(4,128)} %tw_ref.1) | copy-start | bytes 12292
  2.0 2.9 %copy-start.7 = (s32[4,256]{1,0:T(4,128)S(1)}, s32[4,256]{1,0:T(4,128)}, u32[]{:S(2)}) copy-start(s32[4,256]{1,0:T(4,128)} %face_ref.1) | copy-start | bytes 12292
  2.0 4.1 %collective-permute-start = (f32[2,3,32,128]{3,2,1,0:T(8,128)S(1)}, f32[2,3,32,128]{3,2,1,0:T(8,128)S(1)}, u32[]{:S(2)}, u32[]{:S(2)}) collective-permute-start(f32[2,3,32,128]{3,2,1,0:T(8,128)S(1)} %get-tuple-element.69), channel_id=1, source_target_pairs={{0,4},{4,0},{8,12},{12,8},{16,20},{20,16},{24,28},{28,24},{32,36},... | collective-permute-start | bytes 294920 | tf_op jit(solution)/shard_map/ppermute | solution.py:604
  4.1 2.0 %collective-permute-start.1 = (f32[2,3,32,128]{3,2,1,0:T(8,128)S(1)}, f32[2,3,32,128]{3,2,1,0:T(8,128)S(1)}, u32[]{:S(2)}, u32[]{:S(2)}) collective-permute-start(f32[2,3,32,128]{3,2,1,0:T(8,128)S(1)} %get-tuple-element.68), channel_id=1, source_target_pairs={{4,8},{12,16},{20,24},{28,32},{36,40},{44,48},{52,56},{60,64},{68,... | collective-permute-start | bytes 294920 | tf_op jit(solution)/shard_map/ppermute | solution.py:604
  4.9 1.3 copy-start.4
  4.9 1.3 copy-start.5
  7.0 3.1 %collective-permute-start.2 = (f32[320,128]{1,0:T(8,128)S(1)}, f32[320,128]{1,0:T(8,128)S(1)}, u32[]{:S(2)}, u32[]{:S(2)}) collective-permute-start(f32[320,128]{1,0:T(8,128)S(1)} %pad_maximum_fusion.6), channel_id=1, source_target_pairs={{0,1},{1,0},{2,3},{3,2},{4,5},{5,4},{6,7},{7,6},{8,9},{9,8},{10,11... | collective-permute-start | bytes 491528 | tf_op jit(solution)/shard_map/ppermute | solution.py:35
  10.2 10.0 %collective-permute-start.3 = (f32[448,128]{1,0:T(8,128)S(1)}, f32[448,128]{1,0:T(8,128)S(1)}, u32[]{:S(2)}, u32[]{:S(2)}) collective-permute-start(f32[448,128]{1,0:T(8,128)S(1)} %pad_maximum_fusion.3), channel_id=1, source_target_pairs={{0,2},{1,3},{2,0},{3,1},{4,6},{5,7},{6,4},{7,5},{8,10},{9,11},{10,... | collective-permute-start | bytes 688136 | tf_op jit(solution)/shard_map/ppermute | solution.py:35
  21.5 1.3 copy-start.17
  21.5 5.2 %collective-permute-start.4 = (f32[4,256]{1,0:T(4,128)S(1)}, f32[4,256]{1,0:T(4,128)S(1)}, u32[]{:S(2)}, u32[]{:S(2)}) collective-permute-start(f32[4,256]{1,0:T(4,128)S(1)} %pad_maximum_fusion.11), channel_id=1, source_target_pairs={{4,0},{8,4},{12,8},{16,12},{20,16},{24,20},{28,24},{32,28},{36,32}... | collective-permute-start | bytes 12296 | tf_op jit(solution)/shard_map/ppermute | solution.py:39
  26.7 0.8 copy-start.10
  29.7 5.2 %collective-permute-start.5 = (f32[3,56,256]{2,0,1:T(4,128)S(1)}, f32[3,56,256]{2,0,1:T(4,128)S(1)}, u32[]{:S(2)}, u32[]{:S(2)}) collective-permute-start(f32[3,56,256]{2,0,1:T(4,128)S(1)} %copy.41), channel_id=1, source_target_pairs={{0,1},{1,0},{2,3},{3,2},{4,5},{5,4},{6,7},{7,6},{8,9},{9,8},{10,11... | collective-permute-start | bytes 516104 | tf_op jit(solution)/shard_map/ppermute | solution.py:35
  35.0 8.4 %collective-permute-start.6 = (f32[3,56,256]{2,0,1:T(4,128)S(1)}, f32[3,56,256]{2,0,1:T(4,128)S(1)}, u32[]{:S(2)}, u32[]{:S(2)}) collective-permute-start(f32[3,56,256]{2,0,1:T(4,128)S(1)} %copy_add_fusion.1), channel_id=1, source_target_pairs={{0,2},{1,3},{2,0},{3,1},{4,6},{5,7},{6,4},{7,5},{8,10},{9,11},{10,... | collective-permute-start | bytes 516104 | tf_op jit(solution)/shard_map/ppermute | solution.py:35
  38.0 5.0 %collective-permute-start.7 = (f32[3,256]{1,0:T(4,128)S(1)}, f32[3,256]{1,0:T(4,128)S(1)}, u32[]{:S(2)}, u32[]{:S(2)}) collective-permute-start(f32[3,256]{1,0:T(4,128)S(1)} %get-tuple-element.91), channel_id=1, source_target_pairs={{0,4},{1,7},{2,6},{3,5},{4,0},{5,3},{6,2},{7,1},{8,12},{9,15},{10,... | collective-permute-start | bytes 9224 | tf_op jit(solution)/shard_map/ppermute | solution.py:602
  41.5 1.5 %collective-permute-start.8 = (f32[3,256]{1,0:T(4,128)S(1)}, f32[3,256]{1,0:T(4,128)S(1)}, u32[]{:S(2)}, u32[]{:S(2)}) collective-permute-start(f32[3,256]{1,0:T(4,128)S(1)} %get-tuple-element.90), channel_id=1, source_target_pairs={{4,8},{5,11},{6,10},{7,9},{12,16},{13,19},{14,18},{15,17},{20,24},... | collective-permute-start | bytes 9224 | tf_op jit(solution)/shard_map/ppermute | solution.py:602
  43.4 2.1 %collective-permute-start.9 = (f32[2,3,256]{2,1,0:T(4,128)S(1)}, f32[2,3,256]{2,1,0:T(4,128)S(1)}, u32[]{:S(2)}, u32[]{:S(2)}) collective-permute-start(f32[2,3,256]{2,1,0:T(4,128)S(1)} %pad_maximum_fusion.9), channel_id=1, source_target_pairs={{0,1},{1,0},{2,3},{3,2},{4,5},{5,4},{6,7},{7,6},{8,9},{9,8},{10,11... | collective-permute-start | bytes 18440 | tf_op jit(solution)/shard_map/ppermute | solution.py:35
  45.6 23.3 %copy-start.12 = (f32[2,3,32,512]{3,2,1,0:T(8,128)S(1)}, f32[2,3,32,512]{3,2,1,0:T(8,128)}, u32[]{:S(2)}) copy-start(f32[2,3,32,512]{3,2,1,0:T(8,128)} %get-tuple-element.40) | copy-start | bytes 1179652
  48.8 20.0 %copy-start.11 = (f32[2,3,32,512]{3,2,1,0:T(8,128)S(1)}, f32[2,3,32,512]{3,2,1,0:T(8,128)}, u32[]{:S(2)}) copy-start(f32[2,3,32,512]{3,2,1,0:T(8,128)} %get-tuple-element.41) | copy-start | bytes 1179652
  48.8 31.0 %all-to-all-start = ((f32[128,4,128]{2,1,0:T(4,128)}), f32[128,4,128]{2,1,0:T(4,128)S(1)}, u32[]{:S(2)}, u32[]{:S(2)}) async-start(f32[128,4,128]{2,1,0:T(4,128)} %bitcast.17), calls=%async_computation | async-start | bytes 524288 | tf_op jit(solution)/shard_map/all_to_all | solution.py:631
  69.8 15.6 %collective-permute-start.11 = (f32[2,3,32,512]{3,2,1,0:T(8,128)}, f32[2,3,32,512]{3,2,1,0:T(8,128)S(1)}, u32[]{:S(2)}, u32[]{:S(2)}) collective-permute-start(f32[2,3,32,512]{3,2,1,0:T(8,128)} %get-tuple-element.67), channel_id=1, source_target_pairs={{0,4},{4,0},{8,12},{12,8},{16,20},{20,16},{24,28},{28,24},{32,36},... | collective-permute-start | bytes 1179656 | tf_op jit(solution)/shard_map/ppermute | solution.py:604
  71.2 14.2 %collective-permute-start.12 = (f32[2,3,32,512]{3,2,1,0:T(8,128)}, f32[2,3,32,512]{3,2,1,0:T(8,128)S(1)}, u32[]{:S(2)}, u32[]{:S(2)}) collective-permute-start(f32[2,3,32,512]{3,2,1,0:T(8,128)} %get-tuple-element.66), channel_id=1, source_target_pairs={{4,8},{12,16},{20,24},{28,32},{36,40},{44,48},{52,56},{60,64},{68,... | collective-permute-start | bytes 1179656 | tf_op jit(solution)/shard_map/ppermute | solution.py:604
  81.0 4.4 %collective-permute-start.10 = (f32[3,256]{1,0:T(4,128)S(1)}, f32[3,256]{1,0:T(4,128)S(1)}, u32[]{:S(2)}, u32[]{:S(2)}) collective-permute-start(f32[3,256]{1,0:T(4,128)S(1)} %bitcast.69), channel_id=1, source_target_pairs={{4,0},{8,4},{12,8},{16,12},{20,16},{24,20},{28,24},{32,28},{36,32}... | collective-permute-start | bytes 9224 | tf_op jit(solution)/shard_map/ppermute | solution.py:39
  87.6 5.3 %collective-permute-start.13 = (f32[3,56,256]{2,0,1:T(4,128)S(1)}, f32[3,56,256]{2,0,1:T(4,128)S(1)}, u32[]{:S(2)}, u32[]{:S(2)}) collective-permute-start(f32[3,56,256]{2,0,1:T(4,128)S(1)} %copy.45), channel_id=1, source_target_pairs={{0,1},{1,0},{2,3},{3,2},{4,5},{5,4},{6,7},{7,6},{8,9},{9,8},{10,11... | collective-permute-start | bytes 516104 | tf_op jit(solution)/shard_map/ppermute | solution.py:35
  92.9 4.1 %copy-start.13 = (f32[1,8,4,512]{3,2,1,0:T(4,128)S(1)}, f32[1,8,4,512]{3,2,1,0:T(4,128)}, u32[]{:S(2)}) copy-start(f32[1,8,4,512]{3,2,1,0:T(4,128)} %get-tuple-element.72) | copy-start | bytes 196612
  92.9 4.1 %copy-start.14 = (f32[1,8,4,512]{3,2,1,0:T(4,128)S(1)}, f32[1,8,4,512]{3,2,1,0:T(4,128)}, u32[]{:S(2)}) copy-start(f32[1,8,4,512]{3,2,1,0:T(4,128)} %get-tuple-element.73) | copy-start | bytes 196612
  92.9 4.1 %copy-start.15 = (f32[1,8,4,512]{3,2,1,0:T(4,128)S(1)}, f32[1,8,4,512]{3,2,1,0:T(4,128)}, u32[]{:S(2)}) copy-start(f32[1,8,4,512]{3,2,1,0:T(4,128)} %get-tuple-element.100) | copy-start | bytes 196612
  92.9 4.1 %copy-start.16 = (f32[1,8,4,512]{3,2,1,0:T(4,128)S(1)}, f32[1,8,4,512]{3,2,1,0:T(4,128)}, u32[]{:S(2)}) copy-start(f32[1,8,4,512]{3,2,1,0:T(4,128)} %get-tuple-element.101) | copy-start | bytes 196612
  93.0 8.6 %collective-permute-start.14 = (f32[3,56,256]{2,0,1:T(4,128)S(1)}, f32[3,56,256]{2,0,1:T(4,128)S(1)}, u32[]{:S(2)}, u32[]{:S(2)}) collective-permute-start(f32[3,56,256]{2,0,1:T(4,128)S(1)} %copy_add_fusion), channel_id=1, source_target_pairs={{0,2},{1,3},{2,0},{3,1},{4,6},{5,7},{6,4},{7,5},{8,10},{9,11},{10,... | collective-permute-start | bytes 516104 | tf_op jit(solution)/shard_map/ppermute | solution.py:35
  94.1 5.0 %collective-permute-start.15 = (f32[3,256]{1,0:T(4,128)S(1)}, f32[3,256]{1,0:T(4,128)S(1)}, u32[]{:S(2)}, u32[]{:S(2)}) collective-permute-start(f32[3,256]{1,0:T(4,128)S(1)} %get-tuple-element.89), channel_id=1, source_target_pairs={{0,4},{1,7},{2,6},{3,5},{4,0},{5,3},{6,2},{7,1},{8,12},{9,15},{10,... | collective-permute-start | bytes 9224 | tf_op jit(solution)/shard_map/ppermute | solution.py:602
  96.3 2.7 %collective-permute-start.16 = (f32[3,256]{1,0:T(4,128)S(1)}, f32[3,256]{1,0:T(4,128)S(1)}, u32[]{:S(2)}, u32[]{:S(2)}) collective-permute-start(f32[3,256]{1,0:T(4,128)S(1)} %get-tuple-element.88), channel_id=1, source_target_pairs={{4,8},{5,11},{6,10},{7,9},{12,16},{13,19},{14,18},{15,17},{20,24},... | collective-permute-start | bytes 9224 | tf_op jit(solution)/shard_map/ppermute | solution.py:602
  101.7 2.1 %collective-permute-start.17 = (f32[2,3,256]{2,1,0:T(4,128)S(1)}, f32[2,3,256]{2,1,0:T(4,128)S(1)}, u32[]{:S(2)}, u32[]{:S(2)}) collective-permute-start(f32[2,3,256]{2,1,0:T(4,128)S(1)} %pad_maximum_fusion.10), channel_id=1, source_target_pairs={{0,1},{1,0},{2,3},{3,2},{4,5},{5,4},{6,7},{7,6},{8,9},{9,8},{10,11... | collective-permute-start | bytes 18440 | tf_op jit(solution)/shard_map/ppermute | solution.py:35
  103.8 5.6 %collective-permute-start.18 = (f32[2,14,4,512]{3,2,1,0:T(4,128)S(1)}, f32[2,14,4,512]{3,2,1,0:T(4,128)S(1)}, u32[]{:S(2)}, u32[]{:S(2)}) collective-permute-start(f32[2,14,4,512]{3,2,1,0:T(4,128)S(1)} %get-tuple-element.55), channel_id=1, source_target_pairs={{0,1},{1,0},{2,3},{3,2},{4,5},{5,4},{6,7},{7,6},{8,9},{9,8},{10,11... | collective-permute-start | bytes 688136 | tf_op jit(solution)/shard_map/ppermute | solution.py:35
  104.3 8.8 %collective-permute-start.19 = (f32[2,14,4,512]{3,2,1,0:T(4,128)S(1)}, f32[2,14,4,512]{3,2,1,0:T(4,128)S(1)}, u32[]{:S(2)}, u32[]{:S(2)}) collective-permute-start(f32[2,14,4,512]{3,2,1,0:T(4,128)S(1)} %get-tuple-element.56), channel_id=1, source_target_pairs={{1,2},{2,1},{5,6},{6,5},{9,10},{10,9},{13,14},{14,13},{17,18},{18,... | collective-permute-start | bytes 688136 | tf_op jit(solution)/shard_map/ppermute | solution.py:679
  113.1 20.8 %all-to-all-start.1 = ((f32[128,1,128]{2,1,0:T(1,128)}), f32[128,1,128]{2,1,0:T(1,128)S(1)}, u32[]{:S(2)}, u32[]{:S(2)}) async-start(f32[128,1,128]{2,1,0:T(1,128)} %bitcast.28), calls=%async_computation.1 | async-start | bytes 131072 | tf_op jit(solution)/shard_map/all_to_all | solution.py:631

commit v6 on v5

--- a/solution.py
+++ b/solution.py
@@ -277,7 +277,8 @@
         hf, lf = source_of(v_ref, seg_ref, pick_ref)
         hw, lw = source_of(w_ref, seg_ref, pick_ref)
         table = jnp.concatenate([hf, lf, hw, lw], axis=0)
-        n256 = lax.broadcasted_iota(jnp.int32, (256, 128), 0)
+        n256 = lax.broadcasted_iota(jnp.int32, (256, 128), 0).astype(F32).astype(BF)
+        unit, none = jnp.ones((256, 128), BF), jnp.zeros((256, 128), BF)
         n8 = lax.broadcasted_iota(jnp.int32, (8, 128), 0)
         for x in range(8):
             tf = jnp.zeros((8, 128), F32)
@@ -285,7 +286,7 @@
             for k in range(4):
                 row = k * 8 + x
                 node = pick_ref[row : row + 1, :].astype(jnp.int32)
-                oh = (n256 == (node & 255)).astype(F32).astype(BF)
+                oh = jnp.where(n256 == (node & 255).astype(F32).astype(BF), unit, none)
                 r = jnp.dot(table, oh, preferred_element_type=F32)
                 u = jnp.where(n8 == (node >> 8), pick_ref[32 + row : 33 + row, :], 0.0)
                 tf = tf + (r[0:8] + r[8:16]) * u
@@ -392,14 +393,16 @@
     wall = pltpu.roll(wall16, 13, 0)[0:8]
     hi, lo = split(wall)
     table = jnp.concatenate([hi, lo], axis=0)
-    i128 = lax.broadcasted_iota(jnp.int32, (128, 256), 0)
+    b128 = lax.broadcasted_iota(jnp.int32, (128, 256), 0).astype(F32).astype(BF)
+    one, nil = jnp.ones((128, 256), BF), jnp.zeros((128, 256), BF)
     i8 = lax.broadcasted_iota(jnp.int32, (8, 256), 0)
     f_ref[...] = load_ref[...]
     for g in range(4):
         total = jnp.zeros((8, 256), F32)
         for k in range(4):
             face = seg_ref[g, k : k + 1, :].astype(jnp.int32)
-            oh = (i128 == ((face >> 8) * 32 + (face & 31))).astype(F32).astype(BF)
+            lane = (face >> 8) * 32 + (face & 31)
+            oh = jnp.where(b128 == lane.astype(F32).astype(BF), one, nil)
             r = jnp.dot(table, oh, preferred_element_type=F32)
             w = jnp.where(i8 == ((face >> 5) & 7), seg_ref[g, 4 + k : 5 + k, :], 0.0)
             total = total + (r[:8] + r[8:]) * w

time: 133 us -> 134 us (level); the launches traced: 135 us -> 133 us
  starting transfers between devices: 69 us -> 60.7 us
  Pallas kernels: 19.3 us -> 24.4 us
  waiting for transfers between devices: 38.1 us -> 39.6 us
    ppermute x9, starting transfers between devices: 20.4 us -> 13.8 us  [swap(): return lax.ppermute(x, AXES, [(i, i ^ mask) for i in range(N_DEV)])]
    pallas_call x2, Pallas kernels: 4.19 us -> 8.1 us  [stiff_apply(): pl.pallas_call(apply_body, out_shape=jax.ShapeDtypeStruct((3, VR, 256), F...]
    ppermute x9, waiting for transfers between devices: 13 us -> 15.6 us  [swap(): return lax.ppermute(x, AXES, [(i, i ^ mask) for i in range(N_DEV)])]
    all_to_all x2, starting transfers between devices: 31.4 us -> 29.6 us  [to_all(): return lax.all_to_all(x, AXES, 0, 0, tiled=True)]
    pallas_call x2, Pallas kernels: 5.69 us -> 7.14 us  [settle(): pl.pallas_call(functools.partial(settle_body, first=first), out_shape=tup...]
  transfers between devices with their start and end apart: 22 -> 22, of which waited for: 16 -> 16; matrix products, arithmetic and copies ran while one was open for 3% -> 3% of each run, Pallas kernels for 7% -> 8%
where the time goes in v6:
time: 134 us; the launch traced here: 133 us
  starting transfers between devices  60.7 us (45%)
  waiting for transfers between devices  39.6 us (30%)
  Pallas kernels  24.4 us (18%)
  local copies, waits for them, and re-layouts  3.42 us (3%)
  other arithmetic  3.02 us (2%)
  between operations  1.97 us (1%)
    all_to_all x2, starting transfers between devices, to_all(): return lax.all_to_all(x, AXES, 0, 0, tiled=True)  29.6 us
    ppermute x9, waiting for transfers between devices, swap(): return lax.ppermute(x, AXES, [(i, i ^ mask) for i in range(N_DEV)])  15.6 us
    ppermute x9, starting transfers between devices, swap(): return lax.ppermute(x, AXES, [(i, i ^ mask) for i in range(N_DEV)])  13.8 us
    all_to_all x2, waiting for transfers between devices, to_all(): return lax.all_to_all(x, AXES, 0, 0, tiled=True)  11.7 us
    pallas_call x2, Pallas kernels, stiff_apply(): pl.pallas_call(apply_body, out_shape=jax.ShapeDtypeStruct((3, VR, 256), F...  8.1 us
    ppermute x4, starting transfers between devices, beside(): got.append(lax.ppermute(send, AXES, both_ends))  8 us
    pallas_call x2, Pallas kernels, settle(): pl.pallas_call(functools.partial(settle_body, first=first), out_shape=tup...  7.14 us
    ppermute x2, waiting for transfers between devices, from_gx(): lax.ppermute(x, 'gx', [(i, i + by) for i in range(N_GX) if 0 <= i + by <...  5.98 us
  transfers between devices with their start and end apart: 22, of which 16 were waited for; matrix products, arithmetic and copies ran while one was open for 3% of the time, Pallas kernels for 8%

profile of v6, /device:TPU:1, one launch (start us, length us, event | category | flops | bytes accessed | tf_op | source)
XLA Modules:
  0.0 133.2 jit_solution(7101125552526388447)
XLA Ops:
  0.7 1.1 slice_bitcast_fusion.1
  2.0 2.1 %collective-permute-start = (f32[2,3,32,128]{3,2,1,0:T(8,128)S(1)}, f32[2,3,32,128]{3,2,1,0:T(8,128)S(1)}, u32[]{:S(2)}, u32[]{:S(2)}) collective-permute-start(f32[2,3,32,128]{3,2,1,0:T(8,128)S(1)} %get-tuple-element.69), channel_id=1, source_target_pairs={{0,4},{4,0},{8,12},{12,8},{16,20},{20,16},{24,28},{28,24},{32,36},... | collective-permute-start | bytes 294920 | tf_op jit(solution)/shard_map/ppermute | solution.py:607
  4.1 0.7 collective-permute-start.1
  5.1 1.1 collective-permute-done.xa_ref
  6.2 0.8 shard_map.140
  7.0 2.1 %collective-permute-start.2 = (f32[320,128]{1,0:T(8,128)S(1)}, f32[320,128]{1,0:T(8,128)S(1)}, u32[]{:S(2)}, u32[]{:S(2)}) collective-permute-start(f32[320,128]{1,0:T(8,128)S(1)} %pad_maximum_fusion.6), channel_id=1, source_target_pairs={{0,1},{1,0},{2,3},{3,2},{4,5},{5,4},{6,7},{7,6},{8,9},{9,8},{10,11... | collective-permute-start | bytes 491528 | tf_op jit(solution)/shard_map/ppermute | solution.py:35
  9.1 1.0 collective-permute-done.2
  10.2 3.1 %collective-permute-start.3 = (f32[448,128]{1,0:T(8,128)S(1)}, f32[448,128]{1,0:T(8,128)S(1)}, u32[]{:S(2)}, u32[]{:S(2)}) collective-permute-start(f32[448,128]{1,0:T(8,128)S(1)} %pad_maximum_fusion.3), channel_id=1, source_target_pairs={{0,2},{1,3},{2,0},{3,1},{4,6},{5,7},{6,4},{7,5},{8,10},{9,11},{10,... | collective-permute-start | bytes 688136 | tf_op jit(solution)/shard_map/ppermute | solution.py:35
  13.2 0.7 slice_bitcast_fusion.8
  13.9 6.2 %collective-permute-done.3 = f32[448,128]{1,0:T(8,128)S(1)} collective-permute-done((f32[448,128]{1,0:T(8,128)S(1)}, f32[448,128]{1,0:T(8,128)S(1)}, u32[]{:S(2)}, u32[]{:S(2)}) %collective-permute-start.3) | collective-permute-done | bytes 229408 | tf_op jit(solution)/shard_map/ppermute | solution.py:35
  20.5 0.9 shard_map.142
  21.4 1.3 collective-permute-start.4
  23.4 3.2 %collective-permute-done.4 = f32[4,256]{1,0:T(4,128)S(1)} collective-permute-done((f32[4,256]{1,0:T(4,128)S(1)}, f32[4,256]{1,0:T(4,128)S(1)}, u32[]{:S(2)}, u32[]{:S(2)}) %collective-permute-start.4) | collective-permute-done | bytes 4128 | tf_op jit(solution)/shard_map/ppermute | solution.py:39
  26.7 0.7 copy-done.10
  27.4 4.0 %shard_map.143 = f32[3,56,256]{2,1,0:T(8,128)S(1)} custom-call(s32[1]{0:T(128)S(6)} %copy.59.live_ref.refs_1_, f32[3,56,256]{2,1,0:T(8,128)S(1)} %broadcast_select_fusion.8.v_ref.refs_6_, s32[27,384]{1,0:T(8,128)S(1)} %copy-done.10, f32[1,384]{1,0:T(1,128)S(1)} %reshape.42.coef_ref.refs_8_, f32[81,81]{1,0:T(8,128)S(1)} %copy-done.2), custom_call_target="tpu_custom_call" | custom-call | flops 6000000000 | bytes 24000000 | tf_op jit(solution)/shard_map/pallas_call | solution.py:151
  31.5 2.1 %collective-permute-start.5 = (f32[3,56,256]{2,0,1:T(4,128)S(1)}, f32[3,56,256]{2,0,1:T(4,128)S(1)}, u32[]{:S(2)}, u32[]{:S(2)}) collective-permute-start(f32[3,56,256]{2,0,1:T(4,128)S(1)} %copy.41), channel_id=1, source_target_pairs={{0,1},{1,0},{2,3},{3,2},{4,5},{5,4},{6,7},{7,6},{8,9},{9,8},{10,11... | collective-permute-start | bytes 516104 | tf_op jit(solution)/shard_map/ppermute | solution.py:35
  33.7 0.9 pad_maximum_fusion
  34.9 1.1 collective-permute-start.6
  36.0 3.5 %collective-permute-start.7 = (f32[3,256]{1,0:T(4,128)S(1)}, f32[3,256]{1,0:T(4,128)S(1)}, u32[]{:S(2)}, u32[]{:S(2)}) collective-permute-start(f32[3,256]{1,0:T(4,128)S(1)} %get-tuple-element.91), channel_id=1, source_target_pairs={{0,4},{1,7},{2,6},{3,5},{4,0},{5,3},{6,2},{7,1},{8,12},{9,15},{10,... | collective-permute-start | bytes 9224 | tf_op jit(solution)/shard_map/ppermute | solution.py:605
  39.5 0.6 collective-permute-start.8
  40.2 0.7 collective-permute-done.7
  40.9 2.4 %collective-permute-done.6 = f32[3,56,256]{2,0,1:T(4,128)S(1)} collective-permute-done((f32[3,56,256]{2,0,1:T(4,128)S(1)}, f32[3,56,256]{2,0,1:T(4,128)S(1)}, u32[]{:S(2)}, u32[]{:S(2)}) %collective-permute-start.6) | collective-permute-done | bytes 172064 | tf_op jit(solution)/shard_map/ppermute | solution.py:35
  43.4 1.3 collective-permute-start.9
  44.7 0.7 collective-permute-done.9
  45.5 3.8 %shard_map.144 = (f32[3,56,256]{2,1,0:T(8,128)S(1)}, f32[512,128]{1,0:T(8,128)}, f32[16,128]{1,0:T(8,128)S(1)}) custom-call(s32[2]{0:T(128)S(1)} %pad_add_fusion.at_ref.refs_0_, s32[1]{0:T(128)S(6)} %copy.59.live_ref.refs_1_, f32[3,56,256]{2,1,0:T(8,128)S(1)} %copy.42.refs_2_, f32[3,56,256]{2,1,0:T(8,128)S(1)} %copy.43.refs_3_, ...), custom_call_target="tpu_custom_call" | custom-call | flops 6000000000 | bytes 24000000 | tf_op jit(solution)/shard_map/pallas_call | solution.py:347
  49.3 18.5 %all-to-all-start = ((f32[128,4,128]{2,1,0:T(4,128)}), f32[128,4,128]{2,1,0:T(4,128)S(1)}, u32[]{:S(2)}, u32[]{:S(2)}) async-start(f32[128,4,128]{2,1,0:T(4,128)} %bitcast.17), calls=%async_computation | async-start | bytes 524288 | tf_op jit(solution)/shard_map/all_to_all | solution.py:634
  67.8 1.0 broadcast_select_fusion.3
  68.8 1.4 %collective-permute-start.11 = (f32[2,3,32,512]{3,2,1,0:T(8,128)}, f32[2,3,32,512]{3,2,1,0:T(8,128)S(1)}, u32[]{:S(2)}, u32[]{:S(2)}) collective-permute-start(f32[2,3,32,512]{3,2,1,0:T(8,128)} %get-tuple-element.67), channel_id=1, source_target_pairs={{0,4},{4,0},{8,12},{12,8},{16,20},{20,16},{24,28},{28,24},{32,36},... | collective-permute-start | bytes 1179656 | tf_op jit(solution)/shard_map/ppermute | solution.py:607
  70.2 0.7 collective-permute-start.12
  70.9 7.9 %all-to-all-done = f32[128,4,128]{2,1,0:T(4,128)S(1)} async-done(((f32[128,4,128]{2,1,0:T(4,128)}), f32[128,4,128]{2,1,0:T(4,128)S(1)}, u32[]{:S(2)}, u32[]{:S(2)}) %all-to-all-start) | async-done | bytes 262176 | tf_op jit(solution)/shard_map/all_to_all | solution.py:634
  78.8 1.0 shard_map.145
  79.8 1.3 collective-permute-start.10
  81.4 2.8 %collective-permute-done.10 = f32[3,256]{1,0:T(4,128)S(1)} collective-permute-done((f32[3,256]{1,0:T(4,128)S(1)}, f32[3,256]{1,0:T(4,128)S(1)}, u32[]{:S(2)}, u32[]{:S(2)}) %collective-permute-start.10) | collective-permute-done | bytes 3104 | tf_op jit(solution)/shard_map/ppermute | solution.py:39
  84.3 4.0 %shard_map.146 = f32[3,56,256]{2,1,0:T(8,128)S(1)} custom-call(s32[1]{0:T(128)S(6)} %copy.59.live_ref.refs_1_, f32[3,56,256]{2,1,0:T(8,128)S(1)} %broadcast_select_fusion.7.v_ref.refs_6_, s32[27,384]{1,0:T(8,128)S(1)} %copy-done.10, f32[1,384]{1,0:T(1,128)S(1)} %reshape.42.coef_ref.refs_8_, f32[81,81]{1,0:T(8,128)S(1)} %copy-done.2), custom_call_target="tpu_custom_call" | custom-call | flops 6000000000 | bytes 24000000 | tf_op jit(solution)/shard_map/pallas_call | solution.py:151
  88.4 2.2 %collective-permute-start.13 = (f32[3,56,256]{2,0,1:T(4,128)S(1)}, f32[3,56,256]{2,0,1:T(4,128)S(1)}, u32[]{:S(2)}, u32[]{:S(2)}) collective-permute-start(f32[3,56,256]{2,0,1:T(4,128)S(1)} %copy.45), channel_id=1, source_target_pairs={{0,1},{1,0},{2,3},{3,2},{4,5},{5,4},{6,7},{7,6},{8,9},{9,8},{10,11... | collective-permute-start | bytes 516104 | tf_op jit(solution)/shard_map/ppermute | solution.py:35
  90.8 1.0 collective-permute-done.13
  92.0 3.2 %collective-permute-start.15 = (f32[3,256]{1,0:T(4,128)S(1)}, f32[3,256]{1,0:T(4,128)S(1)}, u32[]{:S(2)}, u32[]{:S(2)}) collective-permute-start(f32[3,256]{1,0:T(4,128)S(1)} %get-tuple-element.89), channel_id=1, source_target_pairs={{0,4},{1,7},{2,6},{3,5},{4,0},{5,3},{6,2},{7,1},{8,12},{9,15},{10,... | collective-permute-start | bytes 9224 | tf_op jit(solution)/shard_map/ppermute | solution.py:605
  96.0 1.0 collective-permute-done.15
  97.0 3.3 %collective-permute-done.14 = f32[3,56,256]{2,0,1:T(4,128)S(1)} collective-permute-done((f32[3,56,256]{2,0,1:T(4,128)S(1)}, f32[3,56,256]{2,0,1:T(4,128)S(1)}, u32[]{:S(2)}, u32[]{:S(2)}) %collective-permute-start.14) | collective-permute-done | bytes 172064 | tf_op jit(solution)/shard_map/ppermute | solution.py:35
  100.3 1.5 %collective-permute-start.17 = (f32[2,3,256]{2,1,0:T(4,128)S(1)}, f32[2,3,256]{2,1,0:T(4,128)S(1)}, u32[]{:S(2)}, u32[]{:S(2)}) collective-permute-start(f32[2,3,256]{2,1,0:T(4,128)S(1)} %pad_maximum_fusion.10), channel_id=1, source_target_pairs={{0,1},{1,0},{2,3},{3,2},{4,5},{5,4},{6,7},{7,6},{8,9},{9,8},{10,11... | collective-permute-start | bytes 18440 | tf_op jit(solution)/shard_map/ppermute | solution.py:35
  101.9 0.8 collective-permute-done.17
  103.1 2.0 %collective-permute-start.19 = (f32[2,14,4,512]{3,2,1,0:T(4,128)S(1)}, f32[2,14,4,512]{3,2,1,0:T(4,128)S(1)}, u32[]{:S(2)}, u32[]{:S(2)}) collective-permute-start(f32[2,14,4,512]{3,2,1,0:T(4,128)S(1)} %get-tuple-element.56), channel_id=1, source_target_pairs={{1,2},{2,1},{5,6},{6,5},{9,10},{10,9},{13,14},{14,13},{17,18},{18,... | collective-permute-start | bytes 688136 | tf_op jit(solution)/shard_map/ppermute | solution.py:682
  105.1 3.4 %shard_map.147 = (f32[3,56,256]{2,1,0:T(8,128)S(1)}, f32[128,128]{1,0:T(8,128)}) custom-call(s32[2]{0:T(128)S(1)} %pad_add_fusion.at_ref.refs_0_, s32[1]{0:T(128)S(6)} %copy.59.live_ref.refs_1_, f32[3,56,256]{2,1,0:T(8,128)S(1)} %copy.46.refs_2_, f32[3,56,256]{2,1,0:T(8,128)S(1)} %copy.47.refs_3_, f32[2,3,256]{2,1,0:T(4,128)S(1)} %fusion.4.refs_4_, ...), custom_call_target="tpu_custom_call" | custom-call | flops 6000000000 | bytes 24000000 | tf_op jit(solution)/shard_map/pallas_call | solution.py:347
  108.4 3.5 %collective-permute-done.19.mid_ref = f32[2,14,4,512]{3,2,1,0:T(4,128)S(1)} collective-permute-done((f32[2,14,4,512]{3,2,1,0:T(4,128)S(1)}, f32[2,14,4,512]{3,2,1,0:T(4,128)S(1)}, u32[]{:S(2)}, u32[]{:S(2)}) %collective-permute-start.19) | collective-permute-done | bytes 229408 | tf_op jit(solution)/shard_map/ppermute | solution.py:682
  111.9 11.0 %all-to-all-start.1 = ((f32[128,1,128]{2,1,0:T(1,128)}), f32[128,1,128]{2,1,0:T(1,128)S(1)}, u32[]{:S(2)}, u32[]{:S(2)}) async-start(f32[128,1,128]{2,1,0:T(1,128)} %bitcast.28), calls=%async_computation.1 | async-start | bytes 131072 | tf_op jit(solution)/shard_map/all_to_all | solution.py:634
  123.0 5.6 %shard_map.148 = f32[8,32,512]{2,1,0:T(8,128)} custom-call(s32[2]{0:T(128)S(1)} %pad_add_fusion.at_ref.refs_0_, f32[8,32,512]{2,1,0:T(8,128)S(1)} %copy-done, f32[8,32,512]{2,1,0:T(8,128)S(1)} %copy-done.1, f32[2,3,32,512]{3,2,1,0:T(8,128)S(1)} %collective-permute-done.11.xa_ref, f32[2,3,32,512]{3,2,1,0:T(8,128)S(1)} %collective-permute-done.12.xb_ref, ...), custom_call_target="tpu_custom_call" | custom-call | flops 100000000 | bytes 20000000 | tf_op jit(solution)/shard_map/pallas_call | solution.py:538
  128.6 3.8 %all-to-all-done.1 = f32[128,1,128]{2,1,0:T(1,128)S(1)} async-done(((f32[128,1,128]{2,1,0:T(1,128)}), f32[128,1,128]{2,1,0:T(1,128)S(1)}, u32[]{:S(2)}, u32[]{:S(2)}) %all-to-all-start.1) | async-done | bytes 65568 | tf_op jit(solution)/shard_map/all_to_all | solution.py:634
  132.4 0.8 shard_map.149
  (106 shorter events, 3.5 us)
Async XLA Ops:
  0.6 1.2 copy-start.1
  1.9 2.9 %copy-start.2 = (f32[81,81]{1,0:T(8,128)S(1)}, f32[81,81]{1,0:T(8,128)}, u32[]{:S(2)}) copy-start(f32[81,81]{1,0:T(8,128)} %stiff_ref.9) | copy-start | bytes 78736
  1.9 2.9 %copy-start.3 = (f32[3,3072]{1,0:T(4,128)S(1)}, f32[3,3072]{1,0:T(4,128)}, u32[]{:S(2)}) copy-start(f32[3,3072]{1,0:T(4,128)} %load_ref.1) | copy-start | bytes 110596
  1.9 2.9 %copy-start.6 = (f32[3072]{0:T(1024)S(1)}, f32[3072]{0:T(1024)}, u32[]{:S(2)}) copy-start(f32[3072]{0:T(1024)} %param.19) | copy-start | bytes 36868
  1.9 2.9 %copy-start.9 = (f32[3,256]{1,0:T(4,128)S(1)}, f32[3,256]{1,0:T(4,128)}, u32[]{:S(2)}) copy-start(f32[3,256]{1,0:T(4,128)} %normal_ref.1) | copy-start | bytes 9220
  1.9 4.2 %copy-start = (f32[8,32,512]{2,1,0:T(8,128)S(1)}, f32[8,32,512]{2,1,0:T(8,128)}, u32[]{:S(2)}) copy-start(f32[8,32,512]{2,1,0:T(8,128)} %fs_ref.3) | copy-start | bytes 1572868
  2.0 2.9 %copy-start.8 = (f32[4,256]{1,0:T(4,128)S(1)}, f32[4,256]{1,0:T(4,128)}, u32[]{:S(2)}) copy-start(f32[4,256]{1,0:T(4,128)} %tw_ref.1) | copy-start | bytes 12292
  2.0 2.9 %copy-start.7 = (s32[4,256]{1,0:T(4,128)S(1)}, s32[4,256]{1,0:T(4,128)}, u32[]{:S(2)}) copy-start(s32[4,256]{1,0:T(4,128)} %face_ref.1) | copy-start | bytes 12292
  2.0 4.1 %collective-permute-start = (f32[2,3,32,128]{3,2,1,0:T(8,128)S(1)}, f32[2,3,32,128]{3,2,1,0:T(8,128)S(1)}, u32[]{:S(2)}, u32[]{:S(2)}) collective-permute-start(f32[2,3,32,128]{3,2,1,0:T(8,128)S(1)} %get-tuple-element.69), channel_id=1, source_target_pairs={{0,4},{4,0},{8,12},{12,8},{16,20},{20,16},{24,28},{28,24},{32,36},... | collective-permute-start | bytes 294920 | tf_op jit(solution)/shard_map/ppermute | solution.py:607
  4.1 2.0 %collective-permute-start.1 = (f32[2,3,32,128]{3,2,1,0:T(8,128)S(1)}, f32[2,3,32,128]{3,2,1,0:T(8,128)S(1)}, u32[]{:S(2)}, u32[]{:S(2)}) collective-permute-start(f32[2,3,32,128]{3,2,1,0:T(8,128)S(1)} %get-tuple-element.68), channel_id=1, source_target_pairs={{4,8},{12,16},{20,24},{28,32},{36,40},{44,48},{52,56},{60,64},{68,... | collective-permute-start | bytes 294920 | tf_op jit(solution)/shard_map/ppermute | solution.py:607
  4.9 1.3 copy-start.4
  4.9 1.3 copy-start.5
  7.0 3.1 %collective-permute-start.2 = (f32[320,128]{1,0:T(8,128)S(1)}, f32[320,128]{1,0:T(8,128)S(1)}, u32[]{:S(2)}, u32[]{:S(2)}) collective-permute-start(f32[320,128]{1,0:T(8,128)S(1)} %pad_maximum_fusion.6), channel_id=1, source_target_pairs={{0,1},{1,0},{2,3},{3,2},{4,5},{5,4},{6,7},{7,6},{8,9},{9,8},{10,11... | collective-permute-start | bytes 491528 | tf_op jit(solution)/shard_map/ppermute | solution.py:35
  10.2 10.0 %collective-permute-start.3 = (f32[448,128]{1,0:T(8,128)S(1)}, f32[448,128]{1,0:T(8,128)S(1)}, u32[]{:S(2)}, u32[]{:S(2)}) collective-permute-start(f32[448,128]{1,0:T(8,128)S(1)} %pad_maximum_fusion.3), channel_id=1, source_target_pairs={{0,2},{1,3},{2,0},{3,1},{4,6},{5,7},{6,4},{7,5},{8,10},{9,11},{10,... | collective-permute-start | bytes 688136 | tf_op jit(solution)/shard_map/ppermute | solution.py:35
  21.4 1.3 %copy-start.17 = (f32[384]{0:T(512)S(1)}, f32[384]{0:T(512)}, u32[]{:S(2)}) copy-start(f32[384]{0:T(512)} %param.16) | copy-start | bytes 4612
  21.4 5.2 %collective-permute-start.4 = (f32[4,256]{1,0:T(4,128)S(1)}, f32[4,256]{1,0:T(4,128)S(1)}, u32[]{:S(2)}, u32[]{:S(2)}) collective-permute-start(f32[4,256]{1,0:T(4,128)S(1)} %pad_maximum_fusion.11), channel_id=1, source_target_pairs={{4,0},{8,4},{12,8},{16,12},{20,16},{24,20},{28,24},{32,28},{36,32}... | collective-permute-start | bytes 12296 | tf_op jit(solution)/shard_map/ppermute | solution.py:39
  26.6 0.8 copy-start.10
  31.5 3.2 %collective-permute-start.5 = (f32[3,56,256]{2,0,1:T(4,128)S(1)}, f32[3,56,256]{2,0,1:T(4,128)S(1)}, u32[]{:S(2)}, u32[]{:S(2)}) collective-permute-start(f32[3,56,256]{2,0,1:T(4,128)S(1)} %copy.41), channel_id=1, source_target_pairs={{0,1},{1,0},{2,3},{3,2},{4,5},{5,4},{6,7},{7,6},{8,9},{9,8},{10,11... | collective-permute-start | bytes 516104 | tf_op jit(solution)/shard_map/ppermute | solution.py:35
  34.9 8.4 %collective-permute-start.6 = (f32[3,56,256]{2,0,1:T(4,128)S(1)}, f32[3,56,256]{2,0,1:T(4,128)S(1)}, u32[]{:S(2)}, u32[]{:S(2)}) collective-permute-start(f32[3,56,256]{2,0,1:T(4,128)S(1)} %copy_add_fusion.1), channel_id=1, source_target_pairs={{0,2},{1,3},{2,0},{3,1},{4,6},{5,7},{6,4},{7,5},{8,10},{9,11},{10,... | collective-permute-start | bytes 516104 | tf_op jit(solution)/shard_map/ppermute | solution.py:35
  36.0 5.0 %collective-permute-start.7 = (f32[3,256]{1,0:T(4,128)S(1)}, f32[3,256]{1,0:T(4,128)S(1)}, u32[]{:S(2)}, u32[]{:S(2)}) collective-permute-start(f32[3,256]{1,0:T(4,128)S(1)} %get-tuple-element.91), channel_id=1, source_target_pairs={{0,4},{1,7},{2,6},{3,5},{4,0},{5,3},{6,2},{7,1},{8,12},{9,15},{10,... | collective-permute-start | bytes 9224 | tf_op jit(solution)/shard_map/ppermute | solution.py:605
  39.5 1.5 %collective-permute-start.8 = (f32[3,256]{1,0:T(4,128)S(1)}, f32[3,256]{1,0:T(4,128)S(1)}, u32[]{:S(2)}, u32[]{:S(2)}) collective-permute-start(f32[3,256]{1,0:T(4,128)S(1)} %get-tuple-element.90), channel_id=1, source_target_pairs={{4,8},{5,11},{6,10},{7,9},{12,16},{13,19},{14,18},{15,17},{20,24},... | collective-permute-start | bytes 9224 | tf_op jit(solution)/shard_map/ppermute | solution.py:605
  43.4 2.1 %collective-permute-start.9 = (f32[2,3,256]{2,1,0:T(4,128)S(1)}, f32[2,3,256]{2,1,0:T(4,128)S(1)}, u32[]{:S(2)}, u32[]{:S(2)}) collective-permute-start(f32[2,3,256]{2,1,0:T(4,128)S(1)} %pad_maximum_fusion.9), channel_id=1, source_target_pairs={{0,1},{1,0},{2,3},{3,2},{4,5},{5,4},{6,7},{7,6},{8,9},{9,8},{10,11... | collective-permute-start | bytes 18440 | tf_op jit(solution)/shard_map/ppermute | solution.py:35
  45.5 22.3 %copy-start.12 = (f32[2,3,32,512]{3,2,1,0:T(8,128)S(1)}, f32[2,3,32,512]{3,2,1,0:T(8,128)}, u32[]{:S(2)}) copy-start(f32[2,3,32,512]{3,2,1,0:T(8,128)} %get-tuple-element.40) | copy-start | bytes 1179652
  49.3 18.6 %copy-start.11 = (f32[2,3,32,512]{3,2,1,0:T(8,128)S(1)}, f32[2,3,32,512]{3,2,1,0:T(8,128)}, u32[]{:S(2)}) copy-start(f32[2,3,32,512]{3,2,1,0:T(8,128)} %get-tuple-element.41) | copy-start | bytes 1179652
  49.3 29.5 %all-to-all-start = ((f32[128,4,128]{2,1,0:T(4,128)}), f32[128,4,128]{2,1,0:T(4,128)S(1)}, u32[]{:S(2)}, u32[]{:S(2)}) async-start(f32[128,4,128]{2,1,0:T(4,128)} %bitcast.17), calls=%async_computation | async-start | bytes 524288 | tf_op jit(solution)/shard_map/all_to_all | solution.py:634
  68.8 15.5 %collective-permute-start.11 = (f32[2,3,32,512]{3,2,1,0:T(8,128)}, f32[2,3,32,512]{3,2,1,0:T(8,128)S(1)}, u32[]{:S(2)}, u32[]{:S(2)}) collective-permute-start(f32[2,3,32,512]{3,2,1,0:T(8,128)} %get-tuple-element.67), channel_id=1, source_target_pairs={{0,4},{4,0},{8,12},{12,8},{16,20},{20,16},{24,28},{28,24},{32,36},... | collective-permute-start | bytes 1179656 | tf_op jit(solution)/shard_map/ppermute | solution.py:607
  70.2 14.1 %collective-permute-start.12 = (f32[2,3,32,512]{3,2,1,0:T(8,128)}, f32[2,3,32,512]{3,2,1,0:T(8,128)S(1)}, u32[]{:S(2)}, u32[]{:S(2)}) collective-permute-start(f32[2,3,32,512]{3,2,1,0:T(8,128)} %get-tuple-element.66), channel_id=1, source_target_pairs={{4,8},{12,16},{20,24},{28,32},{36,40},{44,48},{52,56},{60,64},{68,... | collective-permute-start | bytes 1179656 | tf_op jit(solution)/shard_map/ppermute | solution.py:607
  79.8 4.4 %collective-permute-start.10 = (f32[3,256]{1,0:T(4,128)S(1)}, f32[3,256]{1,0:T(4,128)S(1)}, u32[]{:S(2)}, u32[]{:S(2)}) collective-permute-start(f32[3,256]{1,0:T(4,128)S(1)} %bitcast.69), channel_id=1, source_target_pairs={{4,0},{8,4},{12,8},{16,12},{20,16},{24,20},{28,24},{32,28},{36,32}... | collective-permute-start | bytes 9224 | tf_op jit(solution)/shard_map/ppermute | solution.py:39
  88.4 3.3 %collective-permute-start.13 = (f32[3,56,256]{2,0,1:T(4,128)S(1)}, f32[3,56,256]{2,0,1:T(4,128)S(1)}, u32[]{:S(2)}, u32[]{:S(2)}) collective-permute-start(f32[3,56,256]{2,0,1:T(4,128)S(1)} %copy.45), channel_id=1, source_target_pairs={{0,1},{1,0},{2,3},{3,2},{4,5},{5,4},{6,7},{7,6},{8,9},{9,8},{10,11... | collective-permute-start | bytes 516104 | tf_op jit(solution)/shard_map/ppermute | solution.py:35
  91.8 4.1 %copy-start.13 = (f32[1,8,4,512]{3,2,1,0:T(4,128)S(1)}, f32[1,8,4,512]{3,2,1,0:T(4,128)}, u32[]{:S(2)}) copy-start(f32[1,8,4,512]{3,2,1,0:T(4,128)} %get-tuple-element.72) | copy-start | bytes 196612
  91.8 4.1 %copy-start.14 = (f32[1,8,4,512]{3,2,1,0:T(4,128)S(1)}, f32[1,8,4,512]{3,2,1,0:T(4,128)}, u32[]{:S(2)}) copy-start(f32[1,8,4,512]{3,2,1,0:T(4,128)} %get-tuple-element.73) | copy-start | bytes 196612
  91.8 4.1 %copy-start.15 = (f32[1,8,4,512]{3,2,1,0:T(4,128)S(1)}, f32[1,8,4,512]{3,2,1,0:T(4,128)}, u32[]{:S(2)}) copy-start(f32[1,8,4,512]{3,2,1,0:T(4,128)} %get-tuple-element.100) | copy-start | bytes 196612
  91.8 4.1 %copy-start.16 = (f32[1,8,4,512]{3,2,1,0:T(4,128)S(1)}, f32[1,8,4,512]{3,2,1,0:T(4,128)}, u32[]{:S(2)}) copy-start(f32[1,8,4,512]{3,2,1,0:T(4,128)} %get-tuple-element.101) | copy-start | bytes 196612
  91.9 8.4 %collective-permute-start.14 = (f32[3,56,256]{2,0,1:T(4,128)S(1)}, f32[3,56,256]{2,0,1:T(4,128)S(1)}, u32[]{:S(2)}, u32[]{:S(2)}) collective-permute-start(f32[3,56,256]{2,0,1:T(4,128)S(1)} %copy_add_fusion), channel_id=1, source_target_pairs={{0,2},{1,3},{2,0},{3,1},{4,6},{5,7},{6,4},{7,5},{8,10},{9,11},{10,... | collective-permute-start | bytes 516104 | tf_op jit(solution)/shard_map/ppermute | solution.py:35
  92.0 5.0 %collective-permute-start.15 = (f32[3,256]{1,0:T(4,128)S(1)}, f32[3,256]{1,0:T(4,128)S(1)}, u32[]{:S(2)}, u32[]{:S(2)}) collective-permute-start(f32[3,256]{1,0:T(4,128)S(1)} %get-tuple-element.89), channel_id=1, source_target_pairs={{0,4},{1,7},{2,6},{3,5},{4,0},{5,3},{6,2},{7,1},{8,12},{9,15},{10,... | collective-permute-start | bytes 9224 | tf_op jit(solution)/shard_map/ppermute | solution.py:605
  95.2 1.8 %collective-permute-start.16 = (f32[3,256]{1,0:T(4,128)S(1)}, f32[3,256]{1,0:T(4,128)S(1)}, u32[]{:S(2)}, u32[]{:S(2)}) collective-permute-start(f32[3,256]{1,0:T(4,128)S(1)} %get-tuple-element.88), channel_id=1, source_target_pairs={{4,8},{5,11},{6,10},{7,9},{12,16},{13,19},{14,18},{15,17},{20,24},... | collective-permute-start | bytes 9224 | tf_op jit(solution)/shard_map/ppermute | solution.py:605
  100.3 2.3 %collective-permute-start.17 = (f32[2,3,256]{2,1,0:T(4,128)S(1)}, f32[2,3,256]{2,1,0:T(4,128)S(1)}, u32[]{:S(2)}, u32[]{:S(2)}) collective-permute-start(f32[2,3,256]{2,1,0:T(4,128)S(1)} %pad_maximum_fusion.10), channel_id=1, source_target_pairs={{0,1},{1,0},{2,3},{3,2},{4,5},{5,4},{6,7},{7,6},{8,9},{9,8},{10,11... | collective-permute-start | bytes 18440 | tf_op jit(solution)/shard_map/ppermute | solution.py:35
  102.7 5.8 %collective-permute-start.18 = (f32[2,14,4,512]{3,2,1,0:T(4,128)S(1)}, f32[2,14,4,512]{3,2,1,0:T(4,128)S(1)}, u32[]{:S(2)}, u32[]{:S(2)}) collective-permute-start(f32[2,14,4,512]{3,2,1,0:T(4,128)S(1)} %get-tuple-element.55), channel_id=1, source_target_pairs={{0,1},{1,0},{2,3},{3,2},{4,5},{5,4},{6,7},{7,6},{8,9},{9,8},{10,11... | collective-permute-start | bytes 688136 | tf_op jit(solution)/shard_map/ppermute | solution.py:35
  103.1 8.8 %collective-permute-start.19 = (f32[2,14,4,512]{3,2,1,0:T(4,128)S(1)}, f32[2,14,4,512]{3,2,1,0:T(4,128)S(1)}, u32[]{:S(2)}, u32[]{:S(2)}) collective-permute-start(f32[2,14,4,512]{3,2,1,0:T(4,128)S(1)} %get-tuple-element.56), channel_id=1, source_target_pairs={{1,2},{2,1},{5,6},{6,5},{9,10},{10,9},{13,14},{14,13},{17,18},{18,... | collective-permute-start | bytes 688136 | tf_op jit(solution)/shard_map/ppermute | solution.py:682
  111.9 20.5 %all-to-all-start.1 = ((f32[128,1,128]{2,1,0:T(1,128)}), f32[128,1,128]{2,1,0:T(1,128)S(1)}, u32[]{:S(2)}, u32[]{:S(2)}) async-start(f32[128,1,128]{2,1,0:T(1,128)} %bitcast.28), calls=%async_computation.1 | async-start | bytes 131072 | tf_op jit(solution)/shard_map/all_to_all | solution.py:634
